TPU v7x, 256 devices: a whole 4x4x8 slice. The times are simulated.
256 devices in a mesh: gx: 16 (over x, y), gy: 8 (over z), gz: 2 (over core).
Axes of the slice: x: 4, y: 4, z: 8, core: 2. Of those that a mesh axis runs over, the one named last changes fastest.
Arguments:
- state: float32 [64, 32, 5, 15, 256], P('gx', 'gy', None, None, 'gz'), may hold values from -0.75 to 0.75
- source: float32 [64, 32, 5, 15, 256], P('gx', 'gy', None, None, 'gz'), may hold values from -0.75 to 0.75
- x_faces: float32 [2, 64, 32, 5, 256], P(None, 'gx', 'gy', None, 'gz'), may hold values from 1 to 4
- y_faces: float32 [2, 64, 32, 5, 256], P(None, 'gx', 'gy', None, 'gz'), may hold values from 1 to 4
- couple: float32 [64, 32, 5, 5, 256], P('gx', 'gy', None, None, 'gz'), may hold values from -0.004 to 0.03, as said below
- omega: float32 [1], replicated, may hold values from 0.5 to 1.5
Outputs:
- new_state: float32 [64, 32, 5, 15, 256], P('gx', 'gy', None, None, 'gz')
Inputs may be any that keep to these rules, and one draw needn't show every extreme that they name: In every 5 x 5 block of couple each diagonal entry is positive and exceeds the sum of magnitudes of the other entries of its row.
All inputs are finite; a program needn't handle non-finite values.
Results may differ from a plain program's by a relative error of at most 0.0003.
Values sent between devices are 32-bit elements; how exact they have to be, the bound alone decides.
No kernel may reach another device: no remote copies, remote signals or barrier semaphores. Data moves between devices by JAX's collectives and lax.ppermute only.
A program may use at most 64 MiB of HBM per device.

v0:
```python
import functools
import math

import jax
import jax.numpy as jnp
import numpy as np
from jax import lax
from jax.experimental import pallas as pl
from jax.experimental.pallas import tpu as pltpu
from jax.sharding import PartitionSpec as P


V = 5
N = 15
B = 4
H = 8
XR = 96
MR = 56
YR = 80
YM = 112
f32 = jnp.float32


def spectral_columns():
    offsets = np.arange(N)
    gaps = offsets[:, None] - offsets[None, :]
    signs = np.where(gaps % 2 == 0, 1.0, -1.0)
    sine = np.where(gaps == 0, 1.0, np.sin(math.pi * gaps / N))
    table = np.where(gaps == 0, 0.0, 0.5 * signs / sine).astype(np.float32)
    return np.ascontiguousarray(np.broadcast_to(table.T[:, :, None], (N, N, 128)))


def lane(shape=(8, 128)):
    return lax.broadcasted_iota(jnp.int32, shape, len(shape) - 1)


def sub(shape=(8, 128)):
    return lax.broadcasted_iota(jnp.int32, shape, len(shape) - 2)


def swap(v):
    return pltpu.roll(v, 64, 1)


def inverse(m):
    m = list(m)
    for p in range(V):
        piv = 1.0 / m[p * V + p]
        for j in range(V):
            if j != p:
                m[p * V + j] = m[p * V + j] * piv
        m[p * V + p] = piv
        for i in range(V):
            if i != p:
                f = m[i * V + p]
                for j in range(V):
                    if j != p:
                        m[i * V + j] = m[i * V + j] - f * m[p * V + j]
                m[i * V + p] = -f * piv
    return m


def dot(terms):
    total = None
    for a, b in terms:
        total = a * b if total is None else total + a * b
    return total


def matmul(a, b):
    return [
        dot([(a[i * V + k], b[k * V + j]) for k in range(V)]) for i in range(V) for j in range(V)
    ]


def pack_edges(load, flag):
    shift = jnp.where(flag == 0, 1, 0)
    lanes = lane((N, 128))
    acc = jnp.zeros((N, 128), f32)
    for c in range(B * B * V):
        x, y, i = c // (B * V), (c // V) % B, c % V
        acc = jnp.where(lanes == c, pltpu.roll(load(x, y, i), shift + c, 1), acc)
    return acc


def edge_kernel(flag_ref, state_ref, first_ref, last_ref, lanes_ref):
    first_ref[...] = state_ref[:, 0]
    last_ref[...] = state_ref[:, B - 1]
    lanes_ref[...] = pack_edges(lambda x, y, i: state_ref[x, y, i], flag_ref[0])


def z_neighbours(v, halo, c, flag, lanes):
    edge = jnp.where(flag == 0, 127, 0)
    low = jnp.where(lanes == 0, 0.0, pltpu.roll(v, 1, 1))
    high = jnp.where(lanes == 127, 0.0, pltpu.roll(v, 127, 1))
    shift = jnp.where(flag == 0, 127 - c, 128 - c)
    far = jnp.where(lanes == edge, pltpu.roll(halo, shift, 1), 0.0)
    return low + high + far


def matrix_kernel(couple_ref, xf_ref, yf_ref, fac_ref, xmat_ref, ymat_ref, mel, lo, hi):
    for a in range(B):
        for b in range(B):
            for i in range(V):
                c = couple_ref[a, b, i]
                mel[pl.ds((a * 25 + i * V) * 8 + b, V, stride=8), :] = c
                mel[pl.ds((b * 25 + i * V) * 8 + 4 + a, V, stride=8), :] = c
            lo[pl.ds(a * V * 8 + b, V, stride=8), :] = xf_ref[0, a, b]
            hi[pl.ds(a * V * 8 + b, V, stride=8), :] = xf_ref[1, a, b]
            lo[pl.ds(b * V * 8 + 4 + a, V, stride=8), :] = yf_ref[0, a, b]
            hi[pl.ds(b * V * 8 + 4 + a, V, stride=8), :] = yf_ref[1, a, b]

    def row(ref, r):
        return ref[r * 8 : r * 8 + 8, :]

    low = [[row(lo, t * V + i) for i in range(V)] for t in range(B)]
    high = [[row(hi, t * V + i) for i in range(V)] for t in range(B)]

    def mid(t):
        m = [row(mel, t * 25 + e) for e in range(25)]
        for i in range(V):
            m[i * V + i] = m[i * V + i] + (low[t][i] + high[t][i])
        return m

    def put(block, m):
        for e in range(25):
            fac_ref[block * 25 + e] = m[e]

    def get(block):
        return [fac_ref[block * 25 + e] for e in range(25)]

    def rows_by(d, m):
        return [d[i] * m[i * V + j] for i in range(V) for j in range(V)]

    def cols_by(m, d):
        return [m[i * V + j] * d[j] for i in range(V) for j in range(V)]

    g0 = inverse(mid(0))
    put(0, g0)
    m1 = mid(1)
    s = rows_by(low[1], cols_by(g0, high[0]))
    g1 = inverse([p - q for p, q in zip(m1, s)])
    put(1, g1)
    m2 = mid(2)
    s = rows_by(low[2], cols_by(g1, high[1]))
    g2 = inverse([p - q for p, q in zip(m2, s)])
    put(2, g2)
    e2 = cols_by(g2, high[2])
    put(8, e2)
    e1 = matmul(get(1), rows_by(high[1], e2))
    put(7, e1)
    e0 = matmul(get(0), rows_by(high[0], e1))
    put(6, e0)
    l0 = cols_by(get(0), low[0])
    l1 = matmul(get(1), rows_by(low[1], l0))
    l2 = matmul(get(2), rows_by(low[2], l1))
    put(5, l2)
    b1 = matmul(get(1), rows_by(high[1], l2))
    l1 = [p + q for p, q in zip(l1, b1)]
    put(4, l1)
    b0 = matmul(get(0), rows_by(high[0], l1))
    l0 = [p + q for p, q in zip(cols_by(get(0), low[0]), b0)]
    put(3, l0)

    lanes = lane()
    m3 = mid(3)
    last_low, last_high = get(5), get(8)
    first_low, first_high = get(3), get(6)

    def x_pair(r, e0, e1):
        for zh in range(2):
            if zh == 0:
                v = jnp.where(lanes < 64, e0, swap(e1))
            else:
                v = jnp.where(lanes < 64, swap(e0), e1)
            for ih in range(2):
                xmat_ref[pl.ds((zh * 2 + ih) * MR + r, 4, stride=4 * MR), :] = v[0:4]

    def y_row(r, e):
        ymat_ref[pl.ds(r, 4, stride=YM), :] = e[4:8]

    for i in range(V):
        for j in range(V):
            e = i * V + j
            a = -(low[3][i] * last_low[e])
            bb = m3[e] - low[3][i] * last_high[e]
            x_pair(e, a, first_high[e])
            x_pair(25 + e, bb, first_low[e])
            y_row(e, a)
            y_row(25 + e, bb)
            y_row(50 + e, first_low[e])
            y_row(75 + e, first_high[e])
        x_pair(50 + i, high[3][i], high[3][i])
        y_row(100 + i, high[3][i])
    for r in range(105, YM):
        y_row(r, jnp.zeros((8, 128), f32))
    x_pair(55, jnp.zeros((8, 128), f32), jnp.zeros((8, 128), f32))


def halves(v):
    return v[0:H], jnp.concatenate([v[H:N], jnp.zeros((1, 128), f32)], axis=0)


def apply(fac_ref, block, line, vec):
    out = []
    for i in range(V):
        out.append(
            dot([(fac_ref[block * 25 + i * V + k, line : line + 1, :], vec[k]) for k in range(V)])
        )
    return out


def condense(fac_ref, line, right, low, high):
    y0 = apply(fac_ref, 0, line, right(0))
    y1 = apply(fac_ref, 1, line, [r + l * y for r, l, y in zip(right(1), low(1), y0)])
    v2 = apply(fac_ref, 2, line, [r + l * y for r, l, y in zip(right(2), low(2), y1)])
    c1 = apply(fac_ref, 1, line, [h * v for h, v in zip(high(1), v2)])
    v1 = [p + q for p, q in zip(y1, c1)]
    c0 = apply(fac_ref, 0, line, [h * v for h, v in zip(high(0), v1)])
    v0 = [p + q for p, q in zip(y0, c0)]
    last = [r + l * v for r, l, v in zip(right(3), low(3), v2)]
    return v0, v1, v2, last


def spectral_terms(load, table, lanes_shape=(N, 128)):
    acc = [None] * V
    for k in range(N):
        t = table[k]
        for i in range(V):
            p = t * load(i, k)
            acc[i] = p if acc[i] is None else acc[i] + p
    return acc


def first_kernel(
    flag_ref, omega_ref, state_ref, source_ref, before_ref, after_ref, halo_ref, xf_ref, yf_ref,
    fac_ref, xmat_ref, spec_ref, r_ref, v_ref, msg_ref, table,
):
    flag = flag_ref[0]
    lanes = lane((N, 128))
    table[...] = spec_ref[...] * omega_ref[0]
    halo = halo_ref[...]
    for y in range(B):
        for x in range(B):
            spec = spectral_terms(lambda i, k: state_ref[x, y, i, k : k + 1, :], table)
            for i in range(V):
                s = state_ref[x, y, i]
                below = state_ref[x, y - 1, i] if y > 0 else before_ref[x, i]
                above = state_ref[x, y + 1, i] if y < B - 1 else after_ref[x, i]
                yl = yf_ref[0, x, y, i : i + 1, :]
                yh = yf_ref[1, x, y, i : i + 1, :]
                zn = z_neighbours(s, halo, (x * B + y) * V + i, flag, lanes)
                r = source_ref[x, y, i] - (yl + yh + 1.0) * s + yl * below + yh * above
                r_ref[x, y, i] = r + 0.5 * zn - spec[i]
    lanes8 = lane()
    for y in range(B):
        v0, v1, v2, last = condense(
            fac_ref, y,
            lambda t: [r_ref[t, y, i] for i in range(V)],
            lambda t: [xf_ref[0, t, y, i : i + 1, :] for i in range(V)],
            lambda t: [xf_ref[1, t, y, i : i + 1, :] for i in range(V)],
        )
        for i in range(V):
            v_ref[0, y, i] = v0[i]
            v_ref[1, y, i] = v1[i]
            v_ref[2, y, i] = v2[i]
            for ih, (e0, e1) in enumerate(zip(halves(last[i]), halves(v0[i]))):
                lo = jnp.where(lanes8 < 64, e0, swap(e1))
                hi = jnp.where(lanes8 < 64, swap(e0), e1)
                for zh, v in enumerate((lo, hi)):
                    msg_ref[y * 4 + zh * 2 + ih, i * H : (i + 1) * H, :] = v
    for d in range(16):
        msg_ref[d, 40:XR, :] = xmat_ref[d * MR : (d + 1) * MR, :]


def reduce_lines(a, b, c, r, shifted, steps, kk, nn, bi):
    for step in range(steps):
        inv = inverse([b[e] for e in range(25)])
        for e in range(25):
            bi[e] = inv[e]
        last = step == steps - 1
        for dst, src in ((kk, a), (nn, c)):
            m = [src[e] for e in range(25)]
            for i in range(V):
                row = [bi[i * V + k] for k in range(V)]
                for j in range(V):
                    dst[i * V + j] = dot([(row[k], m[k * V + j]) for k in range(V)])
        m = [shifted(nn[e], step, -1) for e in range(25)]
        for i in range(V):
            row = [a[i * V + k] for k in range(V)]
            for j in range(V):
                b[i * V + j] = b[i * V + j] - dot([(row[k], m[k * V + j]) for k in range(V)])
        m = [shifted(kk[e], step, 1) for e in range(25)]
        for i in range(V):
            row = [c[i * V + k] for k in range(V)]
            for j in range(V):
                b[i * V + j] = b[i * V + j] - dot([(row[k], m[k * V + j]) for k in range(V)])
        for n in range(H):
            old = [r[i * H + n] for i in range(V)]
            hat = [dot([(bi[i * V + k], old[k]) for k in range(V)]) for i in range(V)]
            before = [shifted(h, step, -1) for h in hat]
            after = [shifted(h, step, 1) for h in hat]
            for i in range(V):
                r[i * H + n] = (
                    old[i]
                    - dot([(a[i * V + k], before[k]) for k in range(V)])
                    - dot([(c[i * V + k], after[k]) for k in range(V)])
                )
        if not last:
            m = [shifted(kk[e], step, -1) for e in range(25)]
            for i in range(V):
                row = [a[i * V + k] for k in range(V)]
                for j in range(V):
                    a[i * V + j] = -dot([(row[k], m[k * V + j]) for k in range(V)])
            m = [shifted(nn[e], step, 1) for e in range(25)]
            for i in range(V):
                row = [c[i * V + k] for k in range(V)]
                for j in range(V):
                    c[i * V + j] = -dot([(row[k], m[k * V + j]) for k in range(V)])
    inv = inverse([b[e] for e in range(25)])
    for e in range(25):
        bi[e] = inv[e]
    for n in range(H):
        old = [r[i * H + n] for i in range(V)]
        for i in range(V):
            r[i * H + n] = dot([(bi[i * V + k], old[k]) for k in range(V)])


def close(b, c, r, fl, fh, first, edge, shift_after, edge_ok):
    for i in range(V):
        h = jnp.where(edge_ok, edge(i), 0.0)
        for j in range(V):
            e = i * V + j
            c[e] = -(h * shift_after(fh(e)))
            b[e] = b[e] - h * shift_after(fl(e))
        for n in range(H):
            r[i * H + n] = r[i * H + n] + h * shift_after(first(i, n))


def x_solver_kernel(msg_ref, out_ref, a, b, c, r, kk, nn, bi, fh, fl, first):
    lanes, subs = lane(), sub()
    left = lanes < 64

    def pair(row):
        p = msg_ref[pl.ds(row, 8, stride=XR), :]
        q = msg_ref[pl.ds(8 * XR + row, 8, stride=XR), :]
        return jnp.where(left, p, swap(q)), jnp.where(left, swap(p), q)

    def before(v, k):
        if k == 8:
            return swap(v)
        v = pltpu.roll(v, k, 0)
        return jnp.where(subs < k, swap(v), v)

    def after(v, k):
        if k == 8:
            return swap(v)
        v = pltpu.roll(v, 8 - k, 0)
        return jnp.where(subs >= 8 - k, swap(v), v)

    def shifted(v, step, sign):
        return before(v, 2**step) if sign < 0 else after(v, 2**step)

    begin = (subs == 0) & left
    end = (subs == 7) & (lanes >= 64)
    for e in range(25):
        low, fh[e] = pair(40 + e)
        a[e] = jnp.where(begin, 0.0, low)
        b[e], fl[e] = pair(65 + e)
    for e in range(40):
        r[e], first[e] = pair(e)
    close(
        b, c, r, lambda e: fl[e], lambda e: fh[e], lambda i, n: first[i * H + n],
        lambda i: pair(90 + i)[0], lambda v: after(v, 1), jnp.logical_not(end),
    )
    reduce_lines(a, b, c, r, shifted, 4, kk, nn, bi)
    for e in range(40):
        u = r[e]
        prev = jnp.where(begin, 0.0, before(u, 1))
        out_ref[pl.ds(e, 8, stride=40), :] = jnp.where(left, prev, swap(u))
        out_ref[pl.ds(320 + e, 8, stride=40), :] = jnp.where(left, swap(prev), u)


def y_solver_kernel(line_ref, msg_ref, mat_ref, out_ref, a, b, c, r, kk, nn, bi):
    subs = sub()

    def rhs(row):
        return msg_ref[pl.ds(row, 8, stride=YR), :]

    def mat(row):
        return mat_ref[:, 0, row, :]

    def before(v, k):
        return pltpu.roll(v, k, 0)

    def after(v, k):
        return pltpu.roll(v, 8 - k, 0)

    def shifted(v, step, sign):
        return before(v, 2**step) if sign < 0 else after(v, 2**step)

    begin = subs == 0
    for e in range(25):
        a[e] = jnp.where(begin, 0.0, mat(e))
        b[e] = mat(25 + e)
    for e in range(40):
        r[e] = rhs(e)
    close(
        b, c, r, lambda e: mat(50 + e), lambda e: mat(75 + e), lambda i, n: rhs(40 + i * H + n),
        lambda i: mat(100 + i), lambda v: after(v, 1), subs != 7,
    )
    reduce_lines(a, b, c, r, shifted, 3, kk, nn, bi)
    for e in range(40):
        u = r[e]
        out_ref[pl.ds(e, 8, stride=YR), :] = jnp.where(begin, 0.0, before(u, 1))
        out_ref[pl.ds(40 + e, 8, stride=YR), :] = u


def middle_kernel(flag_ref, ret_ref, v_ref, fac_ref, h_ref, edge_ref):
    left = lane() < 64
    for y in range(B):
        prev, cur = [], []
        for i in range(V):
            um, u = [], []
            for ih in range(2):
                z0 = ret_ref[y * 4 + ih, i * H : (i + 1) * H, :]
                z1 = ret_ref[y * 4 + 2 + ih, i * H : (i + 1) * H, :]
                um.append(jnp.where(left, z0, swap(z1)))
                u.append(jnp.where(left, swap(z0), z1))
            prev.append(jnp.concatenate(um, axis=0)[:N])
            cur.append(jnp.concatenate(u, axis=0)[:N])
        for t in range(B - 1):
            lo = apply(fac_ref, 3 + t, y, prev)
            hi = apply(fac_ref, 6 + t, y, cur)
            for i in range(V):
                h_ref[t, y, i] = v_ref[t, y, i] + lo[i] + hi[i]
        for i in range(V):
            h_ref[B - 1, y, i] = cur[i]
    edge_ref[...] = pack_edges(lambda x, y, i: h_ref[x, y, i], flag_ref[0])


def second_kernel(
    flag_ref, omega_ref, h_ref, source_ref, r_ref, halo_ref, couple_ref, yf_ref, fac_ref, spec_ref,
    v_ref, msg_ref, table, r2,
):
    flag = flag_ref[0]
    lanes = lane((N, 128))
    table[...] = spec_ref[...] * omega_ref[0]
    halo = halo_ref[...]
    for x in range(B):
        for y in range(B):
            spec = spectral_terms(lambda i, k: h_ref[x, y, i, k : k + 1, :], table)
            h = [h_ref[x, y, i] for i in range(V)]
            for i in range(V):
                zn = z_neighbours(h[i], halo, (x * B + y) * V + i, flag, lanes)
                c = dot([(couple_ref[x, y, i, k : k + 1, :], h[k]) for k in range(V)])
                r = source_ref[x, y, i] - r_ref[x, y, i] + c
                r2[x, y, i] = r - h[i] + 0.5 * zn - spec[i]
    for x in range(B):
        v0, v1, v2, last = condense(
            fac_ref, 4 + x,
            lambda t: [r2[x, t, i] for i in range(V)],
            lambda t: [yf_ref[0, x, t, i : i + 1, :] for i in range(V)],
            lambda t: [yf_ref[1, x, t, i : i + 1, :] for i in range(V)],
        )
        for i in range(V):
            v_ref[x, 0, i] = v0[i]
            v_ref[x, 1, i] = v1[i]
            v_ref[x, 2, i] = v2[i]
            for ih, (e0, e1) in enumerate(zip(halves(last[i]), halves(v0[i]))):
                msg_ref[x * 2 + ih, i * H : (i + 1) * H, :] = e0
                msg_ref[x * 2 + ih, 40 + i * H : 40 + (i + 1) * H, :] = e1


def last_kernel(ret_ref, v_ref, fac_ref, w_ref):
    for x in range(B):
        prev, cur = [], []
        for i in range(V):
            for out, at in ((prev, 0), (cur, 40)):
                rows = [
                    ret_ref[x * 2 + ih, at + i * H : at + (i + 1) * H, :] for ih in range(2)
                ]
                out.append(jnp.concatenate(rows, axis=0)[:N])
        for t in range(B - 1):
            lo = apply(fac_ref, 3 + t, 4 + x, prev)
            hi = apply(fac_ref, 6 + t, 4 + x, cur)
            for i in range(V):
                w_ref[x, t, i] = v_ref[x, t, i] + lo[i] + hi[i]
        for i in range(V):
            w_ref[x, B - 1, i] = cur[i]


smem = pl.BlockSpec(memory_space=pltpu.SMEM)
vmem = pl.BlockSpec(memory_space=pltpu.VMEM)


def sds(*shape):
    return jax.ShapeDtypeStruct(shape, f32)


def scratch(*shape):
    return pltpu.VMEM(shape, f32)


def call(kernel, ins, outs, scratches=(), **more):
    single = not isinstance(outs, (list, tuple))
    return pl.pallas_call(
        kernel,
        in_specs=list(ins),
        out_specs=vmem if single else [vmem] * len(outs),
        out_shape=outs,
        scratch_shapes=list(scratches),
        compiler_params=pltpu.CompilerParams(vmem_limit_bytes=40 * 2**20),
        **more,
    )


def body(state, source, x_faces, y_faces, couple, omega):
    n_y = lax.axis_size("gy")
    flag = lax.axis_index("gz").astype(jnp.int32).reshape(1)
    spec = jnp.asarray(spectral_columns())
    up = [(i, i + 1) for i in range(n_y - 1)]
    down = [(j, i) for i, j in up]
    flip = [(0, 1), (1, 0)]
    field = sds(B, B, V, N, 128)

    first, last, lanes = call(
        edge_kernel, [smem, vmem],
        [sds(B, V, N, 128), sds(B, V, N, 128), sds(N, 128)],
    )(flag, state)
    before = lax.ppermute(last, "gy", up)
    after = lax.ppermute(first, "gy", down)
    halo = lax.ppermute(lanes, "gz", flip)
    fac, xmat, ymat = call(
        matrix_kernel, [vmem] * 3,
        [sds(225, 8, 128), sds(16 * MR, 128), sds(B * YM, 128)],
        [scratch(B * 25 * 8, 128), scratch(B * V * 8, 128), scratch(B * V * 8, 128)],
    )(couple, x_faces, y_faces)
    all_mat = lax.all_gather(ymat, "gy").reshape(n_y, B, YM, 128)
    r1, v, msg = call(
        first_kernel, [smem, smem] + [vmem] * 10,
        [field, sds(B - 1, B, V, N, 128), sds(16, XR, 128)],
        [scratch(N, N, 128)],
    )(flag, omega, state, source, before, after, halo, x_faces, y_faces, fac, xmat, spec)
    got = lax.all_to_all(msg, "gx", 0, 0, tiled=True)
    mats = [scratch(25, 8, 128)] * 3 + [scratch(40, 8, 128)] + [scratch(25, 8, 128)] * 3
    ret = call(
        x_solver_kernel, [vmem], sds(16 * 40, 128),
        mats + [scratch(25, 8, 128), scratch(25, 8, 128), scratch(40, 8, 128)],
    )(got.reshape(16 * XR, 128))
    back = lax.all_to_all(ret.reshape(16, 40, 128), "gx", 0, 0, tiled=True)
    h, edge = call(
        middle_kernel, [smem, vmem, vmem, vmem], [field, sds(N, 128)]
    )(flag, back, v, fac)
    halo = lax.ppermute(edge, "gz", flip)
    v, msg = call(
        second_kernel, [smem, smem] + [vmem] * 8,
        [sds(B, B - 1, V, N, 128), sds(8, YR, 128)],
        [scratch(N, N, 128), scratch(B, B, V, N, 128)],
    )(flag, omega, h, source, r1, halo, couple, y_faces, fac, spec)
    got = lax.all_to_all(msg, "gy", 0, 0, tiled=True)
    line = (lax.axis_index("gy") // 2).astype(jnp.int32).reshape(1)
    ret = pl.pallas_call(
        y_solver_kernel,
        grid_spec=pltpu.PrefetchScalarGridSpec(
            num_scalar_prefetch=1,
            grid=(1,),
            in_specs=[
                pl.BlockSpec((8 * YR, 128), lambda i, line: (0, 0)),
                pl.BlockSpec((8, 1, YM, 128), lambda i, line: (0, line[0], 0, 0)),
            ],
            out_specs=pl.BlockSpec((8 * YR, 128), lambda i, line: (0, 0)),
            scratch_shapes=mats,
        ),
        out_shape=sds(8 * YR, 128),
        compiler_params=pltpu.CompilerParams(vmem_limit_bytes=40 * 2**20),
    )(line, got.reshape(8 * YR, 128), all_mat)
    back = lax.all_to_all(ret.reshape(8, YR, 128), "gy", 0, 0, tiled=True)
    return call(last_kernel, [vmem] * 3, field)(back, v, fac)


def solution(mesh):
    return jax.shard_map(
        body,
        mesh=mesh,
        in_specs=(
            P("gx", "gy", None, None, "gz"),
            P("gx", "gy", None, None, "gz"),
            P(None, "gx", "gy", None, "gz"),
            P(None, "gx", "gy", None, "gz"),
            P("gx", "gy", None, None, "gz"),
            P(),
        ),
        out_specs=P("gx", "gy", None, None, "gz"),
        check_vma=False,
    )
```

profile of v0, /device:TPU:1, one launch (start us, length us, event | category | flops | bytes accessed | tf_op | source)
XLA Modules:
  0.0 113.5 jit_solution(2785351883727447019)
XLA Ops:
  6.5 0.0 all-gather.3.cloned.1.call-start
  6.5 1.0 copy.15.yf_ref
  7.5 1.0 copy.9.couple_ref
  8.5 0.9 copy.14.xf_ref
  9.4 1.5 %shard_map.74 = (f32[225,8,128]{2,1,0:T(8,128)S(1)}, f32[896,128]{1,0:T(8,128)S(1)}, f32[448,128]{1,0:T(8,128)}) custom-call(f32[4,4,5,5,128]{4,3,2,1,0:T(8,128)S(1)} %copy.9.couple_ref, f32[2,4,4,5,128]{4,3,2,1,0:T(8,128)S(1)} %copy.14.xf_ref, f32[2,4,4,5,128]{4,3,2,1,0:T(8,128)S(1)} %copy.15.yf_ref), custom_call_target="tpu_custom_call" | custom-call | tf_op jit(solution)/shard_map/pallas_call | solution.py:534
  10.9 0.0 all-gather.3.cloned.1.call-update
  10.9 0.0 copy-start.3
  10.9 0.1 copy.12.state_ref
  11.0 0.2 shard_map.73
  11.2 4.4 %collective-permute-start = (f32[4,5,15,128]{3,2,1,0:T(8,128)S(1)}, f32[4,5,15,128]{3,2,1,0:T(8,128)S(1)}, u32[]{:S(2)}, u32[]{:S(2)}) collective-permute-start(f32[4,5,15,128]{3,2,1,0:T(8,128)S(1)} %get-tuple-element.18), channel_id=1, source_target_pairs={{0,2},{2,4},{4,6},{6,8},{8,10},{10,12},{12,14},{1,3},{3,5},{5,7},{... | collective-permute-start | bytes 460808 | tf_op jit(solution)/shard_map/ppermute | solution.py:531
  15.6 1.3 %collective-permute-start.1 = (f32[4,5,15,128]{3,2,1,0:T(8,128)S(1)}, f32[4,5,15,128]{3,2,1,0:T(8,128)S(1)}, u32[]{:S(2)}, u32[]{:S(2)}) collective-permute-start(f32[4,5,15,128]{3,2,1,0:T(8,128)S(1)} %get-tuple-element.19), channel_id=1, source_target_pairs={{2,0},{4,2},{6,4},{8,6},{10,8},{12,10},{14,12},{3,1},{5,3},{7,5},{... | collective-permute-start | bytes 460808 | tf_op jit(solution)/shard_map/ppermute | solution.py:532
  16.9 1.0 collective-permute-start.2
  18.0 0.0 copy-done.3
  18.0 0.1 copy.13.source_ref
  18.7 0.1 collective-permute-done.2.halo_ref
  18.8 0.0 collective-permute-done.before_ref
  18.8 3.8 %collective-permute-done.1.after_ref = f32[4,5,15,128]{3,2,1,0:T(8,128)S(1)} collective-permute-done((f32[4,5,15,128]{3,2,1,0:T(8,128)S(1)}, f32[4,5,15,128]{3,2,1,0:T(8,128)S(1)}, u32[]{:S(2)}, u32[]{:S(2)}) %collective-permute-start.1) | collective-permute-done | bytes 153632 | tf_op jit(solution)/shard_map/ppermute | solution.py:532
  22.6 1.8 %shard_map.75 = (f32[4,4,5,15,128]{4,3,2,1,0:T(8,128)S(1)}, f32[3,4,5,15,128]{4,3,2,1,0:T(8,128)S(1)}, f32[16,96,128]{2,1,0:T(8,128)S(1)}) custom-call(s32[1]{0:T(128)} %bitcast.1.flag_ref, f32[1]{0:T(128)S(6)} %copy.20.omega_ref, f32[4,4,5,15,128]{4,3,2,1,0:T(8,128)S(1)} %copy.12.state_ref, f32[4,4,5,15,128]{4,3,2,1,0:T(8,128)S(1)} %copy.13.source_ref, ...), custom_call_target="tpu_custom_call" | custom-call | tf_op jit(solution)/shard_map/pallas_call | solution.py:540
  24.5 18.3 %all_to_all.20 = f32[16,96,128]{2,1,0:T(8,128)S(1)} all-to-all(f32[16,96,128]{2,1,0:T(8,128)S(1)} %get-tuple-element.23), channel_id=1, replica_groups=mesh['gx'=16,'gy'=8,'gz'=2] {'gx'}, dimensions={0} | all-to-all | bytes 1572864 | tf_op jit(solution)/shard_map/all_to_all | solution.py:545
  42.8 3.1 %shard_map.76 = f32[640,128]{1,0:T(8,128)S(1)} custom-call(f32[1536,128]{1,0:T(8,128)S(1)} %bitcast.7), custom_call_target="tpu_custom_call" | custom-call | tf_op jit(solution)/shard_map/pallas_call | solution.py:547
  45.9 11.4 %all_to_all.21.ret_ref = f32[16,40,128]{2,1,0:T(8,128)S(1)} all-to-all(f32[16,40,128]{2,1,0:T(8,128)S(1)} %bitcast.9), channel_id=1, replica_groups=mesh['gx'=16,'gy'=8,'gz'=2] {'gx'}, dimensions={0} | all-to-all | bytes 655360 | tf_op jit(solution)/shard_map/all_to_all | solution.py:551
  57.3 0.6 shard_map.77
  57.9 4.2 %collective-permute-start.3 = (f32[15,128]{1,0:T(8,128)S(1)}, f32[15,128]{1,0:T(8,128)S(1)}, u32[]{:S(2)}, u32[]{:S(2)}) collective-permute-start(f32[15,128]{1,0:T(8,128)S(1)} %get-tuple-element.27), channel_id=1, source_target_pairs={{0,1},{1,0},{2,3},{3,2},{4,5},{5,4},{6,7},{7,6},{8,9},{9,8},{10,11... | collective-permute-start | bytes 23048 | tf_op jit(solution)/shard_map/ppermute | solution.py:555
  62.2 0.8 collective-permute-done.3.halo_ref
  63.0 2.5 %shard_map.78 = (f32[4,3,5,15,128]{4,3,2,1,0:T(8,128)S(1)}, f32[8,80,128]{2,1,0:T(8,128)}) custom-call(s32[1]{0:T(128)} %bitcast.1.flag_ref, f32[1]{0:T(128)S(6)} %copy.20.omega_ref, f32[4,4,5,15,128]{4,3,2,1,0:T(8,128)S(1)} %get-tuple-element.25.h_ref, f32[4,4,5,15,128]{4,3,2,1,0:T(8,128)S(1)} %copy.13.source_ref, ...), custom_call_target="tpu_custom_call" | custom-call | tf_op jit(solution)/shard_map/pallas_call | solution.py:556
  65.5 7.7 %all-to-all-start.2 = ((f32[8,80,128]{2,1,0:T(8,128)}), f32[8,80,128]{2,1,0:T(8,128)S(1)}, u32[]{:S(2)}, u32[]{:S(2)}) async-start(f32[8,80,128]{2,1,0:T(8,128)} %get-tuple-element.28), calls=%async_computation.2 | async-start | bytes 655360 | tf_op jit(solution)/shard_map/all_to_all | solution.py:561
  73.2 13.7 %all-to-all-done.2 = f32[8,80,128]{2,1,0:T(8,128)S(1)} async-done(((f32[8,80,128]{2,1,0:T(8,128)}), f32[8,80,128]{2,1,0:T(8,128)S(1)}, u32[]{:S(2)}, u32[]{:S(2)}) %all-to-all-start.2) | async-done | bytes 327712 | tf_op jit(solution)/shard_map/all_to_all | solution.py:561
  86.9 1.5 %copy-done = f32[3584,128]{1,0:T(8,128)S(1)} copy-done((f32[3584,128]{1,0:T(8,128)S(1)}, f32[3584,128]{1,0:T(8,128)}, u32[]{:S(2)}) %copy-start) | copy-done | bytes 1835032
  88.4 1.7 %shard_map.79 = f32[640,128]{1,0:T(8,128)S(1)} custom-call(s32[1]{0:T(128)} %bitcast.line_ref, f32[640,128]{1,0:T(8,128)S(1)} %bitcast.10, f32[8,4,112,128]{3,2,1,0:T(8,128)S(1)} %bitcast.8), custom_call_target="tpu_custom_call" | custom-call | tf_op jit(solution)/shard_map/pallas_call | solution.py:563
  90.0 15.2 %all_to_all.22.ret_ref = f32[8,80,128]{2,1,0:T(8,128)S(1)} all-to-all(f32[8,80,128]{2,1,0:T(8,128)S(1)} %bitcast.11), channel_id=1, replica_groups=mesh['gx'=16,'gy'=8,'gz'=2] {'gy'}, dimensions={0} | all-to-all | bytes 655360 | tf_op jit(solution)/shard_map/all_to_all | solution.py:578
  105.2 0.4 shard_map.80
  105.5 1.1 copy.19
  (6 shorter events, 0.0 us)
Async XLA Ops:
  6.5 4.4 %copy-start.2 = (f32[4,4,5,15,128]{4,1,3,2,0:T(4,128)S(1)}, f32[4,4,5,15,128]{4,1,3,2,0:T(4,128)}, u32[]{:S(2)}) copy-start(f32[4,4,5,15,128]{4,1,3,2,0:T(4,128)} %param.7) | copy-start | bytes 1843204
  6.5 80.3 %all-gather.3.cloned.1.call-start = ((), (), s32[]{:S(2)}) async-start(), calls=%async_computation.4 | async-start | bytes 2064384 | tf_op jit(solution)/shard_map/all_gather | solution.py:539
  10.9 11.8 %copy-start.1 = (f32[15,15,128]{2,1,0:T(8,128)S(1)}, f32[15,15,128]{2,1,0:T(8,128)}, u32[]{:S(2)}) copy-start(f32[15,15,128]{2,1,0:T(8,128)} %constant.24.clone.spec_ref) | copy-start | bytes 345604
  10.9 7.1 %copy-start.3 = (f32[4,4,5,15,128]{4,1,3,2,0:T(4,128)S(1)}, f32[4,4,5,15,128]{4,1,3,2,0:T(4,128)}, u32[]{:S(2)}) copy-start(f32[4,4,5,15,128]{4,1,3,2,0:T(4,128)} %param.8) | copy-start | bytes 1843204
  11.2 7.6 %collective-permute-start = (f32[4,5,15,128]{3,2,1,0:T(8,128)S(1)}, f32[4,5,15,128]{3,2,1,0:T(8,128)S(1)}, u32[]{:S(2)}, u32[]{:S(2)}) collective-permute-start(f32[4,5,15,128]{3,2,1,0:T(8,128)S(1)} %get-tuple-element.18), channel_id=1, source_target_pairs={{0,2},{2,4},{4,6},{6,8},{8,10},{10,12},{12,14},{1,3},{3,5},{5,7},{... | collective-permute-start | bytes 460808 | tf_op jit(solution)/shard_map/ppermute | solution.py:531
  15.6 7.0 %collective-permute-start.1 = (f32[4,5,15,128]{3,2,1,0:T(8,128)S(1)}, f32[4,5,15,128]{3,2,1,0:T(8,128)S(1)}, u32[]{:S(2)}, u32[]{:S(2)}) collective-permute-start(f32[4,5,15,128]{3,2,1,0:T(8,128)S(1)} %get-tuple-element.19), channel_id=1, source_target_pairs={{2,0},{4,2},{6,4},{8,6},{10,8},{12,10},{14,12},{3,1},{5,3},{7,5},{... | collective-permute-start | bytes 460808 | tf_op jit(solution)/shard_map/ppermute | solution.py:532
  16.9 1.9 %collective-permute-start.2 = (f32[15,128]{1,0:T(8,128)S(1)}, f32[15,128]{1,0:T(8,128)S(1)}, u32[]{:S(2)}, u32[]{:S(2)}) collective-permute-start(f32[15,128]{1,0:T(8,128)S(1)} %get-tuple-element.20), channel_id=1, source_target_pairs={{0,1},{1,0},{2,3},{3,2},{4,5},{5,4},{6,7},{7,6},{8,9},{9,8},{10,11... | collective-permute-start | bytes 23048 | tf_op jit(solution)/shard_map/ppermute | solution.py:533
  57.9 5.1 %collective-permute-start.3 = (f32[15,128]{1,0:T(8,128)S(1)}, f32[15,128]{1,0:T(8,128)S(1)}, u32[]{:S(2)}, u32[]{:S(2)}) collective-permute-start(f32[15,128]{1,0:T(8,128)S(1)} %get-tuple-element.27), channel_id=1, source_target_pairs={{0,1},{1,0},{2,3},{3,2},{4,5},{5,4},{6,7},{7,6},{8,9},{9,8},{10,11... | collective-permute-start | bytes 23048 | tf_op jit(solution)/shard_map/ppermute | solution.py:555
  65.5 21.3 %all-to-all-start.2 = ((f32[8,80,128]{2,1,0:T(8,128)}), f32[8,80,128]{2,1,0:T(8,128)S(1)}, u32[]{:S(2)}, u32[]{:S(2)}) async-start(f32[8,80,128]{2,1,0:T(8,128)} %get-tuple-element.28), calls=%async_computation.2 | async-start | bytes 655360 | tf_op jit(solution)/shard_map/all_to_all | solution.py:561
  86.9 1.5 %copy-start = (f32[3584,128]{1,0:T(8,128)S(1)}, f32[3584,128]{1,0:T(8,128)}, u32[]{:S(2)}) copy-start(f32[3584,128]{1,0:T(8,128)} %all-gather.3.cloned.1.call-done) | copy-start | bytes 5505028
Sparse Core Ops, SparseCore 0:
  11.0 40.6 all-gather.2
where the time goes:
time: 114 us; the launch traced here: 113 us
  blocking collectives  44.9 us (39%)
  starting transfers between devices  18.6 us (16%)
  waiting for transfers between devices  18.4 us (16%)
  between operations  14.1 us (12%)
  Pallas kernels  11.8 us (10%)
  local copies, waits for them, and re-layouts  5.56 us (5%)
    all_to_all x1, blocking collectives, body(): got = lax.all_to_all(msg, 'gx', 0, 0, tiled=True)  18.3 us
    all_to_all x1, blocking collectives, body(): back = lax.all_to_all(ret.reshape(8, YR, 128), 'gy', 0, 0, tiled=True)  15.2 us
    all_to_all x1, waiting for transfers between devices, body(): got = lax.all_to_all(msg, 'gy', 0, 0, tiled=True)  13.7 us
    all_to_all x1, blocking collectives, body(): back = lax.all_to_all(ret.reshape(16, 40, 128), 'gx', 0, 0, tiled=True)  11.4 us
    all_to_all x1, starting transfers between devices, body(): got = lax.all_to_all(msg, 'gy', 0, 0, tiled=True)  7.66 us
    unnamed x13, local copies, waits for them, and re-layouts  4.5 us
    ppermute x1, starting transfers between devices, body(): before = lax.ppermute(last, 'gy', up)  4.38 us
    ppermute x1, starting transfers between devices, body(): halo = lax.ppermute(edge, 'gz', flip)  4.24 us
  transfers between devices with their start and end apart: 6, of which 4 were waited for; matrix products, arithmetic and copies ran while one was open for 0% of the time, Pallas kernels for 7%

commit v1 on v0

--- a/solution.py
+++ b/solution.py
@@ -16,8 +16,7 @@
 H = 8
 XR = 96
 MR = 56
-YR = 80
-YM = 112
+YR = 136
 f32 = jnp.float32
 
 
@@ -100,15 +99,16 @@
 
 def matrix_kernel(couple_ref, xf_ref, yf_ref, fac_ref, xmat_ref, ymat_ref, mel, lo, hi):
     for a in range(B):
-        for b in range(B):
-            for i in range(V):
-                c = couple_ref[a, b, i]
-                mel[pl.ds((a * 25 + i * V) * 8 + b, V, stride=8), :] = c
-                mel[pl.ds((b * 25 + i * V) * 8 + 4 + a, V, stride=8), :] = c
-            lo[pl.ds(a * V * 8 + b, V, stride=8), :] = xf_ref[0, a, b]
-            hi[pl.ds(a * V * 8 + b, V, stride=8), :] = xf_ref[1, a, b]
-            lo[pl.ds(b * V * 8 + 4 + a, V, stride=8), :] = yf_ref[0, a, b]
-            hi[pl.ds(b * V * 8 + 4 + a, V, stride=8), :] = yf_ref[1, a, b]
+        for i in range(V):
+            for j in range(V):
+                c = couple_ref[a, i, j]
+                e = i * V + j
+                mel[(a * 25 + e) * 8 : (a * 25 + e) * 8 + 4, :] = c
+                mel[pl.ds(e * 8 + 4 + a, B, stride=25 * 8), :] = c
+            lo[(a * V + i) * 8 : (a * V + i) * 8 + 4, :] = xf_ref[0, a, i]
+            hi[(a * V + i) * 8 : (a * V + i) * 8 + 4, :] = xf_ref[1, a, i]
+            lo[pl.ds(i * 8 + 4 + a, B, stride=V * 8), :] = yf_ref[0, a, i]
+            hi[pl.ds(i * 8 + 4 + a, B, stride=V * 8), :] = yf_ref[1, a, i]
 
     def row(ref, r):
         return ref[r * 8 : r * 8 + 8, :]
@@ -167,7 +167,7 @@
     last_low, last_high = get(5), get(8)
     first_low, first_high = get(3), get(6)
 
-    def x_pair(r, e0, e1):
+    def put_pair(r, e0, e1):
         for zh in range(2):
             if zh == 0:
                 v = jnp.where(lanes < 64, e0, swap(e1))
@@ -175,26 +175,19 @@
                 v = jnp.where(lanes < 64, swap(e0), e1)
             for ih in range(2):
                 xmat_ref[pl.ds((zh * 2 + ih) * MR + r, 4, stride=4 * MR), :] = v[0:4]
-
-    def y_row(r, e):
-        ymat_ref[pl.ds(r, 4, stride=YM), :] = e[4:8]
+            ymat_ref[pl.ds(zh * MR + r, 4, stride=2 * MR), :] = v[4:8]
 
     for i in range(V):
         for j in range(V):
             e = i * V + j
-            a = -(low[3][i] * last_low[e])
-            bb = m3[e] - low[3][i] * last_high[e]
-            x_pair(e, a, first_high[e])
-            x_pair(25 + e, bb, first_low[e])
-            y_row(e, a)
-            y_row(25 + e, bb)
-            y_row(50 + e, first_low[e])
-            y_row(75 + e, first_high[e])
-        x_pair(50 + i, high[3][i], high[3][i])
-        y_row(100 + i, high[3][i])
-    for r in range(105, YM):
-        y_row(r, jnp.zeros((8, 128), f32))
-    x_pair(55, jnp.zeros((8, 128), f32), jnp.zeros((8, 128), f32))
+            put_pair(e, -(low[3][i] * last_low[e]), first_high[e])
+            put_pair(25 + e, m3[e] - low[3][i] * last_high[e], first_low[e])
+    zero = jnp.zeros((8, 128), f32)
+    put_pair(50, high[3][0], high[3][1])
+    put_pair(51, high[3][2], high[3][3])
+    put_pair(52, high[3][4], zero)
+    for r in range(53, MR):
+        put_pair(r, zero, zero)
 
 
 def halves(v):
@@ -247,8 +240,8 @@
                 s = state_ref[x, y, i]
                 below = state_ref[x, y - 1, i] if y > 0 else before_ref[x, i]
                 above = state_ref[x, y + 1, i] if y < B - 1 else after_ref[x, i]
-                yl = yf_ref[0, x, y, i : i + 1, :]
-                yh = yf_ref[1, x, y, i : i + 1, :]
+                yl = yf_ref[0, x, i, y : y + 1, :]
+                yh = yf_ref[1, x, i, y : y + 1, :]
                 zn = z_neighbours(s, halo, (x * B + y) * V + i, flag, lanes)
                 r = source_ref[x, y, i] - (yl + yh + 1.0) * s + yl * below + yh * above
                 r_ref[x, y, i] = r + 0.5 * zn - spec[i]
@@ -257,8 +250,8 @@
         v0, v1, v2, last = condense(
             fac_ref, y,
             lambda t: [r_ref[t, y, i] for i in range(V)],
-            lambda t: [xf_ref[0, t, y, i : i + 1, :] for i in range(V)],
-            lambda t: [xf_ref[1, t, y, i : i + 1, :] for i in range(V)],
+            lambda t: [xf_ref[0, t, i, y : y + 1, :] for i in range(V)],
+            lambda t: [xf_ref[1, t, i, y : y + 1, :] for i in range(V)],
         )
         for i in range(V):
             v_ref[0, y, i] = v0[i]
@@ -273,28 +266,32 @@
         msg_ref[d, 40:XR, :] = xmat_ref[d * MR : (d + 1) * MR, :]
 
 
-def reduce_lines(a, b, c, r, shifted, steps, kk, nn, bi):
-    for step in range(steps):
+def minus_product(out, a, m, keep=True):
+    for i in range(V):
+        row = [a[i * V + k] for k in range(V)]
+        for j in range(V):
+            p = dot([(row[k], m[k * V + j]) for k in range(V)])
+            out[i * V + j] = out[i * V + j] - p if keep else -p
+
+
+def left_apply(inv, src, dst):
+    m = [src[e] for e in range(25)]
+    for i in range(V):
+        row = [inv[i * V + k] for k in range(V)]
+        for j in range(V):
+            dst[i * V + j] = dot([(row[k], m[k * V + j]) for k in range(V)])
+
+
+def reduce_lines(a, b, c, r, shifted, steps, kk, nn, bi, lower):
+    def invert():
         inv = inverse([b[e] for e in range(25)])
         for e in range(25):
             bi[e] = inv[e]
-        last = step == steps - 1
-        for dst, src in ((kk, a), (nn, c)):
-            m = [src[e] for e in range(25)]
-            for i in range(V):
-                row = [bi[i * V + k] for k in range(V)]
-                for j in range(V):
-                    dst[i * V + j] = dot([(row[k], m[k * V + j]) for k in range(V)])
-        m = [shifted(nn[e], step, -1) for e in range(25)]
-        for i in range(V):
-            row = [a[i * V + k] for k in range(V)]
-            for j in range(V):
-                b[i * V + j] = b[i * V + j] - dot([(row[k], m[k * V + j]) for k in range(V)])
-        m = [shifted(kk[e], step, 1) for e in range(25)]
-        for i in range(V):
-            row = [c[i * V + k] for k in range(V)]
-            for j in range(V):
-                b[i * V + j] = b[i * V + j] - dot([(row[k], m[k * V + j]) for k in range(V)])
+
+    for step in range(steps - 1):
+        invert()
+        left_apply(bi, a, kk)
+        left_apply(bi, c, nn)
         for n in range(H):
             old = [r[i * H + n] for i in range(V)]
             hat = [dot([(bi[i * V + k], old[k]) for k in range(V)]) for i in range(V)]
@@ -306,20 +303,22 @@
                     - dot([(a[i * V + k], before[k]) for k in range(V)])
                     - dot([(c[i * V + k], after[k]) for k in range(V)])
                 )
-        if not last:
-            m = [shifted(kk[e], step, -1) for e in range(25)]
-            for i in range(V):
-                row = [a[i * V + k] for k in range(V)]
-                for j in range(V):
-                    a[i * V + j] = -dot([(row[k], m[k * V + j]) for k in range(V)])
-            m = [shifted(nn[e], step, 1) for e in range(25)]
-            for i in range(V):
-                row = [c[i * V + k] for k in range(V)]
-                for j in range(V):
-                    c[i * V + j] = -dot([(row[k], m[k * V + j]) for k in range(V)])
-    inv = inverse([b[e] for e in range(25)])
+        minus_product(b, a, [shifted(nn[e], step, -1) for e in range(25)])
+        minus_product(b, c, [shifted(kk[e], step, 1) for e in range(25)])
+        minus_product(a, a, [shifted(kk[e], step, -1) for e in range(25)], keep=False)
+        minus_product(c, c, [shifted(nn[e], step, 1) for e in range(25)], keep=False)
+    invert()
     for e in range(25):
-        bi[e] = inv[e]
+        a[e] = jnp.where(lower, c[e], a[e])
+    left_apply(bi, a, kk)
+    for n in range(H):
+        old = [r[i * H + n] for i in range(V)]
+        hat = [dot([(bi[i * V + k], old[k]) for k in range(V)]) for i in range(V)]
+        far = [shifted(h, steps - 1, 1) for h in hat]
+        for i in range(V):
+            r[i * H + n] = old[i] - dot([(a[i * V + k], far[k]) for k in range(V)])
+    minus_product(b, a, [shifted(kk[e], steps - 1, 1) for e in range(25)])
+    invert()
     for n in range(H):
         old = [r[i * H + n] for i in range(V)]
         for i in range(V):
@@ -371,9 +370,9 @@
         r[e], first[e] = pair(e)
     close(
         b, c, r, lambda e: fl[e], lambda e: fh[e], lambda i, n: first[i * H + n],
-        lambda i: pair(90 + i)[0], lambda v: after(v, 1), jnp.logical_not(end),
+        lambda i: pair(90 + i // 2)[i % 2], lambda v: after(v, 1), jnp.logical_not(end),
     )
-    reduce_lines(a, b, c, r, shifted, 4, kk, nn, bi)
+    reduce_lines(a, b, c, r, shifted, 4, kk, nn, bi, left)
     for e in range(40):
         u = r[e]
         prev = jnp.where(begin, 0.0, before(u, 1))
@@ -381,14 +380,17 @@
         out_ref[pl.ds(320 + e, 8, stride=40), :] = jnp.where(left, swap(prev), u)
 
 
-def y_solver_kernel(line_ref, msg_ref, mat_ref, out_ref, a, b, c, r, kk, nn, bi):
-    subs = sub()
+def y_solver_kernel(msg_ref, out_ref, a, b, c, r, kk, nn, bi, fh, fl):
+    lanes, subs = lane(), sub()
+    left = lanes < 64
 
     def rhs(row):
         return msg_ref[pl.ds(row, 8, stride=YR), :]
 
-    def mat(row):
-        return mat_ref[:, 0, row, :]
+    def pair(row):
+        p = rhs(row)
+        q = swap(p)
+        return jnp.where(left, p, q), jnp.where(left, q, p)
 
     def before(v, k):
         return pltpu.roll(v, k, 0)
@@ -401,19 +403,20 @@
 
     begin = subs == 0
     for e in range(25):
-        a[e] = jnp.where(begin, 0.0, mat(e))
-        b[e] = mat(25 + e)
+        low, fh[e] = pair(80 + e)
+        a[e] = jnp.where(begin, 0.0, low)
+        b[e], fl[e] = pair(105 + e)
     for e in range(40):
         r[e] = rhs(e)
     close(
-        b, c, r, lambda e: mat(50 + e), lambda e: mat(75 + e), lambda i, n: rhs(40 + i * H + n),
-        lambda i: mat(100 + i), lambda v: after(v, 1), subs != 7,
+        b, c, r, lambda e: fl[e], lambda e: fh[e], lambda i, n: rhs(40 + i * H + n),
+        lambda i: pair(130 + i // 2)[i % 2], lambda v: after(v, 1), subs != 7,
     )
-    reduce_lines(a, b, c, r, shifted, 3, kk, nn, bi)
+    reduce_lines(a, b, c, r, shifted, 3, kk, nn, bi, subs < 4)
     for e in range(40):
         u = r[e]
-        out_ref[pl.ds(e, 8, stride=YR), :] = jnp.where(begin, 0.0, before(u, 1))
-        out_ref[pl.ds(40 + e, 8, stride=YR), :] = u
+        out_ref[pl.ds(e, 8, stride=80), :] = jnp.where(begin, 0.0, before(u, 1))
+        out_ref[pl.ds(40 + e, 8, stride=80), :] = u
 
 
 def middle_kernel(flag_ref, ret_ref, v_ref, fac_ref, h_ref, edge_ref):
@@ -440,8 +443,8 @@
 
 
 def second_kernel(
-    flag_ref, omega_ref, h_ref, source_ref, r_ref, halo_ref, couple_ref, yf_ref, fac_ref, spec_ref,
-    v_ref, msg_ref, table, r2,
+    flag_ref, omega_ref, h_ref, source_ref, r_ref, halo_ref, couple_ref, yf_ref, fac_ref, ymat_ref,
+    spec_ref, v_ref, msg_ref, table, r2,
 ):
     flag = flag_ref[0]
     lanes = lane((N, 128))
@@ -453,41 +456,51 @@
             h = [h_ref[x, y, i] for i in range(V)]
             for i in range(V):
                 zn = z_neighbours(h[i], halo, (x * B + y) * V + i, flag, lanes)
-                c = dot([(couple_ref[x, y, i, k : k + 1, :], h[k]) for k in range(V)])
+                c = dot([(couple_ref[x, i, k, y : y + 1, :], h[k]) for k in range(V)])
                 r = source_ref[x, y, i] - r_ref[x, y, i] + c
                 r2[x, y, i] = r - h[i] + 0.5 * zn - spec[i]
+    left = lane() < 64
     for x in range(B):
         v0, v1, v2, last = condense(
             fac_ref, 4 + x,
             lambda t: [r2[x, t, i] for i in range(V)],
-            lambda t: [yf_ref[0, x, t, i : i + 1, :] for i in range(V)],
-            lambda t: [yf_ref[1, x, t, i : i + 1, :] for i in range(V)],
+            lambda t: [yf_ref[0, x, i, t : t + 1, :] for i in range(V)],
+            lambda t: [yf_ref[1, x, i, t : t + 1, :] for i in range(V)],
         )
         for i in range(V):
             v_ref[x, 0, i] = v0[i]
             v_ref[x, 1, i] = v1[i]
             v_ref[x, 2, i] = v2[i]
-            for ih, (e0, e1) in enumerate(zip(halves(last[i]), halves(v0[i]))):
-                msg_ref[x * 2 + ih, i * H : (i + 1) * H, :] = e0
-                msg_ref[x * 2 + ih, 40 + i * H : 40 + (i + 1) * H, :] = e1
+            for at, v in ((0, last[i]), (40, v0[i])):
+                e0, e1 = halves(v)
+                rows = slice(at + i * H, at + (i + 1) * H)
+                msg_ref[x * 2, rows, :] = jnp.where(left, e0, swap(e1))
+                msg_ref[x * 2 + 1, rows, :] = jnp.where(left, swap(e0), e1)
+    for d in range(8):
+        msg_ref[d, 80:YR, :] = ymat_ref[d * MR : (d + 1) * MR, :]
 
 
 def last_kernel(ret_ref, v_ref, fac_ref, w_ref):
+    left = lane() < 64
+
+    def put(x, y, i, v):
+        w_ref[pl.ds((x * V + i) * N * B + y, N, stride=B), :] = v
+
     for x in range(B):
         prev, cur = [], []
         for i in range(V):
             for out, at in ((prev, 0), (cur, 40)):
-                rows = [
-                    ret_ref[x * 2 + ih, at + i * H : at + (i + 1) * H, :] for ih in range(2)
-                ]
+                z0 = ret_ref[x * 2, at + i * H : at + (i + 1) * H, :]
+                z1 = ret_ref[x * 2 + 1, at + i * H : at + (i + 1) * H, :]
+                rows = [jnp.where(left, z0, swap(z1)), jnp.where(left, swap(z0), z1)]
                 out.append(jnp.concatenate(rows, axis=0)[:N])
         for t in range(B - 1):
             lo = apply(fac_ref, 3 + t, 4 + x, prev)
             hi = apply(fac_ref, 6 + t, 4 + x, cur)
             for i in range(V):
-                w_ref[x, t, i] = v_ref[x, t, i] + lo[i] + hi[i]
-        for i in range(V):
-            w_ref[x, B - 1, i] = cur[i]
+                put(x, t, i, v_ref[x, t, i] + lo[i] + hi[i])
+        for i in range(V):
+            put(x, B - 1, i, cur[i])
 
 
 smem = pl.BlockSpec(memory_space=pltpu.SMEM)
@@ -531,12 +544,15 @@
     before = lax.ppermute(last, "gy", up)
     after = lax.ppermute(first, "gy", down)
     halo = lax.ppermute(lanes, "gz", flip)
+    couple = jnp.transpose(couple, (0, 2, 3, 1, 4))
+    x_faces = jnp.transpose(x_faces, (0, 1, 3, 2, 4))
+    y_faces = jnp.transpose(y_faces, (0, 1, 3, 2, 4))
     fac, xmat, ymat = call(
         matrix_kernel, [vmem] * 3,
-        [sds(225, 8, 128), sds(16 * MR, 128), sds(B * YM, 128)],
+        [sds(225, 8, 128), sds(16 * MR, 128), sds(8 * MR, 128)],
         [scratch(B * 25 * 8, 128), scratch(B * V * 8, 128), scratch(B * V * 8, 128)],
+        cost_estimate=pl.CostEstimate(flops=10**8, bytes_accessed=4 * 10**6, transcendentals=0),
     )(couple, x_faces, y_faces)
-    all_mat = lax.all_gather(ymat, "gy").reshape(n_y, B, YM, 128)
     r1, v, msg = call(
         first_kernel, [smem, smem] + [vmem] * 10,
         [field, sds(B - 1, B, V, N, 128), sds(16, XR, 128)],
@@ -554,29 +570,18 @@
     )(flag, back, v, fac)
     halo = lax.ppermute(edge, "gz", flip)
     v, msg = call(
-        second_kernel, [smem, smem] + [vmem] * 8,
+        second_kernel, [smem, smem] + [vmem] * 9,
         [sds(B, B - 1, V, N, 128), sds(8, YR, 128)],
         [scratch(N, N, 128), scratch(B, B, V, N, 128)],
-    )(flag, omega, h, source, r1, halo, couple, y_faces, fac, spec)
+    )(flag, omega, h, source, r1, halo, couple, y_faces, fac, ymat, spec)
     got = lax.all_to_all(msg, "gy", 0, 0, tiled=True)
-    line = (lax.axis_index("gy") // 2).astype(jnp.int32).reshape(1)
-    ret = pl.pallas_call(
-        y_solver_kernel,
-        grid_spec=pltpu.PrefetchScalarGridSpec(
-            num_scalar_prefetch=1,
-            grid=(1,),
-            in_specs=[
-                pl.BlockSpec((8 * YR, 128), lambda i, line: (0, 0)),
-                pl.BlockSpec((8, 1, YM, 128), lambda i, line: (0, line[0], 0, 0)),
-            ],
-            out_specs=pl.BlockSpec((8 * YR, 128), lambda i, line: (0, 0)),
-            scratch_shapes=mats,
-        ),
-        out_shape=sds(8 * YR, 128),
-        compiler_params=pltpu.CompilerParams(vmem_limit_bytes=40 * 2**20),
-    )(line, got.reshape(8 * YR, 128), all_mat)
-    back = lax.all_to_all(ret.reshape(8, YR, 128), "gy", 0, 0, tiled=True)
-    return call(last_kernel, [vmem] * 3, field)(back, v, fac)
+    ret = call(
+        y_solver_kernel, [vmem], sds(8 * 80, 128),
+        mats + [scratch(25, 8, 128), scratch(25, 8, 128)],
+    )(got.reshape(8 * YR, 128))
+    back = lax.all_to_all(ret.reshape(8, 80, 128), "gy", 0, 0, tiled=True)
+    out = call(last_kernel, [vmem] * 3, sds(B * V * N * B, 128))(back, v, fac)
+    return jnp.transpose(out.reshape(B, V, N, B, 128), (0, 3, 1, 2, 4))
 
 
 def solution(mesh):

time: 114 us -> 97.4 us (0.85)
  blocking collectives: 44.9 us -> 68.7 us
  waiting for transfers between devices: 18.4 us -> 2.96 us
  between operations: 14.1 us -> 0.78 us
  starting transfers between devices: 18.6 us -> 11.1 us
  local copies, waits for them, and re-layouts: 5.56 us -> 2.15 us
    all_to_all x1 -> x2, blocking collectives: 15.2 us -> 39.1 us  [the longest x1 25.6 us: body(): got = lax.all_to_all(msg, 'gy', 0, 0, tiled=True)]
    all_to_all x1 -> x0, waiting for transfers between devices: 13.7 us -> none  [body(): got = lax.all_to_all(msg, 'gy', 0, 0, tiled=True)]
    all_to_all x1 -> x0, starting transfers between devices: 7.66 us -> none  [body(): got = lax.all_to_all(msg, 'gy', 0, 0, tiled=True)]
    unnamed x13 -> x12, local copies, waits for them, and re-layouts: 4.5 us -> 2.15 us
    ppermute x1, waiting for transfers between devices: 3.84 us -> 2.13 us  [body(): after = lax.ppermute(first, 'gy', down)]
  transfers between devices with their start and end apart: 6 -> 4, of which waited for: 4 -> 2; matrix products, arithmetic and copies ran while one was open for 0% -> 0% of each run, Pallas kernels for 7% -> 1%
where the time goes in v1:
time: 97.4 us; the launch traced here: 96.6 us
  blocking collectives  68.7 us (71%)
  starting transfers between devices  11.1 us (11%)
  Pallas kernels  10.9 us (11%)
  waiting for transfers between devices  2.96 us (3%)
  local copies, waits for them, and re-layouts  2.15 us (2%)
    all_to_all x1, blocking collectives, body(): got = lax.all_to_all(msg, 'gy', 0, 0, tiled=True)  25.6 us
    all_to_all x1, blocking collectives, body(): got = lax.all_to_all(msg, 'gx', 0, 0, tiled=True)  18.3 us
    all_to_all x1, blocking collectives, body(): back = lax.all_to_all(ret.reshape(8, 80, 128), 'gy', 0, 0, tiled=True)  13.4 us
    all_to_all x1, blocking collectives, body(): back = lax.all_to_all(ret.reshape(16, 40, 128), 'gx', 0, 0, tiled=True)  11.3 us
    ppermute x1, starting transfers between devices, body(): before = lax.ppermute(last, 'gy', up)  4.38 us
    ppermute x1, starting transfers between devices, body(): halo = lax.ppermute(edge, 'gz', flip)  4.35 us
    pallas_call x1, Pallas kernels, body(): call(x_solver_kernel, [vmem], sds(16 * 40, 128), mats + [scratch(25, 8, 1...  3.04 us
    unnamed x12, local copies, waits for them, and re-layouts  2.15 us
  transfers between devices with their start and end apart: 4, of which 2 were waited for; matrix products, arithmetic and copies ran while one was open for 0% of the time, Pallas kernels for 1%

profile of v1, /device:TPU:1, one launch (start us, length us, event | category | flops | bytes accessed | tf_op | source)
XLA Modules:
  0.0 96.6 jit_solution(6040034582943389303)
XLA Ops:
  0.0 1.1 %copy.9.state_ref = f32[4,4,5,15,128]{4,3,2,1,0:T(8,128)S(1)} copy(f32[4,4,5,15,128]{4,1,3,2,0:T(4,128)} %param.7) | data formatting | bytes 1228800 | tf_op args[0]
  1.1 0.0 copy-start.4
  1.2 0.2 shard_map.73
  1.4 4.4 %collective-permute-start = (f32[4,5,15,128]{3,2,1,0:T(8,128)S(1)}, f32[4,5,15,128]{3,2,1,0:T(8,128)S(1)}, u32[]{:S(2)}, u32[]{:S(2)}) collective-permute-start(f32[4,5,15,128]{3,2,1,0:T(8,128)S(1)} %get-tuple-element.18), channel_id=1, source_target_pairs={{0,2},{2,4},{4,6},{6,8},{8,10},{10,12},{12,14},{1,3},{3,5},{5,7},{... | collective-permute-start | bytes 460808 | tf_op jit(solution)/shard_map/ppermute | solution.py:544
  5.8 1.3 %collective-permute-start.1 = (f32[4,5,15,128]{3,2,1,0:T(8,128)S(1)}, f32[4,5,15,128]{3,2,1,0:T(8,128)S(1)}, u32[]{:S(2)}, u32[]{:S(2)}) collective-permute-start(f32[4,5,15,128]{3,2,1,0:T(8,128)S(1)} %get-tuple-element.19), channel_id=1, source_target_pairs={{2,0},{4,2},{6,4},{8,6},{10,8},{12,10},{14,12},{3,1},{5,3},{7,5},{... | collective-permute-start | bytes 460808 | tf_op jit(solution)/shard_map/ppermute | solution.py:545
  7.1 1.0 %collective-permute-start.2 = (f32[15,128]{1,0:T(8,128)S(1)}, f32[15,128]{1,0:T(8,128)S(1)}, u32[]{:S(2)}, u32[]{:S(2)}) collective-permute-start(f32[15,128]{1,0:T(8,128)S(1)} %get-tuple-element.20), channel_id=1, source_target_pairs={{0,1},{1,0},{2,3},{3,2},{4,5},{5,4},{6,7},{7,6},{8,9},{9,8},{10,11... | collective-permute-start | bytes 23048 | tf_op jit(solution)/shard_map/ppermute | solution.py:546
  8.8 0.0 copy-done.4
  8.8 0.0 copy-start.1
  8.8 0.0 copy-start.2
  8.8 0.0 copy-start.3
  8.8 0.1 copy.10.source_ref
  8.9 0.8 copy-done.1
  9.7 0.1 copy-done.2
  9.8 0.1 copy-done.3
  9.8 0.0 copy-start
  9.8 0.8 shard_map.74
  10.7 0.0 collective-permute-done.2.halo_ref
  10.7 0.0 collective-permute-done.before_ref
  10.7 2.1 %collective-permute-done.1.after_ref = f32[4,5,15,128]{3,2,1,0:T(8,128)S(1)} collective-permute-done((f32[4,5,15,128]{3,2,1,0:T(8,128)S(1)}, f32[4,5,15,128]{3,2,1,0:T(8,128)S(1)}, u32[]{:S(2)}, u32[]{:S(2)}) %collective-permute-start.1) | collective-permute-done | bytes 153632 | tf_op jit(solution)/shard_map/ppermute | solution.py:545
  12.8 0.0 copy-done
  12.8 1.9 %shard_map.75 = (f32[4,4,5,15,128]{4,3,2,1,0:T(8,128)S(1)}, f32[3,4,5,15,128]{4,3,2,1,0:T(8,128)S(1)}, f32[16,96,128]{2,1,0:T(8,128)S(1)}) custom-call(s32[1]{0:T(128)} %bitcast.flag_ref, f32[1]{0:T(128)S(6)} %copy.12.omega_ref, f32[4,4,5,15,128]{4,3,2,1,0:T(8,128)S(1)} %copy.9.state_ref, f32[4,4,5,15,128]{4,3,2,1,0:T(8,128)S(1)} %copy.10.source_ref, ...), custom_call_target="tpu_custom_call" | custom-call | tf_op jit(solution)/shard_map/pallas_call | solution.py:556
  14.7 18.3 %all_to_all.20 = f32[16,96,128]{2,1,0:T(8,128)S(1)} all-to-all(f32[16,96,128]{2,1,0:T(8,128)S(1)} %get-tuple-element.23), channel_id=1, replica_groups=mesh['gx'=16,'gy'=8,'gz'=2] {'gx'}, dimensions={0} | all-to-all | bytes 1572864 | tf_op jit(solution)/shard_map/all_to_all | solution.py:561
  33.0 3.0 %shard_map.76 = f32[640,128]{1,0:T(8,128)S(1)} custom-call(f32[1536,128]{1,0:T(8,128)S(1)} %bitcast.11), custom_call_target="tpu_custom_call" | custom-call | tf_op jit(solution)/shard_map/pallas_call | solution.py:563
  36.0 11.3 %all_to_all.21.ret_ref = f32[16,40,128]{2,1,0:T(8,128)S(1)} all-to-all(f32[16,40,128]{2,1,0:T(8,128)S(1)} %bitcast.14), channel_id=1, replica_groups=mesh['gx'=16,'gy'=8,'gz'=2] {'gx'}, dimensions={0} | all-to-all | bytes 655360 | tf_op jit(solution)/shard_map/all_to_all | solution.py:567
  47.3 0.6 shard_map.77
  48.0 4.4 %collective-permute-start.3 = (f32[15,128]{1,0:T(8,128)S(1)}, f32[15,128]{1,0:T(8,128)S(1)}, u32[]{:S(2)}, u32[]{:S(2)}) collective-permute-start(f32[15,128]{1,0:T(8,128)S(1)} %get-tuple-element.27), channel_id=1, source_target_pairs={{0,1},{1,0},{2,3},{3,2},{4,5},{5,4},{6,7},{7,6},{8,9},{9,8},{10,11... | collective-permute-start | bytes 23048 | tf_op jit(solution)/shard_map/ppermute | solution.py:571
  52.3 0.8 collective-permute-done.3.halo_ref
  53.2 1.7 %shard_map.78 = (f32[4,3,5,15,128]{4,3,2,1,0:T(8,128)S(1)}, f32[8,136,128]{2,1,0:T(8,128)S(1)}) custom-call(s32[1]{0:T(128)} %bitcast.flag_ref, f32[1]{0:T(128)S(6)} %copy.12.omega_ref, f32[4,4,5,15,128]{4,3,2,1,0:T(8,128)S(1)} %get-tuple-element.25.h_ref, f32[4,4,5,15,128]{4,3,2,1,0:T(8,128)S(1)} %copy.10.source_ref, ...), custom_call_target="tpu_custom_call" | custom-call | tf_op jit(solution)/shard_map/pallas_call | solution.py:572
  54.9 25.6 %all_to_all.22 = f32[8,136,128]{2,1,0:T(8,128)S(1)} all-to-all(f32[8,136,128]{2,1,0:T(8,128)S(1)} %get-tuple-element.29), channel_id=1, replica_groups=mesh['gx'=16,'gy'=8,'gz'=2] {'gy'}, dimensions={0} | all-to-all | bytes 1114112 | tf_op jit(solution)/shard_map/all_to_all | solution.py:577
  80.5 1.3 %shard_map.79 = f32[640,128]{1,0:T(8,128)S(1)} custom-call(f32[1088,128]{1,0:T(8,128)S(1)} %bitcast.12), custom_call_target="tpu_custom_call" | custom-call | tf_op jit(solution)/shard_map/pallas_call | solution.py:578
  81.8 13.4 %all_to_all.23.ret_ref = f32[8,80,128]{2,1,0:T(8,128)S(1)} all-to-all(f32[8,80,128]{2,1,0:T(8,128)S(1)} %bitcast.13), channel_id=1, replica_groups=mesh['gx'=16,'gy'=8,'gz'=2] {'gy'}, dimensions={0} | all-to-all | bytes 655360 | tf_op jit(solution)/shard_map/all_to_all | solution.py:582
  95.3 1.3 %shard_map.80 = f32[1200,128]{1,0:T(8,128)} custom-call(f32[8,80,128]{2,1,0:T(8,128)S(1)} %all_to_all.23.ret_ref, f32[4,3,5,15,128]{4,3,2,1,0:T(8,128)S(1)} %get-tuple-element.30.v_ref, f32[225,8,128]{2,1,0:T(8,128)S(1)} %get-tuple-element.21.fac_ref), custom_call_target="tpu_custom_call" | custom-call | tf_op jit(solution)/shard_map/pallas_call | solution.py:583
Async XLA Ops:
  1.1 7.6 %copy-start.4 = (f32[4,4,5,15,128]{4,1,3,2,0:T(4,128)S(1)}, f32[4,4,5,15,128]{4,1,3,2,0:T(4,128)}, u32[]{:S(2)}) copy-start(f32[4,4,5,15,128]{4,1,3,2,0:T(4,128)} %param.8) | copy-start | bytes 1843204
  1.4 9.3 %collective-permute-start = (f32[4,5,15,128]{3,2,1,0:T(8,128)S(1)}, f32[4,5,15,128]{3,2,1,0:T(8,128)S(1)}, u32[]{:S(2)}, u32[]{:S(2)}) collective-permute-start(f32[4,5,15,128]{3,2,1,0:T(8,128)S(1)} %get-tuple-element.18), channel_id=1, source_target_pairs={{0,2},{2,4},{4,6},{6,8},{8,10},{10,12},{12,14},{1,3},{3,5},{5,7},{... | collective-permute-start | bytes 460808 | tf_op jit(solution)/shard_map/ppermute | solution.py:544
  5.8 7.0 %collective-permute-start.1 = (f32[4,5,15,128]{3,2,1,0:T(8,128)S(1)}, f32[4,5,15,128]{3,2,1,0:T(8,128)S(1)}, u32[]{:S(2)}, u32[]{:S(2)}) collective-permute-start(f32[4,5,15,128]{3,2,1,0:T(8,128)S(1)} %get-tuple-element.19), channel_id=1, source_target_pairs={{2,0},{4,2},{6,4},{8,6},{10,8},{12,10},{14,12},{3,1},{5,3},{7,5},{... | collective-permute-start | bytes 460808 | tf_op jit(solution)/shard_map/ppermute | solution.py:545
  7.1 3.6 %collective-permute-start.2 = (f32[15,128]{1,0:T(8,128)S(1)}, f32[15,128]{1,0:T(8,128)S(1)}, u32[]{:S(2)}, u32[]{:S(2)}) collective-permute-start(f32[15,128]{1,0:T(8,128)S(1)} %get-tuple-element.20), channel_id=1, source_target_pairs={{0,1},{1,0},{2,3},{3,2},{4,5},{5,4},{6,7},{7,6},{8,9},{9,8},{10,11... | collective-permute-start | bytes 23048 | tf_op jit(solution)/shard_map/ppermute | solution.py:546
  8.8 0.9 copy-start.1
  8.8 1.0 copy-start.2
  8.8 1.0 %copy-start.3 = (f32[2,4,4,5,128]{4,2,3,1,0:T(4,128)S(1)}, f32[2,4,4,5,128]{4,2,3,1,0:T(4,128)}, u32[]{:S(2)}) copy-start(f32[2,4,4,5,128]{4,2,3,1,0:T(4,128)} %param.9) | copy-start | bytes 245764
  9.8 3.0 %copy-start = (f32[15,15,128]{2,1,0:T(8,128)S(1)}, f32[15,15,128]{2,1,0:T(8,128)}, u32[]{:S(2)}) copy-start(f32[15,15,128]{2,1,0:T(8,128)} %constant.6.clone.spec_ref) | copy-start | bytes 345604
  48.0 5.2 %collective-permute-start.3 = (f32[15,128]{1,0:T(8,128)S(1)}, f32[15,128]{1,0:T(8,128)S(1)}, u32[]{:S(2)}, u32[]{:S(2)}) collective-permute-start(f32[15,128]{1,0:T(8,128)S(1)} %get-tuple-element.27), channel_id=1, source_target_pairs={{0,1},{1,0},{2,3},{3,2},{4,5},{5,4},{6,7},{7,6},{8,9},{9,8},{10,11... | collective-permute-start | bytes 23048 | tf_op jit(solution)/shard_map/ppermute | solution.py:571

commit v2 on v1

v2 whole, which is shorter than its diff:
```python
import functools
import math

import jax
import jax.numpy as jnp
import numpy as np
from jax import lax
from jax.experimental import pallas as pl
from jax.experimental.pallas import tpu as pltpu
from jax.sharding import PartitionSpec as P


V = 5
N = 15
B = 4
H = 8
XR = 96
MR = 56
YR = 136
LINE = B * V * N * B
f32 = jnp.float32


def spectral_columns():
    offsets = np.arange(N)
    gaps = offsets[:, None] - offsets[None, :]
    signs = np.where(gaps % 2 == 0, 1.0, -1.0)
    sine = np.where(gaps == 0, 1.0, np.sin(math.pi * gaps / N))
    table = np.where(gaps == 0, 0.0, 0.5 * signs / sine).astype(np.float32)
    return np.ascontiguousarray(np.broadcast_to(table.T[:, :, None], (N, N, 128)))


def lane(shape=(8, 128)):
    return lax.broadcasted_iota(jnp.int32, shape, len(shape) - 1)


def sub(shape=(8, 128)):
    return lax.broadcasted_iota(jnp.int32, shape, len(shape) - 2)


def swap(v):
    return pltpu.roll(v, 64, 1)


def split(e0, e1):
    far, left = swap(e1), lane() < 64
    return jnp.where(left, e0, far), jnp.where(left, far, e0)


def join(z0, z1):
    left = lane() < 64
    return jnp.where(left, z0, z1), swap(jnp.where(left, z1, z0))


def choose(flag, p, q):
    return jnp.where(flag, q, p), jnp.where(flag, p, q)


def inverse(m):
    m = list(m)
    for p in range(V):
        piv = 1.0 / m[p * V + p]
        for j in range(V):
            if j != p:
                m[p * V + j] = m[p * V + j] * piv
        m[p * V + p] = piv
        for i in range(V):
            if i != p:
                f = m[i * V + p]
                for j in range(V):
                    if j != p:
                        m[i * V + j] = m[i * V + j] - f * m[p * V + j]
                m[i * V + p] = -f * piv
    return m


def dot(terms):
    total = None
    for a, b in terms:
        total = a * b if total is None else total + a * b
    return total


def matmul(a, b):
    return [
        dot([(a[i * V + k], b[k * V + j]) for k in range(V)]) for i in range(V) for j in range(V)
    ]


def edge_kernel(flag_ref, state_ref, near_ref, far_ref):
    even = flag_ref[1] == 0
    for x in range(B):
        for i in range(V):
            at = (x * V + i) * N * B
            first = state_ref[pl.ds(at, N, stride=B), :]
            last = state_ref[pl.ds(at + B - 1, N, stride=B), :]
            near_ref[x, i], far_ref[x, i] = choose(even, first, last)


def pack_edges(load, flag):
    shift = jnp.where(flag == 0, 1, 0)
    lanes = lane((N, 128))
    acc = jnp.zeros((N, 128), f32)
    for c in range(B * B * V):
        x, y, i = c // (B * V), (c // V) % B, c % V
        acc = jnp.where(lanes == c, pltpu.roll(load(x, y, i), shift + c, 1), acc)
    return acc


def z_inner(v, lanes):
    low = jnp.where(lanes == 0, 0.0, pltpu.roll(v, 1, 1))
    high = jnp.where(lanes == 127, 0.0, pltpu.roll(v, 127, 1))
    return low + high


def z_outer(halo, c, flag, lanes):
    edge = jnp.where(flag == 0, 127, 0)
    shift = jnp.where(flag == 0, 127 - c, 128 - c)
    return jnp.where(lanes == edge, pltpu.roll(halo, shift, 1), 0.0)


def matrix_kernel(
    flag_ref, state_ref, couple_ref, xf_ref, yf_ref, fac_ref, xmat_ref, ymat_ref, edge_ref, mel, lo, hi
):
    edge_ref[...] = pack_edges(lambda x, y, i: state_ref[x, y, i], flag_ref[0])
    for a in range(B):
        for i in range(V):
            for j in range(V):
                c = couple_ref[a, i, j]
                e = i * V + j
                mel[(a * 25 + e) * 8 : (a * 25 + e) * 8 + 4, :] = c
                mel[pl.ds(e * 8 + 4 + a, B, stride=25 * 8), :] = c
            lo[(a * V + i) * 8 : (a * V + i) * 8 + 4, :] = xf_ref[0, a, i]
            hi[(a * V + i) * 8 : (a * V + i) * 8 + 4, :] = xf_ref[1, a, i]
            lo[pl.ds(i * 8 + 4 + a, B, stride=V * 8), :] = yf_ref[0, a, i]
            hi[pl.ds(i * 8 + 4 + a, B, stride=V * 8), :] = yf_ref[1, a, i]

    def row(ref, r):
        return ref[r * 8 : r * 8 + 8, :]

    low = [[row(lo, t * V + i) for i in range(V)] for t in range(B)]
    high = [[row(hi, t * V + i) for i in range(V)] for t in range(B)]

    def mid(t):
        m = [row(mel, t * 25 + e) for e in range(25)]
        for i in range(V):
            m[i * V + i] = m[i * V + i] + (low[t][i] + high[t][i])
        return m

    def put(block, m):
        for e in range(25):
            fac_ref[block * 25 + e] = m[e]

    def get(block):
        return [fac_ref[block * 25 + e] for e in range(25)]

    def rows_by(d, m):
        return [d[i] * m[i * V + j] for i in range(V) for j in range(V)]

    def cols_by(m, d):
        return [m[i * V + j] * d[j] for i in range(V) for j in range(V)]

    g0 = inverse(mid(0))
    put(0, g0)
    m1 = mid(1)
    s = rows_by(low[1], cols_by(g0, high[0]))
    g1 = inverse([p - q for p, q in zip(m1, s)])
    put(1, g1)
    m2 = mid(2)
    s = rows_by(low[2], cols_by(g1, high[1]))
    g2 = inverse([p - q for p, q in zip(m2, s)])
    put(2, g2)
    e2 = cols_by(g2, high[2])
    put(8, e2)
    e1 = matmul(get(1), rows_by(high[1], e2))
    put(7, e1)
    e0 = matmul(get(0), rows_by(high[0], e1))
    put(6, e0)
    l0 = cols_by(get(0), low[0])
    l1 = matmul(get(1), rows_by(low[1], l0))
    l2 = matmul(get(2), rows_by(low[2], l1))
    put(5, l2)
    b1 = matmul(get(1), rows_by(high[1], l2))
    l1 = [p + q for p, q in zip(l1, b1)]
    put(4, l1)
    b0 = matmul(get(0), rows_by(high[0], l1))
    l0 = [p + q for p, q in zip(cols_by(get(0), low[0]), b0)]
    put(3, l0)

    lanes = lane()
    m3 = mid(3)
    last_low, last_high = get(5), get(8)
    first_low, first_high = get(3), get(6)

    blocks = [[], [], [], []]
    for i in range(V):
        for j in range(V):
            e = i * V + j
            blocks[0].append(-(low[3][i] * last_low[e]))
            blocks[1].append(m3[e] - low[3][i] * last_high[e])
            blocks[2].append(first_low[e])
            blocks[3].append(first_high[e])
    zero = jnp.zeros((8, 128), f32)
    edge = [high[3][i] for i in range(V)]
    odd = flag_ref[4] == 1
    for r in range(55):
        if r < 50:
            e0, e1 = blocks[0 if r < 25 else 1][r % 25], blocks[3 if r < 25 else 2][r % 25]
        else:
            e0, e1 = edge[r - 50], zero
        for zh, v in enumerate(split(*choose(odd, e0, e1))):
            for ih in range(2):
                xmat_ref[pl.ds((zh * 2 + ih) * MR + r, 4, stride=4 * MR), :] = v[0:4]
        for zh, v in enumerate(split(e0, e1)):
            ymat_ref[pl.ds(zh * MR + r, 4, stride=2 * MR), :] = v[4:8]
    for d in range(16):
        xmat_ref[d * MR + 55 : (d + 1) * MR, :] = jnp.zeros((1, 128), f32)
    for d in range(8):
        ymat_ref[d * MR + 55 : (d + 1) * MR, :] = jnp.zeros((1, 128), f32)


def halves(v):
    return v[0:H], jnp.concatenate([v[H:N], jnp.zeros((1, 128), f32)], axis=0)


def apply(fac_ref, block, line, vec):
    out = []
    for i in range(V):
        out.append(
            dot([(fac_ref[block * 25 + i * V + k, line : line + 1, :], vec[k]) for k in range(V)])
        )
    return out


def condense(fac_ref, line, right, low, high):
    y0 = apply(fac_ref, 0, line, right(0))
    y1 = apply(fac_ref, 1, line, [r + l * y for r, l, y in zip(right(1), low(1), y0)])
    v2 = apply(fac_ref, 2, line, [r + l * y for r, l, y in zip(right(2), low(2), y1)])
    c1 = apply(fac_ref, 1, line, [h * v for h, v in zip(high(1), v2)])
    v1 = [p + q for p, q in zip(y1, c1)]
    c0 = apply(fac_ref, 0, line, [h * v for h, v in zip(high(0), v1)])
    v0 = [p + q for p, q in zip(y0, c0)]
    last = [r + l * v for r, l, v in zip(right(3), low(3), v2)]
    return v0, v1, v2, last


def spectral_terms(load, table, lanes_shape=(N, 128)):
    acc = [None] * V
    for k in range(N):
        t = table[k]
        for i in range(V):
            p = t * load(i, k)
            acc[i] = p if acc[i] is None else acc[i] + p
    return acc


def scaled_table(spec_ref, omega_ref, table):
    table[...] = spec_ref[...] * omega_ref[0]


def inner_kernel(omega_ref, state_ref, source_ref, yf_ref, spec_ref, r_ref, table):
    lanes = lane((N, 128))
    scaled_table(spec_ref, omega_ref, table)
    for y in range(B):
        for x in range(B):
            spec = spectral_terms(lambda i, k: state_ref[x, y, i, k : k + 1, :], table)
            for i in range(V):
                s = state_ref[x, y, i]
                yl = yf_ref[0, x, i, y : y + 1, :]
                yh = yf_ref[1, x, i, y : y + 1, :]
                r = source_ref[x, y, i] - (yl + yh + 1.0) * s + 0.5 * z_inner(s, lanes)
                if y > 0:
                    r = r + yl * state_ref[x, y - 1, i]
                if y < B - 1:
                    r = r + yh * state_ref[x, y + 1, i]
                r_ref[x, y, i] = r - spec[i]


def first_kernel(
    flag_ref, part_ref, near_ref, far_ref, halo_ref, xf_ref, yf_ref, fac_ref, xmat_ref,
    r_ref, v_ref, msg_ref,
):
    flag = flag_ref[0]
    lanes = lane((N, 128))
    halo = halo_ref[...]
    even, begin, end = flag_ref[1] == 0, flag_ref[2] == 0, flag_ref[2] == flag_ref[3] - 1
    odd = flag_ref[4] == 1
    for y in range(B):
        for x in range(B):
            for i in range(V):
                r = part_ref[x, y, i] + 0.5 * z_outer(halo, (x * B + y) * V + i, flag, lanes)
                if y == 0:
                    below = jnp.where(even, far_ref[x, i], near_ref[x, i])
                    r = r + yf_ref[0, x, i, y : y + 1, :] * jnp.where(begin, 0.0, below)
                if y == B - 1:
                    above = jnp.where(even, near_ref[x, i], far_ref[x, i])
                    r = r + yf_ref[1, x, i, y : y + 1, :] * jnp.where(end, 0.0, above)
                r_ref[x, y, i] = r
    for y in range(B):
        v0, v1, v2, last = condense(
            fac_ref, y,
            lambda t: [r_ref[t, y, i] for i in range(V)],
            lambda t: [xf_ref[0, t, i, y : y + 1, :] for i in range(V)],
            lambda t: [xf_ref[1, t, i, y : y + 1, :] for i in range(V)],
        )
        for i in range(V):
            v_ref[0, y, i] = v0[i]
            v_ref[1, y, i] = v1[i]
            v_ref[2, y, i] = v2[i]
            for ih, (e0, e1) in enumerate(zip(halves(last[i]), halves(v0[i]))):
                for zh, v in enumerate(split(*choose(odd, e0, e1))):
                    msg_ref[y * 4 + zh * 2 + ih, i * H : (i + 1) * H, :] = v
    for d in range(16):
        msg_ref[d, 40:XR, :] = xmat_ref[d * MR : (d + 1) * MR, :]


def minus_product(out, a, m, keep=True, into=None):
    into = out if into is None else into
    for i in range(V):
        row = [a[i * V + k] for k in range(V)]
        for j in range(V):
            p = dot([(row[k], m[k * V + j]) for k in range(V)])
            into[i * V + j] = out[i * V + j] - p if keep else -p


def left_apply(inv, src, dst):
    m = [src[e] for e in range(25)]
    for i in range(V):
        row = [inv[i * V + k] for k in range(V)]
        for j in range(V):
            dst[i * V + j] = dot([(row[k], m[k * V + j]) for k in range(V)])


def reduce_lines(a, b, c, r, around, far, steps, kk, nn, bi, lower):
    def invert():
        inv = inverse([b[e] for e in range(25)])
        for e in range(25):
            bi[e] = inv[e]

    for step in range(steps - 1):
        k = 2**step
        invert()
        left_apply(bi, a, kk)
        left_apply(bi, c, nn)
        for n in range(H):
            old = [r[i * H + n] for i in range(V)]
            hat = [dot([(bi[i * V + q], old[q]) for q in range(V)]) for i in range(V)]
            near = [around(h, k) for h in hat]
            for i in range(V):
                r[i * H + n] = (
                    old[i]
                    - dot([(a[i * V + q], near[q][0]) for q in range(V)])
                    - dot([(c[i * V + q], near[q][1]) for q in range(V)])
                )
        near = [around(nn[e], k) for e in range(25)]
        minus_product(b, a, [v[0] for v in near])
        minus_product(c, c, [v[1] for v in near], keep=False, into=nn)
        near = [around(kk[e], k) for e in range(25)]
        minus_product(b, c, [v[1] for v in near])
        minus_product(a, a, [v[0] for v in near], keep=False)
        for e in range(25):
            c[e] = nn[e]
    invert()
    for e in range(25):
        a[e] = jnp.where(lower, c[e], a[e])
    left_apply(bi, a, kk)
    for n in range(H):
        old = [r[i * H + n] for i in range(V)]
        hat = [dot([(bi[i * V + q], old[q]) for q in range(V)]) for i in range(V)]
        other = [far(h) for h in hat]
        for i in range(V):
            r[i * H + n] = old[i] - dot([(a[i * V + q], other[q]) for q in range(V)])
    minus_product(b, a, [far(kk[e]) for e in range(25)])
    invert()
    for n in range(H):
        old = [r[i * H + n] for i in range(V)]
        for i in range(V):
            r[i * H + n] = dot([(bi[i * V + q], old[q]) for q in range(V)])


def close(b, c, r, fl, fh, first, edge, edge_ok):
    for i in range(V):
        h = jnp.where(edge_ok, edge(i), 0.0)
        for j in range(V):
            e = i * V + j
            c[e] = -(h * fh(e))
            b[e] = b[e] - h * fl(e)
        for n in range(H):
            r[i * H + n] = r[i * H + n] + h * first(i * H + n)


def x_solver_kernel(flag_ref, msg_ref, out_ref, a, b, c, r, kk, nn, bi):
    lanes, subs = lane(), sub()
    even = lanes < 64
    even = jnp.logical_xor(even, flag_ref[5] == 1)

    def pair(row):
        return [msg_ref[pl.ds(row + p * XR, 8, stride=2 * XR), :] for p in range(2)]

    def own(row):
        p, q = pair(row)
        return jnp.where(even, p, q)

    def following(row):
        p, q = pair(row)
        v = jnp.where(even, q, p)
        return jnp.where(even, v, pltpu.roll(v, 7, 0))

    def around(v, k):
        if k > 1:
            return pltpu.roll(v, k // 2, 0), pltpu.roll(v, 8 - k // 2, 0)
        v = swap(v)
        return jnp.where(even, pltpu.roll(v, 1, 0), v), jnp.where(even, v, pltpu.roll(v, 7, 0))

    def far(v):
        return pltpu.roll(v, 4, 0)

    begin = (subs == 0) & even
    end = (subs == 7) & jnp.logical_not(even)
    for e in range(25):
        a[e] = jnp.where(begin, 0.0, own(40 + e))
        b[e] = own(65 + e)
    for e in range(40):
        r[e] = own(e)
    close(
        b, c, r, lambda e: following(65 + e), lambda e: following(40 + e), following,
        lambda i: own(90 + i), jnp.logical_not(end),
    )
    reduce_lines(a, b, c, r, around, far, 4, kk, nn, bi, subs < 4)
    for e in range(40):
        u = r[e]
        v = swap(u)
        before = jnp.where(subs == 0, 0.0, pltpu.roll(v, 1, 0))
        out_ref[pl.ds(e, 8, stride=80), :] = jnp.where(even, before, v)
        out_ref[pl.ds(40 + e, 8, stride=80), :] = u


def y_solver_kernel(flag_ref, msg_ref, out_ref, a, b, c, r, kk, nn, bi, fh, fl):
    lanes, subs = lane(), sub()
    left = jnp.logical_xor(lanes < 64, flag_ref[6] == 1)

    def rhs(row):
        return msg_ref[pl.ds(row, 8, stride=YR), :]

    def following(v):
        return pltpu.roll(v, 7, 0)

    def pair(row):
        p = rhs(80 + row)
        q = swap(p)
        return jnp.where(left, p, q), jnp.where(left, q, p)

    def around(v, k):
        return pltpu.roll(v, k, 0), pltpu.roll(v, 8 - k, 0)

    begin = subs == 0
    for e in range(25):
        low, fh[e] = pair(e)
        a[e] = jnp.where(begin, 0.0, low)
        b[e], fl[e] = pair(25 + e)
    for e in range(40):
        r[e] = rhs(e)
    close(
        b, c, r, lambda e: following(fl[e]), lambda e: following(fh[e]),
        lambda e: following(rhs(40 + e)), lambda i: pair(50 + i)[0], subs != 7,
    )
    reduce_lines(a, b, c, r, around, lambda v: pltpu.roll(v, 4, 0), 3, kk, nn, bi, subs < 4)
    for e in range(40):
        u = r[e]
        out_ref[pl.ds(e, 8, stride=80), :] = jnp.where(begin, 0.0, pltpu.roll(u, 1, 0))
        out_ref[pl.ds(40 + e, 8, stride=80), :] = u


def middle_kernel(flag_ref, ret_ref, v_ref, fac_ref, h_ref, edge_ref):
    for y in range(B):
        prev, cur = [], []
        for i in range(V):
            um, u = [], []
            for ih in range(2):
                z = [ret_ref[y * 4 + 2 * zh + ih, i * H : (i + 1) * H, :] for zh in range(2)]
                p, q = join(*z)
                um.append(p)
                u.append(q)
            prev.append(jnp.concatenate(um, axis=0)[:N])
            cur.append(jnp.concatenate(u, axis=0)[:N])
        for t in range(B - 1):
            lo = apply(fac_ref, 3 + t, y, prev)
            hi = apply(fac_ref, 6 + t, y, cur)
            for i in range(V):
                h_ref[t, y, i] = v_ref[t, y, i] + lo[i] + hi[i]
        for i in range(V):
            h_ref[B - 1, y, i] = cur[i]
    edge_ref[...] = pack_edges(lambda x, y, i: h_ref[x, y, i], flag_ref[0])


def second_inner_kernel(
    omega_ref, h_ref, source_ref, r_ref, couple_ref, spec_ref, part_ref, table
):
    lanes = lane((N, 128))
    scaled_table(spec_ref, omega_ref, table)
    for x in range(B):
        for y in range(B):
            spec = spectral_terms(lambda i, k: h_ref[x, y, i, k : k + 1, :], table)
            h = [h_ref[x, y, i] for i in range(V)]
            for i in range(V):
                c = dot([(couple_ref[x, i, k, y : y + 1, :], h[k]) for k in range(V)])
                r = source_ref[x, y, i] - r_ref[x, y, i] + c
                part_ref[x, y, i] = r - h[i] + 0.5 * z_inner(h[i], lanes) - spec[i]


def second_kernel(flag_ref, part_ref, halo_ref, yf_ref, fac_ref, ymat_ref, v_ref, msg_ref):
    flag = flag_ref[0]
    lanes = lane((N, 128))
    halo = halo_ref[...]

    def right(x, t, i):
        return part_ref[x, t, i] + 0.5 * z_outer(halo, (x * B + t) * V + i, flag, lanes)

    for x in range(B):
        v0, v1, v2, last = condense(
            fac_ref, 4 + x,
            lambda t: [right(x, t, i) for i in range(V)],
            lambda t: [yf_ref[0, x, i, t : t + 1, :] for i in range(V)],
            lambda t: [yf_ref[1, x, i, t : t + 1, :] for i in range(V)],
        )
        for i in range(V):
            v_ref[x, 0, i] = v0[i]
            v_ref[x, 1, i] = v1[i]
            v_ref[x, 2, i] = v2[i]
            for at, v in ((0, last[i]), (40, v0[i])):
                for zh, m in enumerate(split(*halves(v))):
                    msg_ref[x * 2 + zh, at + i * H : at + (i + 1) * H, :] = m
    for d in range(8):
        msg_ref[d, 80:YR, :] = ymat_ref[d * MR : (d + 1) * MR, :]


def last_kernel(ret_ref, v_ref, fac_ref, w_ref):
    def put(x, y, i, v):
        w_ref[pl.ds((x * V + i) * N * B + y, N, stride=B), :] = v

    for x in range(B):
        prev, cur = [], []
        for i in range(V):
            for out, at in ((prev, 0), (cur, 40)):
                z = [ret_ref[x * 2 + zh, at + i * H : at + (i + 1) * H, :] for zh in range(2)]
                rows = join(*z)
                out.append(jnp.concatenate(rows, axis=0)[:N])
        for t in range(B - 1):
            lo = apply(fac_ref, 3 + t, 4 + x, prev)
            hi = apply(fac_ref, 6 + t, 4 + x, cur)
            for i in range(V):
                put(x, t, i, v_ref[x, t, i] + lo[i] + hi[i])
        for i in range(V):
            put(x, B - 1, i, cur[i])


smem = pl.BlockSpec(memory_space=pltpu.SMEM)
vmem = pl.BlockSpec(memory_space=pltpu.VMEM)


def sds(*shape):
    return jax.ShapeDtypeStruct(shape, f32)


def scratch(*shape):
    return pltpu.VMEM(shape, f32)


def call(kernel, ins, outs, scratches=(), **more):
    single = not isinstance(outs, (list, tuple))
    return pl.pallas_call(
        kernel,
        in_specs=list(ins),
        out_specs=vmem if single else [vmem] * len(outs),
        out_shape=outs,
        scratch_shapes=list(scratches),
        compiler_params=pltpu.CompilerParams(vmem_limit_bytes=40 * 2**20),
        **more,
    )


def cost(us):
    return pl.CostEstimate(flops=0, bytes_accessed=int(us * 3.6e6), transcendentals=0)


def body(state, source, x_faces, y_faces, couple, omega):
    n_y = lax.axis_size("gy")
    at_x = lax.axis_index("gx").astype(jnp.int32)
    at_y = lax.axis_index("gy").astype(jnp.int32)
    at_z = lax.axis_index("gz").astype(jnp.int32)
    flag = jnp.stack(
        [at_z, at_y & 1, at_y, jnp.full((), n_y, jnp.int32), at_x & 1, (at_x >> 1) & 1, at_y & 1]
    )
    spec = jnp.asarray(spectral_columns())
    pairs = [(i, i ^ 1) for i in range(n_y)]
    other_pairs = [(i, (i + 1) % n_y if i % 2 else (i - 1) % n_y) for i in range(n_y)]
    flip = [(0, 1), (1, 0)]
    field = sds(B, B, V, N, 128)
    mats = [scratch(25, 8, 128)] * 3 + [scratch(40, 8, 128)] + [scratch(25, 8, 128)] * 3

    rows = jnp.transpose(state, (0, 2, 3, 1, 4)).reshape(LINE, 128)
    near, far = call(
        edge_kernel, [smem, vmem], [sds(B, V, N, 128), sds(B, V, N, 128)]
    )(flag, rows)
    near = lax.ppermute(near, "gy", pairs)
    far = lax.ppermute(far, "gy", other_pairs)
    couple = jnp.transpose(couple, (0, 2, 3, 1, 4))
    x_faces = jnp.transpose(x_faces, (0, 1, 3, 2, 4))
    y_faces = jnp.transpose(y_faces, (0, 1, 3, 2, 4))
    fac, xmat, ymat, edge = call(
        matrix_kernel, [smem] + [vmem] * 4,
        [sds(225, 8, 128), sds(16 * MR, 128), sds(8 * MR, 128), sds(N, 128)],
        [scratch(B * 25 * 8, 128), scratch(B * V * 8, 128), scratch(B * V * 8, 128)],
        cost_estimate=cost(1),
    )(flag, state, couple, x_faces, y_faces)
    halo = lax.ppermute(edge, "gz", flip)
    part = call(
        inner_kernel, [smem] + [vmem] * 4, field, [scratch(N, N, 128)], cost_estimate=cost(1),
    )(omega, state, source, y_faces, spec)
    r1, v, msg = call(
        first_kernel, [smem] + [vmem] * 8,
        [field, sds(B - 1, B, V, N, 128), sds(16, XR, 128)],
    )(flag, part, near, far, halo, x_faces, y_faces, fac, xmat)
    got = lax.all_to_all(msg, "gx", 0, 0, tiled=True)
    ret = call(x_solver_kernel, [smem, vmem], sds(16 * 40, 128), mats)(
        flag, got.reshape(16 * XR, 128)
    )
    back = lax.all_to_all(ret.reshape(16, 40, 128), "gx", 0, 0, tiled=True)
    h, edge = call(middle_kernel, [smem, vmem, vmem, vmem], [field, sds(N, 128)])(
        flag, back, v, fac
    )
    halo = lax.ppermute(edge, "gz", flip)
    part = call(
        second_inner_kernel, [smem] + [vmem] * 5, field, [scratch(N, N, 128)],
        cost_estimate=cost(1),
    )(omega, h, source, r1, couple, spec)
    v, msg = call(
        second_kernel, [smem] + [vmem] * 5, [sds(B, B - 1, V, N, 128), sds(8, YR, 128)]
    )(flag, part, halo, y_faces, fac, ymat)
    got = lax.all_to_all(msg, "gy", 0, 0, tiled=True)
    ret = call(
        y_solver_kernel, [smem, vmem], sds(8 * 80, 128),
        mats + [scratch(25, 8, 128), scratch(25, 8, 128)],
    )(flag, got.reshape(8 * YR, 128))
    back = lax.all_to_all(ret.reshape(8, 80, 128), "gy", 0, 0, tiled=True)
    out = call(last_kernel, [vmem] * 3, sds(LINE, 128))(back, v, fac)
    return jnp.transpose(out.reshape(B, V, N, B, 128), (0, 3, 1, 2, 4))


def solution(mesh):
    return jax.shard_map(
        body,
        mesh=mesh,
        in_specs=(
            P("gx", "gy", None, None, "gz"),
            P("gx", "gy", None, None, "gz"),
            P(None, "gx", "gy", None, "gz"),
            P(None, "gx", "gy", None, "gz"),
            P("gx", "gy", None, None, "gz"),
            P(),
        ),
        out_specs=P("gx", "gy", None, None, "gz"),
        check_vma=False,
    )
```

time: 97.4 us -> 95.3 us (0.978)
  waiting for transfers between devices: 2.96 us -> 0.01 us
  Pallas kernels: 10.9 us -> 13.5 us
  blocking collectives: 68.7 us -> 67.6 us
    all_to_all x1, blocking collectives: 25.6 us -> 21.3 us  [body(): got = lax.all_to_all(msg, 'gy', 0, 0, tiled=True)]
    pallas_call x7 -> x9, Pallas kernels: 10.3 us -> 12.4 us  [the longest x1 2.69 us: body(): call(x_solver_kernel, [smem, vmem], sds(16 * 40, 128), mats)]
    ppermute x3 -> x2, waiting for transfers between devices: 2.13 us -> 0.01 us  [the longest x1 0.01 us: body(): far = lax.ppermute(far, 'gy', other_pairs)]
    all_to_all x1, blocking collectives: 18.3 us -> 20 us  [body(): got = lax.all_to_all(msg, 'gx', 0, 0, tiled=True)]
    all_to_all x1, blocking collectives: 13.4 us -> 14.7 us  [body(): back = lax.all_to_all(ret.reshape(8, 80, 128), 'gy', 0, 0, tiled=True)]
    ppermute x1 -> x2, starting transfers between devices: 4.35 us -> 3.74 us  [body(): halo = lax.ppermute(edge, 'gz', flip)]
    ppermute x3 -> x2, starting transfers between devices: 6.71 us -> 7.22 us  [the longest x1 4.67 us: body(): far = lax.ppermute(far, 'gy', other_pairs)]
    unnamed x12 -> x14, local copies, waits for them, and re-layouts: 2.15 us -> 2.05 us
  transfers between devices with their start and end apart: 4 -> 4, of which waited for: 2 -> 0; matrix products, arithmetic and copies ran while one was open for 0% -> 0% of each run, Pallas kernels for 1% -> 4%
where the time goes in v2:
time: 95.3 us; the launch traced here: 95 us
  blocking collectives  67.6 us (71%)
  Pallas kernels  13.5 us (14%)
  starting transfers between devices  11 us (12%)
  local copies, waits for them, and re-layouts  2.13 us (2%)
    all_to_all x1, blocking collectives, body(): got = lax.all_to_all(msg, 'gy', 0, 0, tiled=True)  21.3 us
    all_to_all x1, blocking collectives, body(): got = lax.all_to_all(msg, 'gx', 0, 0, tiled=True)  20 us
    all_to_all x1, blocking collectives, body(): back = lax.all_to_all(ret.reshape(8, 80, 128), 'gy', 0, 0, tiled=True)  14.7 us
    all_to_all x1, blocking collectives, body(): back = lax.all_to_all(ret.reshape(16, 40, 128), 'gx', 0, 0, tiled=True)  11.6 us
    ppermute x1, starting transfers between devices, body(): far = lax.ppermute(far, 'gy', other_pairs)  4.67 us
    ppermute x2, starting transfers between devices, body(): halo = lax.ppermute(edge, 'gz', flip)  3.74 us
    pallas_call x1, Pallas kernels, body(): call(x_solver_kernel, [smem, vmem], sds(16 * 40, 128), mats)  2.69 us
    ppermute x1, starting transfers between devices, body(): near = lax.ppermute(near, 'gy', pairs)  2.55 us
  transfers between devices with their start and end apart: 4, of which 0 were waited for; matrix products, arithmetic and copies ran while one was open for 0% of the time, Pallas kernels for 4%

profile of v2, /device:TPU:1, one launch (start us, length us, event | category | flops | bytes accessed | tf_op | source)
XLA Modules:
  0.0 95.0 jit_solution(365112647051451713)
XLA Ops:
  0.0 0.1 stack.24.flag_ref
  0.1 1.1 %copy-done = f32[4,4,5,15,128]{4,1,3,2,0:T(4,128)S(1)} copy-done((f32[4,4,5,15,128]{4,1,3,2,0:T(4,128)S(1)}, f32[4,4,5,15,128]{4,1,3,2,0:T(4,128)}, u32[]{:S(2)}) %copy-start) | copy-done | bytes 614424
  1.2 0.6 shard_map.74
  1.7 2.6 %collective-permute-start = (f32[4,5,15,128]{3,2,1,0:T(8,128)S(1)}, f32[4,5,15,128]{3,2,1,0:T(8,128)S(1)}, u32[]{:S(2)}, u32[]{:S(2)}) collective-permute-start(f32[4,5,15,128]{3,2,1,0:T(8,128)S(1)} %get-tuple-element.18), channel_id=1, source_target_pairs={{0,2},{2,0},{4,6},{6,4},{8,10},{10,8},{12,14},{14,12},{1,3},{3,1},... | collective-permute-start | bytes 460808 | tf_op jit(solution)/shard_map/ppermute | solution.py:605
  4.3 4.7 %collective-permute-start.1 = (f32[4,5,15,128]{3,2,1,0:T(8,128)S(1)}, f32[4,5,15,128]{3,2,1,0:T(8,128)S(1)}, u32[]{:S(2)}, u32[]{:S(2)}) collective-permute-start(f32[4,5,15,128]{3,2,1,0:T(8,128)S(1)} %get-tuple-element.19), channel_id=1, source_target_pairs={{0,14},{2,4},{4,2},{6,8},{8,6},{10,12},{12,10},{14,0},{1,15},{3,5}... | collective-permute-start | bytes 460808 | tf_op jit(solution)/shard_map/ppermute | solution.py:606
  9.0 0.1 copy.8.state_ref
  9.0 0.0 copy-start.5
  9.1 0.0 copy-done.1
  9.1 0.0 copy-done.2
  9.1 0.0 copy-done.4
  9.1 1.4 %shard_map.75 = (f32[225,8,128]{2,1,0:T(8,128)S(1)}, f32[896,128]{1,0:T(8,128)S(1)}, f32[448,128]{1,0:T(8,128)S(1)}, f32[15,128]{1,0:T(8,128)S(1)}) custom-call(s32[7]{0:T(128)S(1)} %stack.24.flag_ref, f32[4,4,5,15,128]{4,3,2,1,0:T(8,128)S(1)} %copy.8.state_ref, f32[4,5,5,4,128]{4,3,2,1,0:T(4,128)S(1)} %bitcast.27, f32[2,4,5,4,128]{4,3,2,1,0:T(4,128)S(1)} %bitcast.29, ...), custom_call_target="tpu_custom_call" | custom-call | bytes 3600000 | tf_op jit(solution)/shard_map/pallas_call | solution.py:610
  10.5 1.3 %collective-permute-start.2 = (f32[15,128]{1,0:T(8,128)S(1)}, f32[15,128]{1,0:T(8,128)S(1)}, u32[]{:S(2)}, u32[]{:S(2)}) collective-permute-start(f32[15,128]{1,0:T(8,128)S(1)} %get-tuple-element.20), channel_id=1, source_target_pairs={{0,1},{1,0},{2,3},{3,2},{4,5},{5,4},{6,7},{7,6},{8,9},{9,8},{10,11... | collective-permute-start | bytes 23048 | tf_op jit(solution)/shard_map/ppermute | solution.py:616
  12.5 0.0 copy-start.3
  12.5 0.1 copy.9.source_ref
  12.6 0.8 copy-done.3
  13.4 1.1 %shard_map.73.part_ref = f32[4,4,5,15,128]{4,3,2,1,0:T(8,128)S(1)} custom-call(f32[1]{0:T(128)S(6)} %copy.12.omega_ref, f32[4,4,5,15,128]{4,3,2,1,0:T(8,128)S(1)} %copy.8.state_ref, f32[4,4,5,15,128]{4,3,2,1,0:T(8,128)S(1)} %copy.9.source_ref, f32[2,4,5,4,128]{4,3,2,1,0:T(4,128)S(1)} %bitcast.22, f32[15,15,128]{2,1,0:T(8,128)S(1)} %copy-done.3), custom_call_target="tpu_custom_call" | custom-call | bytes 3600000 | tf_op jit(solution)/shard_map/pallas_call | solution.py:617
  14.5 0.0 collective-permute-done.2.halo_ref
  14.5 0.0 collective-permute-done.near_ref
  14.5 0.0 collective-permute-done.1.far_ref
  14.5 1.2 %shard_map.76 = (f32[4,4,5,15,128]{4,3,2,1,0:T(8,128)S(1)}, f32[3,4,5,15,128]{4,3,2,1,0:T(8,128)S(1)}, f32[16,96,128]{2,1,0:T(8,128)S(1)}) custom-call(s32[7]{0:T(128)S(1)} %stack.24.flag_ref, f32[4,4,5,15,128]{4,3,2,1,0:T(8,128)S(1)} %shard_map.73.part_ref, f32[4,5,15,128]{3,2,1,0:T(8,128)S(1)} %collective-permute-done.near_ref, ...), custom_call_target="tpu_custom_call" | custom-call | tf_op jit(solution)/shard_map/pallas_call | solution.py:620
  15.7 20.0 %all_to_all.20 = f32[16,96,128]{2,1,0:T(8,128)S(1)} all-to-all(f32[16,96,128]{2,1,0:T(8,128)S(1)} %get-tuple-element.23), channel_id=1, replica_groups=mesh['gx'=16,'gy'=8,'gz'=2] {'gx'}, dimensions={0} | all-to-all | bytes 1572864 | tf_op jit(solution)/shard_map/all_to_all | solution.py:624
  35.7 2.7 %shard_map.77 = f32[640,128]{1,0:T(8,128)S(1)} custom-call(s32[7]{0:T(128)S(1)} %stack.24.flag_ref, f32[1536,128]{1,0:T(8,128)S(1)} %bitcast.18), custom_call_target="tpu_custom_call" | custom-call | tf_op jit(solution)/shard_map/pallas_call | solution.py:625
  38.4 11.6 %all_to_all.21.ret_ref = f32[16,40,128]{2,1,0:T(8,128)S(1)} all-to-all(f32[16,40,128]{2,1,0:T(8,128)S(1)} %bitcast.26), channel_id=1, replica_groups=mesh['gx'=16,'gy'=8,'gz'=2] {'gx'}, dimensions={0} | all-to-all | bytes 655360 | tf_op jit(solution)/shard_map/all_to_all | solution.py:628
  50.0 1.1 %shard_map.78 = (f32[4,4,5,15,128]{4,3,2,1,0:T(8,128)S(1)}, f32[15,128]{1,0:T(8,128)S(1)}) custom-call(s32[7]{0:T(128)S(1)} %stack.24.flag_ref, f32[16,40,128]{2,1,0:T(8,128)S(1)} %all_to_all.21.ret_ref, f32[3,4,5,15,128]{4,3,2,1,0:T(8,128)S(1)} %get-tuple-element.24.v_ref, f32[225,8,128]{2,1,0:T(8,128)S(1)} %get-tuple-element.21.fac_ref), custom_call_target="tpu_custom_call" | custom-call | tf_op jit(solution)/shard_map/pallas_call | solution.py:629
  51.1 2.4 %collective-permute-start.3 = (f32[15,128]{1,0:T(8,128)S(1)}, f32[15,128]{1,0:T(8,128)S(1)}, u32[]{:S(2)}, u32[]{:S(2)}) collective-permute-start(f32[15,128]{1,0:T(8,128)S(1)} %get-tuple-element.27), channel_id=1, source_target_pairs={{0,1},{1,0},{2,3},{3,2},{4,5},{5,4},{6,7},{7,6},{8,9},{9,8},{10,11... | collective-permute-start | bytes 23048 | tf_op jit(solution)/shard_map/ppermute | solution.py:632
  53.5 1.3 %shard_map.79.part_ref = f32[4,4,5,15,128]{4,3,2,1,0:T(8,128)S(1)} custom-call(f32[1]{0:T(128)S(6)} %copy.12.omega_ref, f32[4,4,5,15,128]{4,3,2,1,0:T(8,128)S(1)} %get-tuple-element.25.h_ref, f32[4,4,5,15,128]{4,3,2,1,0:T(8,128)S(1)} %copy.9.source_ref, f32[4,4,5,15,128]{4,3,2,1,0:T(8,128)S(1)} %get-tuple-element.26.r_ref, ...), custom_call_target="tpu_custom_call" | custom-call | bytes 3600000 | tf_op jit(solution)/shard_map/pallas_call | solution.py:633
  54.8 0.0 collective-permute-done.3.halo_ref
  54.8 1.1 %shard_map.80 = (f32[4,3,5,15,128]{4,3,2,1,0:T(8,128)S(1)}, f32[8,136,128]{2,1,0:T(8,128)S(1)}) custom-call(s32[7]{0:T(128)S(1)} %stack.24.flag_ref, f32[4,4,5,15,128]{4,3,2,1,0:T(8,128)S(1)} %shard_map.79.part_ref, f32[15,128]{1,0:T(8,128)S(1)} %collective-permute-done.3.halo_ref, f32[2,4,5,4,128]{4,3,2,1,0:T(4,128)S(1)} %bitcast.24, ...), custom_call_target="tpu_custom_call" | custom-call | tf_op jit(solution)/shard_map/pallas_call | solution.py:637
  55.9 21.3 %all_to_all.22 = f32[8,136,128]{2,1,0:T(8,128)S(1)} all-to-all(f32[8,136,128]{2,1,0:T(8,128)S(1)} %get-tuple-element.29), channel_id=1, replica_groups=mesh['gx'=16,'gy'=8,'gz'=2] {'gy'}, dimensions={0} | all-to-all | bytes 1114112 | tf_op jit(solution)/shard_map/all_to_all | solution.py:640
  77.2 1.9 %shard_map.81 = f32[640,128]{1,0:T(8,128)S(1)} custom-call(s32[7]{0:T(128)S(1)} %stack.24.flag_ref, f32[1088,128]{1,0:T(8,128)S(1)} %bitcast.20), custom_call_target="tpu_custom_call" | custom-call | tf_op jit(solution)/shard_map/pallas_call | solution.py:641
  79.1 14.7 %all_to_all.23.ret_ref = f32[8,80,128]{2,1,0:T(8,128)S(1)} all-to-all(f32[8,80,128]{2,1,0:T(8,128)S(1)} %bitcast.25), channel_id=1, replica_groups=mesh['gx'=16,'gy'=8,'gz'=2] {'gy'}, dimensions={0} | all-to-all | bytes 655360 | tf_op jit(solution)/shard_map/all_to_all | solution.py:645
  93.8 1.2 %shard_map.82 = f32[1200,128]{1,0:T(8,128)} custom-call(f32[8,80,128]{2,1,0:T(8,128)S(1)} %all_to_all.23.ret_ref, f32[4,3,5,15,128]{4,3,2,1,0:T(8,128)S(1)} %get-tuple-element.30.v_ref, f32[225,8,128]{2,1,0:T(8,128)S(1)} %get-tuple-element.21.fac_ref), custom_call_target="tpu_custom_call" | custom-call | tf_op jit(solution)/shard_map/pallas_call | solution.py:646
  (5 shorter events, 0.0 us)
Async XLA Ops:
  0.1 1.1 %copy-start = (f32[4,4,5,15,128]{4,1,3,2,0:T(4,128)S(1)}, f32[4,4,5,15,128]{4,1,3,2,0:T(4,128)}, u32[]{:S(2)}) copy-start(f32[4,4,5,15,128]{4,1,3,2,0:T(4,128)} %param.7) | copy-start | bytes 1843204
  1.7 12.8 %collective-permute-start = (f32[4,5,15,128]{3,2,1,0:T(8,128)S(1)}, f32[4,5,15,128]{3,2,1,0:T(8,128)S(1)}, u32[]{:S(2)}, u32[]{:S(2)}) collective-permute-start(f32[4,5,15,128]{3,2,1,0:T(8,128)S(1)} %get-tuple-element.18), channel_id=1, source_target_pairs={{0,2},{2,0},{4,6},{6,4},{8,10},{10,8},{12,14},{14,12},{1,3},{3,1},... | collective-permute-start | bytes 460808 | tf_op jit(solution)/shard_map/ppermute | solution.py:605
  4.3 4.8 %copy-start.1 = (f32[2,4,4,5,128]{4,2,3,1,0:T(4,128)S(1)}, f32[2,4,4,5,128]{4,2,3,1,0:T(4,128)}, u32[]{:S(2)}) copy-start(f32[2,4,4,5,128]{4,2,3,1,0:T(4,128)} %param.10) | copy-start | bytes 245764
  4.3 4.8 %copy-start.2 = (f32[4,4,5,5,128]{4,1,3,2,0:T(4,128)S(1)}, f32[4,4,5,5,128]{4,1,3,2,0:T(4,128)}, u32[]{:S(2)}) copy-start(f32[4,4,5,5,128]{4,1,3,2,0:T(4,128)} %param.11) | copy-start | bytes 614404
  4.3 4.8 %copy-start.4 = (f32[2,4,4,5,128]{4,2,3,1,0:T(4,128)S(1)}, f32[2,4,4,5,128]{4,2,3,1,0:T(4,128)}, u32[]{:S(2)}) copy-start(f32[2,4,4,5,128]{4,2,3,1,0:T(4,128)} %param.9) | copy-start | bytes 245764
  4.3 10.2 %collective-permute-start.1 = (f32[4,5,15,128]{3,2,1,0:T(8,128)S(1)}, f32[4,5,15,128]{3,2,1,0:T(8,128)S(1)}, u32[]{:S(2)}, u32[]{:S(2)}) collective-permute-start(f32[4,5,15,128]{3,2,1,0:T(8,128)S(1)} %get-tuple-element.19), channel_id=1, source_target_pairs={{0,14},{2,4},{4,2},{6,8},{8,6},{10,12},{12,10},{14,0},{1,15},{3,5}... | collective-permute-start | bytes 460808 | tf_op jit(solution)/shard_map/ppermute | solution.py:606
  9.0 3.4 %copy-start.5 = (f32[4,4,5,15,128]{4,1,3,2,0:T(4,128)S(1)}, f32[4,4,5,15,128]{4,1,3,2,0:T(4,128)}, u32[]{:S(2)}) copy-start(f32[4,4,5,15,128]{4,1,3,2,0:T(4,128)} %param.8) | copy-start | bytes 1843204
  10.5 4.0 %collective-permute-start.2 = (f32[15,128]{1,0:T(8,128)S(1)}, f32[15,128]{1,0:T(8,128)S(1)}, u32[]{:S(2)}, u32[]{:S(2)}) collective-permute-start(f32[15,128]{1,0:T(8,128)S(1)} %get-tuple-element.20), channel_id=1, source_target_pairs={{0,1},{1,0},{2,3},{3,2},{4,5},{5,4},{6,7},{7,6},{8,9},{9,8},{10,11... | collective-permute-start | bytes 23048 | tf_op jit(solution)/shard_map/ppermute | solution.py:616
  12.5 0.9 copy-start.3
  51.1 3.7 %collective-permute-start.3 = (f32[15,128]{1,0:T(8,128)S(1)}, f32[15,128]{1,0:T(8,128)S(1)}, u32[]{:S(2)}, u32[]{:S(2)}) collective-permute-start(f32[15,128]{1,0:T(8,128)S(1)} %get-tuple-element.27), channel_id=1, source_target_pairs={{0,1},{1,0},{2,3},{3,2},{4,5},{5,4},{6,7},{7,6},{8,9},{9,8},{10,11... | collective-permute-start | bytes 23048 | tf_op jit(solution)/shard_map/ppermute | solution.py:632

commit v3 on v2

--- a/solution.py
+++ b/solution.py
@@ -3,7 +3,6 @@
 
 import jax
 import jax.numpy as jnp
-import numpy as np
 from jax import lax
 from jax.experimental import pallas as pl
 from jax.experimental.pallas import tpu as pltpu
@@ -21,13 +20,18 @@
 f32 = jnp.float32
 
 
-def spectral_columns():
-    offsets = np.arange(N)
-    gaps = offsets[:, None] - offsets[None, :]
-    signs = np.where(gaps % 2 == 0, 1.0, -1.0)
-    sine = np.where(gaps == 0, 1.0, np.sin(math.pi * gaps / N))
-    table = np.where(gaps == 0, 0.0, 0.5 * signs / sine).astype(np.float32)
-    return np.ascontiguousarray(np.broadcast_to(table.T[:, :, None], (N, N, 128)))
+def spectral_entry(gap):
+    return 0.0 if gap == 0 else 0.5 * (-1) ** gap / math.sin(math.pi * gap / N)
+
+
+def spectral_table(omega, table):
+    subs = sub((N, 128))
+    entries = {gap: omega * spectral_entry(gap) for gap in range(1 - N, N)}
+    for k in range(N):
+        column = jnp.zeros((N, 128), f32)
+        for j in range(N):
+            column = jnp.where(subs == j, entries[j - k], column)
+        table[k] = column
 
 
 def lane(shape=(8, 128)):
@@ -87,8 +91,8 @@
     ]
 
 
-def edge_kernel(flag_ref, state_ref, near_ref, far_ref):
-    even = flag_ref[1] == 0
+def edge_kernel(state_ref, near_ref, far_ref):
+    even = lax.axis_index("gy") % 2 == 0
     for x in range(B):
         for i in range(V):
             at = (x * V + i) * N * B
@@ -120,9 +124,11 @@
 
 
 def matrix_kernel(
-    flag_ref, state_ref, couple_ref, xf_ref, yf_ref, fac_ref, xmat_ref, ymat_ref, edge_ref, mel, lo, hi
+    omega_ref, state_ref, couple_ref, xf_ref, yf_ref, fac_ref, xmat_ref, ymat_ref,
+    edge_ref, table_ref, mel, lo, hi,
 ):
-    edge_ref[...] = pack_edges(lambda x, y, i: state_ref[x, y, i], flag_ref[0])
+    spectral_table(omega_ref[0], table_ref)
+    edge_ref[...] = pack_edges(lambda x, y, i: state_ref[x, y, i], lax.axis_index("gz"))
     for a in range(B):
         for i in range(V):
             for j in range(V):
@@ -202,20 +208,18 @@
             blocks[3].append(first_high[e])
     zero = jnp.zeros((8, 128), f32)
     edge = [high[3][i] for i in range(V)]
-    odd = flag_ref[4] == 1
+    odd = lax.axis_index("gx") % 2 == 1
     for r in range(55):
         if r < 50:
             e0, e1 = blocks[0 if r < 25 else 1][r % 25], blocks[3 if r < 25 else 2][r % 25]
         else:
             e0, e1 = edge[r - 50], zero
         for zh, v in enumerate(split(*choose(odd, e0, e1))):
-            for ih in range(2):
-                xmat_ref[pl.ds((zh * 2 + ih) * MR + r, 4, stride=4 * MR), :] = v[0:4]
+            xmat_ref[pl.ds(zh * MR + r, 4, stride=2 * MR), :] = v[0:4]
         for zh, v in enumerate(split(e0, e1)):
             ymat_ref[pl.ds(zh * MR + r, 4, stride=2 * MR), :] = v[4:8]
-    for d in range(16):
+    for d in range(8):
         xmat_ref[d * MR + 55 : (d + 1) * MR, :] = jnp.zeros((1, 128), f32)
-    for d in range(8):
         ymat_ref[d * MR + 55 : (d + 1) * MR, :] = jnp.zeros((1, 128), f32)
 
 
@@ -254,13 +258,8 @@
     return acc
 
 
-def scaled_table(spec_ref, omega_ref, table):
-    table[...] = spec_ref[...] * omega_ref[0]
-
-
-def inner_kernel(omega_ref, state_ref, source_ref, yf_ref, spec_ref, r_ref, table):
+def inner_kernel(state_ref, source_ref, yf_ref, table, r_ref):
     lanes = lane((N, 128))
-    scaled_table(spec_ref, omega_ref, table)
     for y in range(B):
         for x in range(B):
             spec = spectral_terms(lambda i, k: state_ref[x, y, i, k : k + 1, :], table)
@@ -277,14 +276,15 @@
 
 
 def first_kernel(
-    flag_ref, part_ref, near_ref, far_ref, halo_ref, xf_ref, yf_ref, fac_ref, xmat_ref,
+    part_ref, near_ref, far_ref, halo_ref, xf_ref, yf_ref, fac_ref, xmat_ref,
     r_ref, v_ref, msg_ref,
 ):
-    flag = flag_ref[0]
+    flag = lax.axis_index("gz")
     lanes = lane((N, 128))
     halo = halo_ref[...]
-    even, begin, end = flag_ref[1] == 0, flag_ref[2] == 0, flag_ref[2] == flag_ref[3] - 1
-    odd = flag_ref[4] == 1
+    at = lax.axis_index("gy")
+    even, begin, end = at % 2 == 0, at == 0, at == lax.axis_size("gy") - 1
+    odd = lax.axis_index("gx") % 2 == 1
     for y in range(B):
         for x in range(B):
             for i in range(V):
@@ -311,66 +311,70 @@
                 for zh, v in enumerate(split(*choose(odd, e0, e1))):
                     msg_ref[y * 4 + zh * 2 + ih, i * H : (i + 1) * H, :] = v
     for d in range(16):
-        msg_ref[d, 40:XR, :] = xmat_ref[d * MR : (d + 1) * MR, :]
-
-
-def minus_product(out, a, m, keep=True, into=None):
-    into = out if into is None else into
+        msg_ref[d, 40:XR, :] = xmat_ref[d // 2 * MR : (d // 2 + 1) * MR, :]
+
+
+def product(a, m):
+    out = []
     for i in range(V):
         row = [a[i * V + k] for k in range(V)]
-        for j in range(V):
-            p = dot([(row[k], m[k * V + j]) for k in range(V)])
-            into[i * V + j] = out[i * V + j] - p if keep else -p
-
-
-def left_apply(inv, src, dst):
-    m = [src[e] for e in range(25)]
-    for i in range(V):
-        row = [inv[i * V + k] for k in range(V)]
-        for j in range(V):
-            dst[i * V + j] = dot([(row[k], m[k * V + j]) for k in range(V)])
-
-
-def reduce_lines(a, b, c, r, around, far, steps, kk, nn, bi, lower):
+        out += [dot([(row[k], m[k * V + j]) for k in range(V)]) for j in range(V)]
+    return out
+
+
+def reduce_lines(a, b, c, r, prepare, before, after, far, steps, kk, nn, bi, lower):
     def invert():
         inv = inverse([b[e] for e in range(25)])
         for e in range(25):
             bi[e] = inv[e]
 
+    def put(dst, m, sign=1):
+        for e in range(25):
+            dst[e] = m[e] if sign > 0 else -m[e]
+
+    def subtract(m):
+        for e in range(25):
+            b[e] = b[e] - m[e]
+
     for step in range(steps - 1):
         k = 2**step
+
+        def low(m):
+            return [before(v, k) for v in m]
+
+        def high(m):
+            return [after(v, k) for v in m]
+
         invert()
-        left_apply(bi, a, kk)
-        left_apply(bi, c, nn)
+        m = [prepare(bi[e], k) for e in range(25)]
+        put(kk, product(a, low(m)))
+        put(nn, product(c, high(m)))
         for n in range(H):
             old = [r[i * H + n] for i in range(V)]
-            hat = [dot([(bi[i * V + q], old[q]) for q in range(V)]) for i in range(V)]
-            near = [around(h, k) for h in hat]
+            m = [prepare(v, k) for v in old]
+            m = low(m), high(m)
             for i in range(V):
                 r[i * H + n] = (
                     old[i]
-                    - dot([(a[i * V + q], near[q][0]) for q in range(V)])
-                    - dot([(c[i * V + q], near[q][1]) for q in range(V)])
+                    - dot([(kk[i * V + q], m[0][q]) for q in range(V)])
+                    - dot([(nn[i * V + q], m[1][q]) for q in range(V)])
                 )
-        near = [around(nn[e], k) for e in range(25)]
-        minus_product(b, a, [v[0] for v in near])
-        minus_product(c, c, [v[1] for v in near], keep=False, into=nn)
-        near = [around(kk[e], k) for e in range(25)]
-        minus_product(b, c, [v[1] for v in near])
-        minus_product(a, a, [v[0] for v in near], keep=False)
-        for e in range(25):
-            c[e] = nn[e]
+        m = [prepare(c[e], k) for e in range(25)]
+        subtract(product(kk, low(m)))
+        put(c, product(nn, high(m)), -1)
+        m = [prepare(a[e], k) for e in range(25)]
+        subtract(product(nn, high(m)))
+        put(a, product(kk, low(m)), -1)
     invert()
     for e in range(25):
         a[e] = jnp.where(lower, c[e], a[e])
-    left_apply(bi, a, kk)
+    put(kk, product(a, [far(bi[e]) for e in range(25)]))
     for n in range(H):
         old = [r[i * H + n] for i in range(V)]
-        hat = [dot([(bi[i * V + q], old[q]) for q in range(V)]) for i in range(V)]
-        other = [far(h) for h in hat]
-        for i in range(V):
-            r[i * H + n] = old[i] - dot([(a[i * V + q], other[q]) for q in range(V)])
-    minus_product(b, a, [far(kk[e]) for e in range(25)])
+        other = [far(v) for v in old]
+        for i in range(V):
+            r[i * H + n] = old[i] - dot([(kk[i * V + q], other[q]) for q in range(V)])
+    subtract(product(kk, [far(a[e]) for e in range(25)]))
     invert()
     for n in range(H):
         old = [r[i * H + n] for i in range(V)]
@@ -378,39 +382,41 @@
             r[i * H + n] = dot([(bi[i * V + q], old[q]) for q in range(V)])
 
 
-def close(b, c, r, fl, fh, first, edge, edge_ok):
+def close(b, c, fl, fh, edge):
     for i in range(V):
-        h = jnp.where(edge_ok, edge(i), 0.0)
         for j in range(V):
             e = i * V + j
-            c[e] = -(h * fh(e))
-            b[e] = b[e] - h * fl(e)
-        for n in range(H):
-            r[i * H + n] = r[i * H + n] + h * first(i * H + n)
-
-
-def x_solver_kernel(flag_ref, msg_ref, out_ref, a, b, c, r, kk, nn, bi):
+            c[e] = -(edge[i] * fh[e])
+            b[e] = b[e] - edge[i] * fl[e]
+
+
+def x_solver_kernel(msg_ref, out_ref, a, b, c, r, kk, nn, bi, fh, fl):
     lanes, subs = lane(), sub()
     even = lanes < 64
-    even = jnp.logical_xor(even, flag_ref[5] == 1)
+    even = jnp.logical_xor(even, lax.axis_index("gx") // 2 % 2 == 1)
 
     def pair(row):
         return [msg_ref[pl.ds(row + p * XR, 8, stride=2 * XR), :] for p in range(2)]
 
-    def own(row):
-        p, q = pair(row)
+    def own(p, q):
         return jnp.where(even, p, q)
 
-    def following(row):
-        p, q = pair(row)
+    def following(p, q):
         v = jnp.where(even, q, p)
         return jnp.where(even, v, pltpu.roll(v, 7, 0))
 
-    def around(v, k):
+    def prepare(v, k):
+        return swap(v) if k == 1 else v
+
+    def before(v, k):
         if k > 1:
-            return pltpu.roll(v, k // 2, 0), pltpu.roll(v, 8 - k // 2, 0)
-        v = swap(v)
-        return jnp.where(even, pltpu.roll(v, 1, 0), v), jnp.where(even, v, pltpu.roll(v, 7, 0))
+            return pltpu.roll(v, k // 2, 0)
+        return jnp.where(even, pltpu.roll(v, 1, 0), v)
+
+    def after(v, k):
+        if k > 1:
+            return pltpu.roll(v, 8 - k // 2, 0)
+        return jnp.where(even, v, pltpu.roll(v, 7, 0))
 
     def far(v):
         return pltpu.roll(v, 4, 0)
@@ -418,15 +424,16 @@
     begin = (subs == 0) & even
     end = (subs == 7) & jnp.logical_not(even)
     for e in range(25):
-        a[e] = jnp.where(begin, 0.0, own(40 + e))
-        b[e] = own(65 + e)
+        p, q = pair(40 + e)
+        a[e], fh[e] = jnp.where(begin, 0.0, own(p, q)), following(p, q)
+        p, q = pair(65 + e)
+        b[e], fl[e] = own(p, q), following(p, q)
+    edge = [jnp.where(end, 0.0, own(*pair(90 + i))) for i in range(V)]
+    close(b, c, fl, fh, edge)
     for e in range(40):
-        r[e] = own(e)
-    close(
-        b, c, r, lambda e: following(65 + e), lambda e: following(40 + e), following,
-        lambda i: own(90 + i), jnp.logical_not(end),
-    )
-    reduce_lines(a, b, c, r, around, far, 4, kk, nn, bi, subs < 4)
+        p, q = pair(e)
+        r[e] = own(p, q) + edge[e // H] * following(p, q)
+    reduce_lines(a, b, c, r, prepare, before, after, far, 4, kk, nn, bi, subs < 4)
     for e in range(40):
         u = r[e]
         v = swap(u)
@@ -435,9 +442,9 @@
         out_ref[pl.ds(40 + e, 8, stride=80), :] = u
 
 
-def y_solver_kernel(flag_ref, msg_ref, out_ref, a, b, c, r, kk, nn, bi, fh, fl):
+def y_solver_kernel(msg_ref, out_ref, a, b, c, r, kk, nn, bi, fh, fl):
     lanes, subs = lane(), sub()
-    left = jnp.logical_xor(lanes < 64, flag_ref[6] == 1)
+    left = jnp.logical_xor(lanes < 64, lax.axis_index("gy") % 2 == 1)
 
     def rhs(row):
         return msg_ref[pl.ds(row, 8, stride=YR), :]
@@ -446,32 +453,32 @@
         return pltpu.roll(v, 7, 0)
 
     def pair(row):
-        p = rhs(80 + row)
+        p = rhs(row)
         q = swap(p)
         return jnp.where(left, p, q), jnp.where(left, q, p)
 
-    def around(v, k):
-        return pltpu.roll(v, k, 0), pltpu.roll(v, 8 - k, 0)
-
     begin = subs == 0
     for e in range(25):
-        low, fh[e] = pair(e)
-        a[e] = jnp.where(begin, 0.0, low)
-        b[e], fl[e] = pair(25 + e)
+        low, high = pair(80 + e)
+        a[e], fh[e] = jnp.where(begin, 0.0, low), following(high)
+        b[e], high = pair(105 + e)
+        fl[e] = following(high)
+    edge = [jnp.where(subs == 7, 0.0, pair(130 + i)[0]) for i in range(V)]
+    close(b, c, fl, fh, edge)
     for e in range(40):
-        r[e] = rhs(e)
-    close(
-        b, c, r, lambda e: following(fl[e]), lambda e: following(fh[e]),
-        lambda e: following(rhs(40 + e)), lambda i: pair(50 + i)[0], subs != 7,
+        r[e] = rhs(e) + edge[e // H] * following(rhs(40 + e))
+    reduce_lines(
+        a, b, c, r, lambda v, k: v, lambda v, k: pltpu.roll(v, k, 0),
+        lambda v, k: pltpu.roll(v, 8 - k, 0), lambda v: pltpu.roll(v, 4, 0),
+        3, kk, nn, bi, subs < 4,
     )
-    reduce_lines(a, b, c, r, around, lambda v: pltpu.roll(v, 4, 0), 3, kk, nn, bi, subs < 4)
     for e in range(40):
         u = r[e]
         out_ref[pl.ds(e, 8, stride=80), :] = jnp.where(begin, 0.0, pltpu.roll(u, 1, 0))
         out_ref[pl.ds(40 + e, 8, stride=80), :] = u
 
 
-def middle_kernel(flag_ref, ret_ref, v_ref, fac_ref, h_ref, edge_ref):
+def middle_kernel(ret_ref, v_ref, fac_ref, h_ref, edge_ref):
     for y in range(B):
         prev, cur = [], []
         for i in range(V):
@@ -490,14 +497,11 @@
                 h_ref[t, y, i] = v_ref[t, y, i] + lo[i] + hi[i]
         for i in range(V):
             h_ref[B - 1, y, i] = cur[i]
-    edge_ref[...] = pack_edges(lambda x, y, i: h_ref[x, y, i], flag_ref[0])
-
-
-def second_inner_kernel(
-    omega_ref, h_ref, source_ref, r_ref, couple_ref, spec_ref, part_ref, table
-):
+    edge_ref[...] = pack_edges(lambda x, y, i: h_ref[x, y, i], lax.axis_index("gz"))
+
+
+def second_inner_kernel(h_ref, source_ref, r_ref, couple_ref, table, part_ref):
     lanes = lane((N, 128))
-    scaled_table(spec_ref, omega_ref, table)
     for x in range(B):
         for y in range(B):
             spec = spectral_terms(lambda i, k: h_ref[x, y, i, k : k + 1, :], table)
@@ -508,8 +512,8 @@
                 part_ref[x, y, i] = r - h[i] + 0.5 * z_inner(h[i], lanes) - spec[i]
 
 
-def second_kernel(flag_ref, part_ref, halo_ref, yf_ref, fac_ref, ymat_ref, v_ref, msg_ref):
-    flag = flag_ref[0]
+def second_kernel(part_ref, halo_ref, yf_ref, fac_ref, ymat_ref, v_ref, msg_ref):
+    flag = lax.axis_index("gz")
     lanes = lane((N, 128))
     halo = halo_ref[...]
 
@@ -585,63 +589,52 @@
 
 def body(state, source, x_faces, y_faces, couple, omega):
     n_y = lax.axis_size("gy")
-    at_x = lax.axis_index("gx").astype(jnp.int32)
-    at_y = lax.axis_index("gy").astype(jnp.int32)
-    at_z = lax.axis_index("gz").astype(jnp.int32)
-    flag = jnp.stack(
-        [at_z, at_y & 1, at_y, jnp.full((), n_y, jnp.int32), at_x & 1, (at_x >> 1) & 1, at_y & 1]
-    )
-    spec = jnp.asarray(spectral_columns())
     pairs = [(i, i ^ 1) for i in range(n_y)]
     other_pairs = [(i, (i + 1) % n_y if i % 2 else (i - 1) % n_y) for i in range(n_y)]
     flip = [(0, 1), (1, 0)]
     field = sds(B, B, V, N, 128)
     mats = [scratch(25, 8, 128)] * 3 + [scratch(40, 8, 128)] + [scratch(25, 8, 128)] * 3
 
-    rows = jnp.transpose(state, (0, 2, 3, 1, 4)).reshape(LINE, 128)
-    near, far = call(
-        edge_kernel, [smem, vmem], [sds(B, V, N, 128), sds(B, V, N, 128)]
-    )(flag, rows)
-    near = lax.ppermute(near, "gy", pairs)
-    far = lax.ppermute(far, "gy", other_pairs)
     couple = jnp.transpose(couple, (0, 2, 3, 1, 4))
     x_faces = jnp.transpose(x_faces, (0, 1, 3, 2, 4))
     y_faces = jnp.transpose(y_faces, (0, 1, 3, 2, 4))
-    fac, xmat, ymat, edge = call(
+    rows = jnp.transpose(state, (0, 2, 3, 1, 4)).reshape(LINE, 128)
+    near, far = call(edge_kernel, [vmem], [sds(B, V, N, 128), sds(B, V, N, 128)])(rows)
+    near = lax.ppermute(near, "gy", pairs)
+    far = lax.ppermute(far, "gy", other_pairs)
+    fac, xmat, ymat, edge, table = call(
         matrix_kernel, [smem] + [vmem] * 4,
-        [sds(225, 8, 128), sds(16 * MR, 128), sds(8 * MR, 128), sds(N, 128)],
+        [
+            sds(225, 8, 128), sds(8 * MR, 128), sds(8 * MR, 128), sds(N, 128),
+            sds(N, N, 128),
+        ],
         [scratch(B * 25 * 8, 128), scratch(B * V * 8, 128), scratch(B * V * 8, 128)],
         cost_estimate=cost(1),
-    )(flag, state, couple, x_faces, y_faces)
+    )(omega, state, couple, x_faces, y_faces)
     halo = lax.ppermute(edge, "gz", flip)
     part = call(
-        inner_kernel, [smem] + [vmem] * 4, field, [scratch(N, N, 128)], cost_estimate=cost(1),
-    )(omega, state, source, y_faces, spec)
+        inner_kernel, [vmem] * 4, field, cost_estimate=cost(1)
+    )(state, source, y_faces, table)
     r1, v, msg = call(
-        first_kernel, [smem] + [vmem] * 8,
+        first_kernel, [vmem] * 8,
         [field, sds(B - 1, B, V, N, 128), sds(16, XR, 128)],
-    )(flag, part, near, far, halo, x_faces, y_faces, fac, xmat)
+    )(part, near, far, halo, x_faces, y_faces, fac, xmat)
     got = lax.all_to_all(msg, "gx", 0, 0, tiled=True)
-    ret = call(x_solver_kernel, [smem, vmem], sds(16 * 40, 128), mats)(
-        flag, got.reshape(16 * XR, 128)
-    )
+    mats += [scratch(25, 8, 128)] * 2
+    ret = call(x_solver_kernel, [vmem], sds(16 * 40, 128), mats)(got.reshape(16 * XR, 128))
     back = lax.all_to_all(ret.reshape(16, 40, 128), "gx", 0, 0, tiled=True)
-    h, edge = call(middle_kernel, [smem, vmem, vmem, vmem], [field, sds(N, 128)])(
-        flag, back, v, fac
-    )
+    h, edge = call(middle_kernel, [vmem] * 3, [field, sds(N, 128)])(back, v, fac)
     halo = lax.ppermute(edge, "gz", flip)
     part = call(
-        second_inner_kernel, [smem] + [vmem] * 5, field, [scratch(N, N, 128)],
-        cost_estimate=cost(1),
-    )(omega, h, source, r1, couple, spec)
+        second_inner_kernel, [vmem] * 5, field, cost_estimate=cost(1)
+    )(h, source, r1, couple, table)
     v, msg = call(
-        second_kernel, [smem] + [vmem] * 5, [sds(B, B - 1, V, N, 128), sds(8, YR, 128)]
-    )(flag, part, halo, y_faces, fac, ymat)
+        second_kernel, [vmem] * 5, [sds(B, B - 1, V, N, 128), sds(8, YR, 128)]
+    )(part, halo, y_faces, fac, ymat)
     got = lax.all_to_all(msg, "gy", 0, 0, tiled=True)
     ret = call(
-        y_solver_kernel, [smem, vmem], sds(8 * 80, 128),
-        mats + [scratch(25, 8, 128), scratch(25, 8, 128)],
-    )(flag, got.reshape(8 * YR, 128))
+        y_solver_kernel, [vmem], sds(8 * 80, 128), mats
+    )(got.reshape(8 * YR, 128))
     back = lax.all_to_all(ret.reshape(8, 80, 128), "gy", 0, 0, tiled=True)
     out = call(last_kernel, [vmem] * 3, sds(LINE, 128))(back, v, fac)
     return jnp.transpose(out.reshape(B, V, N, B, 128), (0, 3, 1, 2, 4))

time: 95.3 us -> 91.3 us (0.958)
  Pallas kernels: 13.5 us -> 9.21 us
  starting transfers between devices: 11 us -> 12.3 us
    pallas_call x9, Pallas kernels: 12.3 us -> 7.87 us  [the longest x1 1.88 us: body(): call(x_solver_kernel, [vmem], sds(16 * 40, 128), mats)]
    ppermute x2, starting transfers between devices: 3.74 us -> 5.09 us  [body(): halo = lax.ppermute(edge, 'gz', flip)]
    all_to_all x1, blocking collectives: 21.3 us -> 22.5 us  [body(): got = lax.all_to_all(msg, 'gy', 0, 0, tiled=True)]
    all_to_all x1, blocking collectives: 20 us -> 18.9 us  [body(): got = lax.all_to_all(msg, 'gx', 0, 0, tiled=True)]
    unnamed x14 -> x12, local copies, waits for them, and re-layouts: 2.05 us -> 1.22 us
  transfers between devices with their start and end apart: 4 -> 4, of which waited for: 0 -> 0; matrix products, arithmetic and copies ran while one was open for 0% -> 0% of each run, Pallas kernels for 4% -> 3%
where the time goes in v3:
time: 91.3 us; the launch traced here: 91.1 us
  blocking collectives  67.5 us (74%)
  starting transfers between devices  12.3 us (13%)
  Pallas kernels  9.21 us (10%)
  local copies, waits for them, and re-layouts  1.22 us (1%)
    all_to_all x1, blocking collectives, body(): got = lax.all_to_all(msg, 'gy', 0, 0, tiled=True)  22.5 us
    all_to_all x1, blocking collectives, body(): got = lax.all_to_all(msg, 'gx', 0, 0, tiled=True)  18.9 us
    all_to_all x1, blocking collectives, body(): back = lax.all_to_all(ret.reshape(8, 80, 128), 'gy', 0, 0, tiled=True)  14.7 us
    all_to_all x1, blocking collectives, body(): back = lax.all_to_all(ret.reshape(16, 40, 128), 'gx', 0, 0, tiled=True)  11.4 us
    ppermute x2, starting transfers between devices, body(): halo = lax.ppermute(edge, 'gz', flip)  5.09 us
    ppermute x1, starting transfers between devices, body(): far = lax.ppermute(far, 'gy', other_pairs)  4.67 us
    ppermute x1, starting transfers between devices, body(): near = lax.ppermute(near, 'gy', pairs)  2.55 us
    pallas_call x1, Pallas kernels, body(): call(x_solver_kernel, [vmem], sds(16 * 40, 128), mats)  1.88 us
  transfers between devices with their start and end apart: 4, of which 0 were waited for; matrix products, arithmetic and copies ran while one was open for 0% of the time, Pallas kernels for 3%

profile of v3, /device:TPU:1, one launch (start us, length us, event | category | flops | bytes accessed | tf_op | source)
XLA Modules:
  0.0 91.1 jit_solution(17064627372646454982)
XLA Ops:
  0.0 0.0 copy-start
  0.0 1.1 %copy-done = f32[4,4,5,15,128]{4,1,3,2,0:T(4,128)S(1)} copy-done((f32[4,4,5,15,128]{4,1,3,2,0:T(4,128)S(1)}, f32[4,4,5,15,128]{4,1,3,2,0:T(4,128)}, u32[]{:S(2)}) %copy-start) | copy-done | bytes 614424
  1.1 2.6 %collective-permute-start = (f32[4,5,15,128]{3,2,1,0:T(8,128)S(1)}, f32[4,5,15,128]{3,2,1,0:T(8,128)S(1)}, u32[]{:S(2)}, u32[]{:S(2)}) collective-permute-start(f32[4,5,15,128]{3,2,1,0:T(8,128)S(1)} %get-tuple-element.20), channel_id=1, source_target_pairs={{0,2},{2,0},{4,6},{6,4},{8,10},{10,8},{12,14},{14,12},{1,3},{3,1},... | collective-permute-start | bytes 460808 | tf_op jit(solution)/shard_map/ppermute | solution.py:603
  3.7 0.0 copy-start.1
  3.7 0.0 copy-start.2
  3.7 4.7 %collective-permute-start.1 = (f32[4,5,15,128]{3,2,1,0:T(8,128)S(1)}, f32[4,5,15,128]{3,2,1,0:T(8,128)S(1)}, u32[]{:S(2)}, u32[]{:S(2)}) collective-permute-start(f32[4,5,15,128]{3,2,1,0:T(8,128)S(1)} %get-tuple-element.21), channel_id=1, source_target_pairs={{0,14},{2,4},{4,2},{6,8},{8,6},{10,12},{12,10},{14,0},{1,15},{3,5}... | collective-permute-start | bytes 460808 | tf_op jit(solution)/shard_map/ppermute | solution.py:604
  8.3 0.1 copy.8.state_ref
  8.4 0.0 copy-start.4
  9.1 0.0 copy-done.1
  9.2 0.0 copy-done.2
  9.2 0.0 copy-done.3
  9.2 0.8 shard_map.64
  9.9 1.3 %collective-permute-start.2 = (f32[15,128]{1,0:T(8,128)S(1)}, f32[15,128]{1,0:T(8,128)S(1)}, u32[]{:S(2)}, u32[]{:S(2)}) collective-permute-start(f32[15,128]{1,0:T(8,128)S(1)} %get-tuple-element.22), channel_id=1, source_target_pairs={{0,1},{1,0},{2,3},{3,2},{4,5},{5,4},{6,7},{7,6},{8,9},{9,8},{10,11... | collective-permute-start | bytes 23048 | tf_op jit(solution)/shard_map/ppermute | solution.py:614
  11.3 0.0 copy-done.4
  11.3 0.1 copy.9.source_ref
  11.3 1.1 %shard_map.65.part_ref = f32[4,4,5,15,128]{4,3,2,1,0:T(8,128)S(1)} custom-call(f32[4,4,5,15,128]{4,3,2,1,0:T(8,128)S(1)} %copy.8.state_ref, f32[4,4,5,15,128]{4,3,2,1,0:T(8,128)S(1)} %copy.9.source_ref, f32[2,4,5,4,128]{4,3,2,1,0:T(4,128)S(1)} %bitcast.17, f32[15,15,128]{2,1,0:T(8,128)S(1)} %get-tuple-element.19.table), custom_call_target="tpu_custom_call" | custom-call | bytes 3600000 | tf_op jit(solution)/shard_map/pallas_call | solution.py:615
  12.4 0.0 collective-permute-done.2.halo_ref
  12.5 0.0 collective-permute-done.near_ref
  12.5 0.0 collective-permute-done.1.far_ref
  12.5 0.7 shard_map.67
  13.1 18.9 %all_to_all.20 = f32[16,96,128]{2,1,0:T(8,128)S(1)} all-to-all(f32[16,96,128]{2,1,0:T(8,128)S(1)} %get-tuple-element.25), channel_id=1, replica_groups=mesh['gx'=16,'gy'=8,'gz'=2] {'gx'}, dimensions={0} | all-to-all | bytes 1572864 | tf_op jit(solution)/shard_map/all_to_all | solution.py:622
  32.0 1.9 %shard_map.68 = f32[640,128]{1,0:T(8,128)S(1)} custom-call(f32[1536,128]{1,0:T(8,128)S(1)} %bitcast.13), custom_call_target="tpu_custom_call" | custom-call | tf_op jit(solution)/shard_map/pallas_call | solution.py:624
  33.9 11.4 %all_to_all.21.ret_ref = f32[16,40,128]{2,1,0:T(8,128)S(1)} all-to-all(f32[16,40,128]{2,1,0:T(8,128)S(1)} %bitcast.21), channel_id=1, replica_groups=mesh['gx'=16,'gy'=8,'gz'=2] {'gx'}, dimensions={0} | all-to-all | bytes 655360 | tf_op jit(solution)/shard_map/all_to_all | solution.py:625
  45.3 0.6 shard_map.69
  45.9 3.8 %collective-permute-start.3 = (f32[15,128]{1,0:T(8,128)S(1)}, f32[15,128]{1,0:T(8,128)S(1)}, u32[]{:S(2)}, u32[]{:S(2)}) collective-permute-start(f32[15,128]{1,0:T(8,128)S(1)} %get-tuple-element.29), channel_id=1, source_target_pairs={{0,1},{1,0},{2,3},{3,2},{4,5},{5,4},{6,7},{7,6},{8,9},{9,8},{10,11... | collective-permute-start | bytes 23048 | tf_op jit(solution)/shard_map/ppermute | solution.py:627
  49.6 1.1 %shard_map.70.part_ref = f32[4,4,5,15,128]{4,3,2,1,0:T(8,128)S(1)} custom-call(f32[4,4,5,15,128]{4,3,2,1,0:T(8,128)S(1)} %get-tuple-element.27.h_ref, f32[4,4,5,15,128]{4,3,2,1,0:T(8,128)S(1)} %copy.9.source_ref, f32[4,4,5,15,128]{4,3,2,1,0:T(8,128)S(1)} %get-tuple-element.28.r_ref, f32[4,5,5,4,128]{4,3,2,1,0:T(4,128)S(1)} %bitcast.23, ...), custom_call_target="tpu_custom_call" | custom-call | bytes 3600000 | tf_op jit(solution)/shard_map/pallas_call | solution.py:628
  50.8 0.0 collective-permute-done.3.halo_ref
  50.8 0.5 shard_map.71
  51.3 22.5 %all_to_all.22 = f32[8,136,128]{2,1,0:T(8,128)S(1)} all-to-all(f32[8,136,128]{2,1,0:T(8,128)S(1)} %get-tuple-element.31), channel_id=1, replica_groups=mesh['gx'=16,'gy'=8,'gz'=2] {'gy'}, dimensions={0} | all-to-all | bytes 1114112 | tf_op jit(solution)/shard_map/all_to_all | solution.py:634
  73.8 1.2 %shard_map.72 = f32[640,128]{1,0:T(8,128)S(1)} custom-call(f32[1088,128]{1,0:T(8,128)S(1)} %bitcast.15), custom_call_target="tpu_custom_call" | custom-call | tf_op jit(solution)/shard_map/pallas_call | solution.py:635
  75.0 14.7 %all_to_all.23.ret_ref = f32[8,80,128]{2,1,0:T(8,128)S(1)} all-to-all(f32[8,80,128]{2,1,0:T(8,128)S(1)} %bitcast.20), channel_id=1, replica_groups=mesh['gx'=16,'gy'=8,'gz'=2] {'gy'}, dimensions={0} | all-to-all | bytes 655360 | tf_op jit(solution)/shard_map/all_to_all | solution.py:638
  89.7 1.3 %shard_map.73 = f32[1200,128]{1,0:T(8,128)} custom-call(f32[8,80,128]{2,1,0:T(8,128)S(1)} %all_to_all.23.ret_ref, f32[4,3,5,15,128]{4,3,2,1,0:T(8,128)S(1)} %get-tuple-element.32.v_ref, f32[225,8,128]{2,1,0:T(8,128)S(1)} %get-tuple-element.23.fac_ref), custom_call_target="tpu_custom_call" | custom-call | tf_op jit(solution)/shard_map/pallas_call | solution.py:639
  (2 shorter events, 0.0 us)
Async XLA Ops:
  0.0 1.1 %copy-start = (f32[4,4,5,15,128]{4,1,3,2,0:T(4,128)S(1)}, f32[4,4,5,15,128]{4,1,3,2,0:T(4,128)}, u32[]{:S(2)}) copy-start(f32[4,4,5,15,128]{4,1,3,2,0:T(4,128)} %param.6) | copy-start | bytes 1843204
  1.1 11.3 %collective-permute-start = (f32[4,5,15,128]{3,2,1,0:T(8,128)S(1)}, f32[4,5,15,128]{3,2,1,0:T(8,128)S(1)}, u32[]{:S(2)}, u32[]{:S(2)}) collective-permute-start(f32[4,5,15,128]{3,2,1,0:T(8,128)S(1)} %get-tuple-element.20), channel_id=1, source_target_pairs={{0,2},{2,0},{4,6},{6,4},{8,10},{10,8},{12,14},{14,12},{1,3},{3,1},... | collective-permute-start | bytes 460808 | tf_op jit(solution)/shard_map/ppermute | solution.py:603
  3.7 5.5 %copy-start.1 = (f32[2,4,4,5,128]{4,2,3,1,0:T(4,128)S(1)}, f32[2,4,4,5,128]{4,2,3,1,0:T(4,128)}, u32[]{:S(2)}) copy-start(f32[2,4,4,5,128]{4,2,3,1,0:T(4,128)} %param.9) | copy-start | bytes 245764
  3.7 5.5 %copy-start.2 = (f32[4,4,5,5,128]{4,1,3,2,0:T(4,128)S(1)}, f32[4,4,5,5,128]{4,1,3,2,0:T(4,128)}, u32[]{:S(2)}) copy-start(f32[4,4,5,5,128]{4,1,3,2,0:T(4,128)} %param.10) | copy-start | bytes 614404
  3.7 5.5 %copy-start.3 = (f32[2,4,4,5,128]{4,2,3,1,0:T(4,128)S(1)}, f32[2,4,4,5,128]{4,2,3,1,0:T(4,128)}, u32[]{:S(2)}) copy-start(f32[2,4,4,5,128]{4,2,3,1,0:T(4,128)} %param.8) | copy-start | bytes 245764
  3.7 8.8 %collective-permute-start.1 = (f32[4,5,15,128]{3,2,1,0:T(8,128)S(1)}, f32[4,5,15,128]{3,2,1,0:T(8,128)S(1)}, u32[]{:S(2)}, u32[]{:S(2)}) collective-permute-start(f32[4,5,15,128]{3,2,1,0:T(8,128)S(1)} %get-tuple-element.21), channel_id=1, source_target_pairs={{0,14},{2,4},{4,2},{6,8},{8,6},{10,12},{12,10},{14,0},{1,15},{3,5}... | collective-permute-start | bytes 460808 | tf_op jit(solution)/shard_map/ppermute | solution.py:604
  8.4 2.8 %copy-start.4 = (f32[4,4,5,15,128]{4,1,3,2,0:T(4,128)S(1)}, f32[4,4,5,15,128]{4,1,3,2,0:T(4,128)}, u32[]{:S(2)}) copy-start(f32[4,4,5,15,128]{4,1,3,2,0:T(4,128)} %param.7) | copy-start | bytes 1843204
  9.9 2.5 %collective-permute-start.2 = (f32[15,128]{1,0:T(8,128)S(1)}, f32[15,128]{1,0:T(8,128)S(1)}, u32[]{:S(2)}, u32[]{:S(2)}) collective-permute-start(f32[15,128]{1,0:T(8,128)S(1)} %get-tuple-element.22), channel_id=1, source_target_pairs={{0,1},{1,0},{2,3},{3,2},{4,5},{5,4},{6,7},{7,6},{8,9},{9,8},{10,11... | collective-permute-start | bytes 23048 | tf_op jit(solution)/shard_map/ppermute | solution.py:614
  45.9 4.9 %collective-permute-start.3 = (f32[15,128]{1,0:T(8,128)S(1)}, f32[15,128]{1,0:T(8,128)S(1)}, u32[]{:S(2)}, u32[]{:S(2)}) collective-permute-start(f32[15,128]{1,0:T(8,128)S(1)} %get-tuple-element.29), channel_id=1, source_target_pairs={{0,1},{1,0},{2,3},{3,2},{4,5},{5,4},{6,7},{7,6},{8,9},{9,8},{10,11... | collective-permute-start | bytes 23048 | tf_op jit(solution)/shard_map/ppermute | solution.py:627

commit v4 on v3

--- a/solution.py
+++ b/solution.py
@@ -93,11 +93,16 @@
 
 def edge_kernel(state_ref, near_ref, far_ref):
     even = lax.axis_index("gy") % 2 == 0
+
+    def line(at):
+        p = state_ref[pl.ds(at, H, stride=B), :]
+        q = state_ref[pl.ds(at + (N - H) * B, H, stride=B), :]
+        return jnp.concatenate([p, q[2 * H - N :]], axis=0)
+
     for x in range(B):
         for i in range(V):
             at = (x * V + i) * N * B
-            first = state_ref[pl.ds(at, N, stride=B), :]
-            last = state_ref[pl.ds(at + B - 1, N, stride=B), :]
+            first, last = line(at), line(at + B - 1)
             near_ref[x, i], far_ref[x, i] = choose(even, first, last)
 
 
@@ -236,15 +241,23 @@
     return out
 
 
-def condense(fac_ref, line, right, low, high):
-    y0 = apply(fac_ref, 0, line, right(0))
-    y1 = apply(fac_ref, 1, line, [r + l * y for r, l, y in zip(right(1), low(1), y0)])
-    v2 = apply(fac_ref, 2, line, [r + l * y for r, l, y in zip(right(2), low(2), y1)])
-    c1 = apply(fac_ref, 1, line, [h * v for h, v in zip(high(1), v2)])
-    v1 = [p + q for p, q in zip(y1, c1)]
-    c0 = apply(fac_ref, 0, line, [h * v for h, v in zip(high(0), v1)])
-    v0 = [p + q for p, q in zip(y0, c0)]
-    last = [r + l * v for r, l, v in zip(right(3), low(3), v2)]
+def condense(fac_ref, at, right, low, high):
+    lines = range(B)
+
+    def each(block, vec):
+        return [apply(fac_ref, block, at + n, vec[n]) for n in lines]
+
+    def plus(p, weights, q):
+        return [[a + w * b for a, w, b in zip(p[n], weights(n), q[n])] for n in lines]
+
+    y0 = each(0, [right(n, 0) for n in lines])
+    y1 = each(1, plus([right(n, 1) for n in lines], lambda n: low(n, 1), y0))
+    v2 = each(2, plus([right(n, 2) for n in lines], lambda n: low(n, 2), y1))
+    c1 = each(1, [[h * v for h, v in zip(high(n, 1), v2[n])] for n in lines])
+    v1 = [[p + q for p, q in zip(y1[n], c1[n])] for n in lines]
+    c0 = each(0, [[h * v for h, v in zip(high(n, 0), v1[n])] for n in lines])
+    v0 = [[p + q for p, q in zip(y0[n], c0[n])] for n in lines]
+    last = plus([right(n, 3) for n in lines], lambda n: low(n, 3), v2)
     return v0, v1, v2, last
 
 
@@ -296,18 +309,18 @@
                     above = jnp.where(even, near_ref[x, i], far_ref[x, i])
                     r = r + yf_ref[1, x, i, y : y + 1, :] * jnp.where(end, 0.0, above)
                 r_ref[x, y, i] = r
+    v0, v1, v2, last = condense(
+        fac_ref, 0,
+        lambda y, t: [r_ref[t, y, i] for i in range(V)],
+        lambda y, t: [xf_ref[0, t, i, y : y + 1, :] for i in range(V)],
+        lambda y, t: [xf_ref[1, t, i, y : y + 1, :] for i in range(V)],
+    )
     for y in range(B):
-        v0, v1, v2, last = condense(
-            fac_ref, y,
-            lambda t: [r_ref[t, y, i] for i in range(V)],
-            lambda t: [xf_ref[0, t, i, y : y + 1, :] for i in range(V)],
-            lambda t: [xf_ref[1, t, i, y : y + 1, :] for i in range(V)],
-        )
-        for i in range(V):
-            v_ref[0, y, i] = v0[i]
-            v_ref[1, y, i] = v1[i]
-            v_ref[2, y, i] = v2[i]
-            for ih, (e0, e1) in enumerate(zip(halves(last[i]), halves(v0[i]))):
+        for i in range(V):
+            v_ref[0, y, i] = v0[y][i]
+            v_ref[1, y, i] = v1[y][i]
+            v_ref[2, y, i] = v2[y][i]
+            for ih, (e0, e1) in enumerate(zip(halves(last[y][i]), halves(v0[y][i]))):
                 for zh, v in enumerate(split(*choose(odd, e0, e1))):
                     msg_ref[y * 4 + zh * 2 + ih, i * H : (i + 1) * H, :] = v
     for d in range(16):
@@ -336,6 +349,7 @@
         for e in range(25):
             b[e] = b[e] - m[e]
 
+    invert()
     for step in range(steps - 1):
         k = 2**step
 
@@ -345,10 +359,16 @@
         def high(m):
             return [after(v, k) for v in m]
 
-        invert()
         m = [prepare(bi[e], k) for e in range(25)]
         put(kk, product(a, low(m)))
         put(nn, product(c, high(m)))
+        mc = [prepare(c[e], k) for e in range(25)]
+        subtract(product(kk, low(mc)))
+        ma = [prepare(a[e], k) for e in range(25)]
+        subtract(product(nn, high(ma)))
+        invert()
+        put(c, product(nn, high(mc)), -1)
+        put(a, product(kk, low(ma)), -1)
         for n in range(H):
             old = [r[i * H + n] for i in range(V)]
             m = [prepare(v, k) for v in old]
@@ -359,27 +379,24 @@
                     - dot([(kk[i * V + q], m[0][q]) for q in range(V)])
                     - dot([(nn[i * V + q], m[1][q]) for q in range(V)])
                 )
-        m = [prepare(c[e], k) for e in range(25)]
-        subtract(product(kk, low(m)))
-        put(c, product(nn, high(m)), -1)
-        m = [prepare(a[e], k) for e in range(25)]
-        subtract(product(nn, high(m)))
-        put(a, product(kk, low(m)), -1)
-    invert()
     for e in range(25):
         a[e] = jnp.where(lower, c[e], a[e])
     put(kk, product(a, [far(bi[e]) for e in range(25)]))
-    for n in range(H):
-        old = [r[i * H + n] for i in range(V)]
-        other = [far(v) for v in old]
-        for i in range(V):
-            r[i * H + n] = old[i] - dot([(kk[i * V + q], other[q]) for q in range(V)])
     subtract(product(kk, [far(a[e]) for e in range(25)]))
     invert()
     for n in range(H):
         old = [r[i * H + n] for i in range(V)]
+        other = [far(v) for v in old]
+        for i in range(V):
+            r[i * H + n] = old[i] - dot([(kk[i * V + q], other[q]) for q in range(V)])
+    for n in range(H):
+        old = [r[i * H + n] for i in range(V)]
         for i in range(V):
             r[i * H + n] = dot([(bi[i * V + q], old[q]) for q in range(V)])
+
+
+def places():
+    return (sub() + 4 * lax.axis_index("gz")) % 8
 
 
 def close(b, c, fl, fh, edge):
@@ -391,7 +408,7 @@
 
 
 def x_solver_kernel(msg_ref, out_ref, a, b, c, r, kk, nn, bi, fh, fl):
-    lanes, subs = lane(), sub()
+    lanes, subs = lane(), places()
     even = lanes < 64
     even = jnp.logical_xor(even, lax.axis_index("gx") // 2 % 2 == 1)
 
@@ -443,7 +460,7 @@
 
 
 def y_solver_kernel(msg_ref, out_ref, a, b, c, r, kk, nn, bi, fh, fl):
-    lanes, subs = lane(), sub()
+    lanes, subs = lane(), places()
     left = jnp.logical_xor(lanes < 64, lax.axis_index("gy") % 2 == 1)
 
     def rhs(row):
@@ -520,18 +537,18 @@
     def right(x, t, i):
         return part_ref[x, t, i] + 0.5 * z_outer(halo, (x * B + t) * V + i, flag, lanes)
 
+    v0, v1, v2, last = condense(
+        fac_ref, 4,
+        lambda x, t: [right(x, t, i) for i in range(V)],
+        lambda x, t: [yf_ref[0, x, i, t : t + 1, :] for i in range(V)],
+        lambda x, t: [yf_ref[1, x, i, t : t + 1, :] for i in range(V)],
+    )
     for x in range(B):
-        v0, v1, v2, last = condense(
-            fac_ref, 4 + x,
-            lambda t: [right(x, t, i) for i in range(V)],
-            lambda t: [yf_ref[0, x, i, t : t + 1, :] for i in range(V)],
-            lambda t: [yf_ref[1, x, i, t : t + 1, :] for i in range(V)],
-        )
-        for i in range(V):
-            v_ref[x, 0, i] = v0[i]
-            v_ref[x, 1, i] = v1[i]
-            v_ref[x, 2, i] = v2[i]
-            for at, v in ((0, last[i]), (40, v0[i])):
+        for i in range(V):
+            v_ref[x, 0, i] = v0[x][i]
+            v_ref[x, 1, i] = v1[x][i]
+            v_ref[x, 2, i] = v2[x][i]
+            for at, v in ((0, last[x][i]), (40, v0[x][i])):
                 for zh, m in enumerate(split(*halves(v))):
                     msg_ref[x * 2 + zh, at + i * H : at + (i + 1) * H, :] = m
     for d in range(8):
@@ -540,7 +557,9 @@
 
 def last_kernel(ret_ref, v_ref, fac_ref, w_ref):
     def put(x, y, i, v):
-        w_ref[pl.ds((x * V + i) * N * B + y, N, stride=B), :] = v
+        at = (x * V + i) * N * B + y
+        w_ref[pl.ds(at, H, stride=B), :] = v[:H]
+        w_ref[pl.ds(at + (N - H) * B, H, stride=B), :] = v[N - H :]
 
     for x in range(B):
         prev, cur = [], []
@@ -583,6 +602,12 @@
     )
 
 
+def exchange(msg, axis):
+    n = lax.axis_size(axis)
+    groups = [[2 * i for i in range(n)], [2 * ((i + n // 2) % n) + 1 for i in range(n)]]
+    return lax.all_to_all(msg, (axis, "gz"), 0, 0, tiled=True, axis_index_groups=groups)
+
+
 def cost(us):
     return pl.CostEstimate(flops=0, bytes_accessed=int(us * 3.6e6), transcendentals=0)
 
@@ -605,10 +630,10 @@
     fac, xmat, ymat, edge, table = call(
         matrix_kernel, [smem] + [vmem] * 4,
         [
-            sds(225, 8, 128), sds(8 * MR, 128), sds(8 * MR, 128), sds(N, 128),
+            sds(225, 8, 128), sds(16 * MR, 128), sds(16 * MR, 128), sds(N, 128),
             sds(N, N, 128),
         ],
-        [scratch(B * 25 * 8, 128), scratch(B * V * 8, 128), scratch(B * V * 8, 128)],
+        [scratch(2 * B * 25 * 8, 128)] + [scratch(2 * B * V * 8, 128)] * 2,
         cost_estimate=cost(1),
     )(omega, state, couple, x_faces, y_faces)
     halo = lax.ppermute(edge, "gz", flip)
@@ -619,10 +644,10 @@
         first_kernel, [vmem] * 8,
         [field, sds(B - 1, B, V, N, 128), sds(16, XR, 128)],
     )(part, near, far, halo, x_faces, y_faces, fac, xmat)
-    got = lax.all_to_all(msg, "gx", 0, 0, tiled=True)
+    got = exchange(msg, "gx")
     mats += [scratch(25, 8, 128)] * 2
     ret = call(x_solver_kernel, [vmem], sds(16 * 40, 128), mats)(got.reshape(16 * XR, 128))
-    back = lax.all_to_all(ret.reshape(16, 40, 128), "gx", 0, 0, tiled=True)
+    back = exchange(ret.reshape(16, 40, 128), "gx")
     h, edge = call(middle_kernel, [vmem] * 3, [field, sds(N, 128)])(back, v, fac)
     halo = lax.ppermute(edge, "gz", flip)
     part = call(
@@ -631,11 +656,11 @@
     v, msg = call(
         second_kernel, [vmem] * 5, [sds(B, B - 1, V, N, 128), sds(8, YR, 128)]
     )(part, halo, y_faces, fac, ymat)
-    got = lax.all_to_all(msg, "gy", 0, 0, tiled=True)
+    got = exchange(msg, "gy")
     ret = call(
         y_solver_kernel, [vmem], sds(8 * 80, 128), mats
     )(got.reshape(8 * YR, 128))
-    back = lax.all_to_all(ret.reshape(8, 80, 128), "gy", 0, 0, tiled=True)
+    back = exchange(ret.reshape(8, 80, 128), "gy")
     out = call(last_kernel, [vmem] * 3, sds(LINE, 128))(back, v, fac)
     return jnp.transpose(out.reshape(B, V, N, B, 128), (0, 3, 1, 2, 4))
 

time: 91.3 us -> 88.2 us (0.966)
  blocking collectives: 67.5 us -> 62.9 us
  starting transfers between devices: 12.3 us -> 13.6 us
    all_to_all x4, blocking collectives: 67.5 us -> 62.9 us  [exchange(): lax.all_to_all(msg, (axis, 'gz'), 0, 0, tiled=True, axis_index_groups=gro...]
    ppermute x2, starting transfers between devices: 5.09 us -> 6.37 us  [body(): halo = lax.ppermute(edge, 'gz', flip)]
  transfers between devices with their start and end apart: 4 -> 4, of which waited for: 0 -> 0; matrix products, arithmetic and copies ran while one was open for 0% -> 0% of each run, Pallas kernels for 3% -> 4%
where the time goes in v4:
time: 88.2 us; the launch traced here: 87.9 us
  blocking collectives  62.9 us (71%)
  starting transfers between devices  13.6 us (15%)
  Pallas kernels  9.32 us (11%)
  local copies, waits for them, and re-layouts  1.22 us (1%)
    all_to_all x4, blocking collectives, exchange(): lax.all_to_all(msg, (axis, 'gz'), 0, 0, tiled=True, axis_index_groups=gro...  62.9 us
    ppermute x2, starting transfers between devices, body(): halo = lax.ppermute(edge, 'gz', flip)  6.37 us
    ppermute x1, starting transfers between devices, body(): far = lax.ppermute(far, 'gy', other_pairs)  4.67 us
    ppermute x1, starting transfers between devices, body(): near = lax.ppermute(near, 'gy', pairs)  2.55 us
    pallas_call x1, Pallas kernels, body(): call(x_solver_kernel, [vmem], sds(16 * 40, 128), mats)  1.89 us
  transfers between devices with their start and end apart: 4, of which 0 were waited for; matrix products, arithmetic and copies ran while one was open for 0% of the time, Pallas kernels for 4%

profile of v4, /device:TPU:1, one launch (start us, length us, event | category | flops | bytes accessed | tf_op | source)
XLA Modules:
  0.0 87.9 jit_solution(9986291899563076011)
XLA Ops:
  0.0 0.0 copy-start
  0.0 1.1 %copy-done = f32[4,4,5,15,128]{4,1,3,2,0:T(4,128)S(1)} copy-done((f32[4,4,5,15,128]{4,1,3,2,0:T(4,128)S(1)}, f32[4,4,5,15,128]{4,1,3,2,0:T(4,128)}, u32[]{:S(2)}) %copy-start) | copy-done | bytes 614424
  1.1 2.6 %collective-permute-start = (f32[4,5,15,128]{3,2,1,0:T(8,128)S(1)}, f32[4,5,15,128]{3,2,1,0:T(8,128)S(1)}, u32[]{:S(2)}, u32[]{:S(2)}) collective-permute-start(f32[4,5,15,128]{3,2,1,0:T(8,128)S(1)} %get-tuple-element.20), channel_id=1, source_target_pairs={{0,2},{2,0},{4,6},{6,4},{8,10},{10,8},{12,14},{14,12},{1,3},{3,1},... | collective-permute-start | bytes 460808 | tf_op jit(solution)/shard_map/ppermute | solution.py:628
  3.7 0.0 copy-start.1
  3.7 0.0 copy-start.2
  3.7 4.7 %collective-permute-start.1 = (f32[4,5,15,128]{3,2,1,0:T(8,128)S(1)}, f32[4,5,15,128]{3,2,1,0:T(8,128)S(1)}, u32[]{:S(2)}, u32[]{:S(2)}) collective-permute-start(f32[4,5,15,128]{3,2,1,0:T(8,128)S(1)} %get-tuple-element.21), channel_id=1, source_target_pairs={{0,14},{2,4},{4,2},{6,8},{8,6},{10,12},{12,10},{14,0},{1,15},{3,5}... | collective-permute-start | bytes 460808 | tf_op jit(solution)/shard_map/ppermute | solution.py:629
  8.3 0.1 copy.8.state_ref
  8.4 0.0 copy-start.4
  9.1 0.0 copy-done.1
  9.1 0.0 copy-done.2
  9.2 0.0 copy-done.3
  9.2 0.8 shard_map.64
  9.9 1.3 %collective-permute-start.2 = (f32[15,128]{1,0:T(8,128)S(1)}, f32[15,128]{1,0:T(8,128)S(1)}, u32[]{:S(2)}, u32[]{:S(2)}) collective-permute-start(f32[15,128]{1,0:T(8,128)S(1)} %get-tuple-element.22), channel_id=1, source_target_pairs={{0,1},{1,0},{2,3},{3,2},{4,5},{5,4},{6,7},{7,6},{8,9},{9,8},{10,11... | collective-permute-start | bytes 23048 | tf_op jit(solution)/shard_map/ppermute | solution.py:639
  11.3 0.0 copy-done.4
  11.3 0.1 copy.9.source_ref
  11.3 1.1 %shard_map.65.part_ref = f32[4,4,5,15,128]{4,3,2,1,0:T(8,128)S(1)} custom-call(f32[4,4,5,15,128]{4,3,2,1,0:T(8,128)S(1)} %copy.8.state_ref, f32[4,4,5,15,128]{4,3,2,1,0:T(8,128)S(1)} %copy.9.source_ref, f32[2,4,5,4,128]{4,3,2,1,0:T(4,128)S(1)} %bitcast.17, f32[15,15,128]{2,1,0:T(8,128)S(1)} %get-tuple-element.19.table), custom_call_target="tpu_custom_call" | custom-call | bytes 3600000 | tf_op jit(solution)/shard_map/pallas_call | solution.py:640
  12.4 0.0 collective-permute-done.2.halo_ref
  12.4 0.0 collective-permute-done.near_ref
  12.5 0.0 collective-permute-done.1.far_ref
  12.5 0.6 shard_map.67
  13.1 16.9 %all_to_all.20 = f32[16,96,128]{2,1,0:T(8,128)S(1)} all-to-all(f32[16,96,128]{2,1,0:T(8,128)S(1)} %get-tuple-element.25), channel_id=1, replica_groups={{0,16,32,48,64,80,96,112,128,144,160,176,192,208,224,240},{129,145,161,..., dimensions={0} | all-to-all | bytes 1572864 | tf_op jit(solution)/shard_map/all_to_all | solution.py:608
  30.0 1.9 %shard_map.68 = f32[640,128]{1,0:T(8,128)S(1)} custom-call(f32[1536,128]{1,0:T(8,128)S(1)} %bitcast.13), custom_call_target="tpu_custom_call" | custom-call | tf_op jit(solution)/shard_map/pallas_call | solution.py:649
  31.9 11.9 %all_to_all.21.ret_ref = f32[16,40,128]{2,1,0:T(8,128)S(1)} all-to-all(f32[16,40,128]{2,1,0:T(8,128)S(1)} %bitcast.21), channel_id=1, replica_groups={{0,16,32,48,64,80,96,112,128,144,160,176,192,208,224,240},{129,145,161,..., dimensions={0} | all-to-all | bytes 655360 | tf_op jit(solution)/shard_map/all_to_all | solution.py:608
  43.8 0.6 shard_map.69
  44.4 5.0 %collective-permute-start.3 = (f32[15,128]{1,0:T(8,128)S(1)}, f32[15,128]{1,0:T(8,128)S(1)}, u32[]{:S(2)}, u32[]{:S(2)}) collective-permute-start(f32[15,128]{1,0:T(8,128)S(1)} %get-tuple-element.29), channel_id=1, source_target_pairs={{0,1},{1,0},{2,3},{3,2},{4,5},{5,4},{6,7},{7,6},{8,9},{9,8},{10,11... | collective-permute-start | bytes 23048 | tf_op jit(solution)/shard_map/ppermute | solution.py:652
  49.4 1.2 %shard_map.70.part_ref = f32[4,4,5,15,128]{4,3,2,1,0:T(8,128)S(1)} custom-call(f32[4,4,5,15,128]{4,3,2,1,0:T(8,128)S(1)} %get-tuple-element.27.h_ref, f32[4,4,5,15,128]{4,3,2,1,0:T(8,128)S(1)} %copy.9.source_ref, f32[4,4,5,15,128]{4,3,2,1,0:T(8,128)S(1)} %get-tuple-element.28.r_ref, f32[4,5,5,4,128]{4,3,2,1,0:T(4,128)S(1)} %bitcast.23, ...), custom_call_target="tpu_custom_call" | custom-call | bytes 3600000 | tf_op jit(solution)/shard_map/pallas_call | solution.py:653
  50.7 0.0 collective-permute-done.3.halo_ref
  50.7 0.5 shard_map.71
  51.2 20.0 %all_to_all.22 = f32[8,136,128]{2,1,0:T(8,128)S(1)} all-to-all(f32[8,136,128]{2,1,0:T(8,128)S(1)} %get-tuple-element.31), channel_id=1, replica_groups={{0,2,4,6,8,10,12,14},{9,11,13,15,1,3,5,7},{16,18,20,22,24,26,28,30},{25..., dimensions={0} | all-to-all | bytes 1114112 | tf_op jit(solution)/shard_map/all_to_all | solution.py:608
  71.2 1.2 %shard_map.72 = f32[640,128]{1,0:T(8,128)S(1)} custom-call(f32[1088,128]{1,0:T(8,128)S(1)} %bitcast.15), custom_call_target="tpu_custom_call" | custom-call | tf_op jit(solution)/shard_map/pallas_call | solution.py:660
  72.4 14.2 %all_to_all.23.ret_ref = f32[8,80,128]{2,1,0:T(8,128)S(1)} all-to-all(f32[8,80,128]{2,1,0:T(8,128)S(1)} %bitcast.20), channel_id=1, replica_groups={{0,2,4,6,8,10,12,14},{9,11,13,15,1,3,5,7},{16,18,20,22,24,26,28,30},{25..., dimensions={0} | all-to-all | bytes 655360 | tf_op jit(solution)/shard_map/all_to_all | solution.py:608
  86.6 1.3 %shard_map.73 = f32[1200,128]{1,0:T(8,128)} custom-call(f32[8,80,128]{2,1,0:T(8,128)S(1)} %all_to_all.23.ret_ref, f32[4,3,5,15,128]{4,3,2,1,0:T(8,128)S(1)} %get-tuple-element.32.v_ref, f32[225,8,128]{2,1,0:T(8,128)S(1)} %get-tuple-element.23.fac_ref), custom_call_target="tpu_custom_call" | custom-call | tf_op jit(solution)/shard_map/pallas_call | solution.py:664
  (2 shorter events, 0.0 us)
Async XLA Ops:
  0.0 1.1 %copy-start = (f32[4,4,5,15,128]{4,1,3,2,0:T(4,128)S(1)}, f32[4,4,5,15,128]{4,1,3,2,0:T(4,128)}, u32[]{:S(2)}) copy-start(f32[4,4,5,15,128]{4,1,3,2,0:T(4,128)} %param.6) | copy-start | bytes 1843204
  1.1 11.3 %collective-permute-start = (f32[4,5,15,128]{3,2,1,0:T(8,128)S(1)}, f32[4,5,15,128]{3,2,1,0:T(8,128)S(1)}, u32[]{:S(2)}, u32[]{:S(2)}) collective-permute-start(f32[4,5,15,128]{3,2,1,0:T(8,128)S(1)} %get-tuple-element.20), channel_id=1, source_target_pairs={{0,2},{2,0},{4,6},{6,4},{8,10},{10,8},{12,14},{14,12},{1,3},{3,1},... | collective-permute-start | bytes 460808 | tf_op jit(solution)/shard_map/ppermute | solution.py:628
  3.7 5.5 %copy-start.1 = (f32[2,4,4,5,128]{4,2,3,1,0:T(4,128)S(1)}, f32[2,4,4,5,128]{4,2,3,1,0:T(4,128)}, u32[]{:S(2)}) copy-start(f32[2,4,4,5,128]{4,2,3,1,0:T(4,128)} %param.9) | copy-start | bytes 245764
  3.7 5.5 %copy-start.2 = (f32[4,4,5,5,128]{4,1,3,2,0:T(4,128)S(1)}, f32[4,4,5,5,128]{4,1,3,2,0:T(4,128)}, u32[]{:S(2)}) copy-start(f32[4,4,5,5,128]{4,1,3,2,0:T(4,128)} %param.10) | copy-start | bytes 614404
  3.7 5.5 %copy-start.3 = (f32[2,4,4,5,128]{4,2,3,1,0:T(4,128)S(1)}, f32[2,4,4,5,128]{4,2,3,1,0:T(4,128)}, u32[]{:S(2)}) copy-start(f32[2,4,4,5,128]{4,2,3,1,0:T(4,128)} %param.8) | copy-start | bytes 245764
  3.7 8.8 %collective-permute-start.1 = (f32[4,5,15,128]{3,2,1,0:T(8,128)S(1)}, f32[4,5,15,128]{3,2,1,0:T(8,128)S(1)}, u32[]{:S(2)}, u32[]{:S(2)}) collective-permute-start(f32[4,5,15,128]{3,2,1,0:T(8,128)S(1)} %get-tuple-element.21), channel_id=1, source_target_pairs={{0,14},{2,4},{4,2},{6,8},{8,6},{10,12},{12,10},{14,0},{1,15},{3,5}... | collective-permute-start | bytes 460808 | tf_op jit(solution)/shard_map/ppermute | solution.py:629
  8.4 2.8 %copy-start.4 = (f32[4,4,5,15,128]{4,1,3,2,0:T(4,128)S(1)}, f32[4,4,5,15,128]{4,1,3,2,0:T(4,128)}, u32[]{:S(2)}) copy-start(f32[4,4,5,15,128]{4,1,3,2,0:T(4,128)} %param.7) | copy-start | bytes 1843204
  9.9 2.5 %collective-permute-start.2 = (f32[15,128]{1,0:T(8,128)S(1)}, f32[15,128]{1,0:T(8,128)S(1)}, u32[]{:S(2)}, u32[]{:S(2)}) collective-permute-start(f32[15,128]{1,0:T(8,128)S(1)} %get-tuple-element.22), channel_id=1, source_target_pairs={{0,1},{1,0},{2,3},{3,2},{4,5},{5,4},{6,7},{7,6},{8,9},{9,8},{10,11... | collective-permute-start | bytes 23048 | tf_op jit(solution)/shard_map/ppermute | solution.py:639
  44.4 6.3 %collective-permute-start.3 = (f32[15,128]{1,0:T(8,128)S(1)}, f32[15,128]{1,0:T(8,128)S(1)}, u32[]{:S(2)}, u32[]{:S(2)}) collective-permute-start(f32[15,128]{1,0:T(8,128)S(1)} %get-tuple-element.29), channel_id=1, source_target_pairs={{0,1},{1,0},{2,3},{3,2},{4,5},{5,4},{6,7},{7,6},{8,9},{9,8},{10,11... | collective-permute-start | bytes 23048 | tf_op jit(solution)/shard_map/ppermute | solution.py:652

commit v5 on v3

--- a/solution.py
+++ b/solution.py
@@ -15,7 +15,8 @@
 H = 8
 XR = 96
 MR = 56
-YR = 136
+YR = 128
+YM = 48
 LINE = B * V * N * B
 f32 = jnp.float32
 
@@ -124,7 +125,7 @@
 
 
 def matrix_kernel(
-    omega_ref, state_ref, couple_ref, xf_ref, yf_ref, fac_ref, xmat_ref, ymat_ref,
+    omega_ref, state_ref, couple_ref, xf_ref, yf_ref, fac_ref, xmat_ref, ymat_ref, tail_ref,
     edge_ref, table_ref, mel, lo, hi,
 ):
     spectral_table(omega_ref[0], table_ref)
@@ -216,15 +217,19 @@
             e0, e1 = edge[r - 50], zero
         for zh, v in enumerate(split(*choose(odd, e0, e1))):
             xmat_ref[pl.ds(zh * MR + r, 4, stride=2 * MR), :] = v[0:4]
-        for zh, v in enumerate(split(e0, e1)):
-            ymat_ref[pl.ds(zh * MR + r, 4, stride=2 * MR), :] = v[4:8]
+        if r % 25 < 24 and r < 50:
+            for zh, v in enumerate(split(e0, e1)):
+                at = zh * YM + r - r // 25
+                ymat_ref[pl.ds(at, 4, stride=2 * YM), :] = v[4:8]
     for d in range(8):
         xmat_ref[d * MR + 55 : (d + 1) * MR, :] = jnp.zeros((1, 128), f32)
-        ymat_ref[d * MR + 55 : (d + 1) * MR, :] = jnp.zeros((1, 128), f32)
-
-
-def halves(v):
-    return v[0:H], jnp.concatenate([v[H:N], jnp.zeros((1, 128), f32)], axis=0)
+    for k, e in enumerate(edge + [blocks[0][24], blocks[3][24], blocks[1][24], blocks[2][24]]):
+        tail_ref[k] = e
+
+
+def halves(v, tail=None):
+    tail = jnp.zeros((1, 128), f32) if tail is None else tail
+    return v[0:H], jnp.concatenate([v[H:N], tail], axis=0)
 
 
 def apply(fac_ref, block, line, vec):
@@ -382,6 +387,10 @@
             r[i * H + n] = dot([(bi[i * V + q], old[q]) for q in range(V)])
 
 
+def places():
+    return (sub() + 4 * lax.axis_index("gz")) % 8
+
+
 def close(b, c, fl, fh, edge):
     for i in range(V):
         for j in range(V):
@@ -391,7 +400,7 @@
 
 
 def x_solver_kernel(msg_ref, out_ref, a, b, c, r, kk, nn, bi, fh, fl):
-    lanes, subs = lane(), sub()
+    lanes, subs = lane(), places()
     even = lanes < 64
     even = jnp.logical_xor(even, lax.axis_index("gx") // 2 % 2 == 1)
 
@@ -443,7 +452,7 @@
 
 
 def y_solver_kernel(msg_ref, out_ref, a, b, c, r, kk, nn, bi, fh, fl):
-    lanes, subs = lane(), sub()
+    lanes, subs = lane(), places()
     left = jnp.logical_xor(lanes < 64, lax.axis_index("gy") % 2 == 1)
 
     def rhs(row):
@@ -458,12 +467,18 @@
         return jnp.where(left, p, q), jnp.where(left, q, p)
 
     begin = subs == 0
-    for e in range(25):
+    for e in range(24):
         low, high = pair(80 + e)
         a[e], fh[e] = jnp.where(begin, 0.0, low), following(high)
-        b[e], high = pair(105 + e)
+        b[e], high = pair(104 + e)
         fl[e] = following(high)
-    edge = [jnp.where(subs == 7, 0.0, pair(130 + i)[0]) for i in range(V)]
+
+    def tail(row):
+        return pair(row * H + H - 1)[1]
+
+    a[24], fh[24] = jnp.where(begin, 0.0, tail(5)), following(tail(6))
+    b[24], fl[24] = tail(7), following(tail(8))
+    edge = [jnp.where(subs == 7, 0.0, tail(i)) for i in range(V)]
     close(b, c, fl, fh, edge)
     for e in range(40):
         r[e] = rhs(e) + edge[e // H] * following(rhs(40 + e))
@@ -512,7 +527,7 @@
                 part_ref[x, y, i] = r - h[i] + 0.5 * z_inner(h[i], lanes) - spec[i]
 
 
-def second_kernel(part_ref, halo_ref, yf_ref, fac_ref, ymat_ref, v_ref, msg_ref):
+def second_kernel(part_ref, halo_ref, yf_ref, fac_ref, ymat_ref, tail_ref, v_ref, msg_ref):
     flag = lax.axis_index("gz")
     lanes = lane((N, 128))
     halo = halo_ref[...]
@@ -531,11 +546,12 @@
             v_ref[x, 0, i] = v0[i]
             v_ref[x, 1, i] = v1[i]
             v_ref[x, 2, i] = v2[i]
-            for at, v in ((0, last[i]), (40, v0[i])):
-                for zh, m in enumerate(split(*halves(v))):
+            for at, v, k in ((0, last[i], i), (40, v0[i], 5 + i)):
+                tail = tail_ref[k, 4 + x : 5 + x, :] if k < 9 else None
+                for zh, m in enumerate(split(*halves(v, tail))):
                     msg_ref[x * 2 + zh, at + i * H : at + (i + 1) * H, :] = m
     for d in range(8):
-        msg_ref[d, 80:YR, :] = ymat_ref[d * MR : (d + 1) * MR, :]
+        msg_ref[d, 80:YR, :] = ymat_ref[d * YM : (d + 1) * YM, :]
 
 
 def last_kernel(ret_ref, v_ref, fac_ref, w_ref):
@@ -583,6 +599,12 @@
     )
 
 
+def exchange(msg, axis):
+    n = lax.axis_size(axis)
+    groups = [[2 * i for i in range(n)], [2 * ((i + n // 2) % n) + 1 for i in range(n)]]
+    return lax.all_to_all(msg, (axis, "gz"), 0, 0, tiled=True, axis_index_groups=groups)
+
+
 def cost(us):
     return pl.CostEstimate(flops=0, bytes_accessed=int(us * 3.6e6), transcendentals=0)
 
@@ -602,13 +624,13 @@
     near, far = call(edge_kernel, [vmem], [sds(B, V, N, 128), sds(B, V, N, 128)])(rows)
     near = lax.ppermute(near, "gy", pairs)
     far = lax.ppermute(far, "gy", other_pairs)
-    fac, xmat, ymat, edge, table = call(
+    fac, xmat, ymat, tail, edge, table = call(
         matrix_kernel, [smem] + [vmem] * 4,
         [
-            sds(225, 8, 128), sds(8 * MR, 128), sds(8 * MR, 128), sds(N, 128),
+            sds(225, 8, 128), sds(16 * MR, 128), sds(16 * YM, 128), sds(9, 8, 128), sds(N, 128),
             sds(N, N, 128),
         ],
-        [scratch(B * 25 * 8, 128), scratch(B * V * 8, 128), scratch(B * V * 8, 128)],
+        [scratch(2 * B * 25 * 8, 128)] + [scratch(2 * B * V * 8, 128)] * 2,
         cost_estimate=cost(1),
     )(omega, state, couple, x_faces, y_faces)
     halo = lax.ppermute(edge, "gz", flip)
@@ -619,23 +641,23 @@
         first_kernel, [vmem] * 8,
         [field, sds(B - 1, B, V, N, 128), sds(16, XR, 128)],
     )(part, near, far, halo, x_faces, y_faces, fac, xmat)
-    got = lax.all_to_all(msg, "gx", 0, 0, tiled=True)
+    got = exchange(msg, "gx")
     mats += [scratch(25, 8, 128)] * 2
     ret = call(x_solver_kernel, [vmem], sds(16 * 40, 128), mats)(got.reshape(16 * XR, 128))
-    back = lax.all_to_all(ret.reshape(16, 40, 128), "gx", 0, 0, tiled=True)
+    back = exchange(ret.reshape(16, 40, 128), "gx")
     h, edge = call(middle_kernel, [vmem] * 3, [field, sds(N, 128)])(back, v, fac)
     halo = lax.ppermute(edge, "gz", flip)
     part = call(
         second_inner_kernel, [vmem] * 5, field, cost_estimate=cost(1)
     )(h, source, r1, couple, table)
     v, msg = call(
-        second_kernel, [vmem] * 5, [sds(B, B - 1, V, N, 128), sds(8, YR, 128)]
-    )(part, halo, y_faces, fac, ymat)
-    got = lax.all_to_all(msg, "gy", 0, 0, tiled=True)
+        second_kernel, [vmem] * 6, [sds(B, B - 1, V, N, 128), sds(8, YR, 128)]
+    )(part, halo, y_faces, fac, ymat, tail)
+    got = exchange(msg, "gy")
     ret = call(
         y_solver_kernel, [vmem], sds(8 * 80, 128), mats
     )(got.reshape(8 * YR, 128))
-    back = lax.all_to_all(ret.reshape(8, 80, 128), "gy", 0, 0, tiled=True)
+    back = exchange(ret.reshape(8, 80, 128), "gy")
     out = call(last_kernel, [vmem] * 3, sds(LINE, 128))(back, v, fac)
     return jnp.transpose(out.reshape(B, V, N, B, 128), (0, 3, 1, 2, 4))
 

time: 91.3 us -> 87.6 us (0.959)
  blocking collectives: 67.5 us -> 62.2 us
  starting transfers between devices: 12.3 us -> 13.6 us
    all_to_all x4, blocking collectives: 67.5 us -> 62.2 us  [exchange(): lax.all_to_all(msg, (axis, 'gz'), 0, 0, tiled=True, axis_index_groups=gro...]
    ppermute x2, starting transfers between devices: 5.09 us -> 6.41 us  [body(): halo = lax.ppermute(edge, 'gz', flip)]
  transfers between devices with their start and end apart: 4 -> 4, of which waited for: 0 -> 0; matrix products, arithmetic and copies ran while one was open for 0% -> 0% of each run, Pallas kernels for 3% -> 4%
where the time goes in v5:
time: 87.6 us; the launch traced here: 87.4 us
  blocking collectives  62.2 us (71%)
  starting transfers between devices  13.6 us (16%)
  Pallas kernels  9.44 us (11%)
  local copies, waits for them, and re-layouts  1.22 us (1%)
    all_to_all x4, blocking collectives, exchange(): lax.all_to_all(msg, (axis, 'gz'), 0, 0, tiled=True, axis_index_groups=gro...  62.2 us
    ppermute x2, starting transfers between devices, body(): halo = lax.ppermute(edge, 'gz', flip)  6.41 us
    ppermute x1, starting transfers between devices, body(): far = lax.ppermute(far, 'gy', other_pairs)  4.67 us
    ppermute x1, starting transfers between devices, body(): near = lax.ppermute(near, 'gy', pairs)  2.55 us
    pallas_call x1, Pallas kernels, body(): call(x_solver_kernel, [vmem], sds(16 * 40, 128), mats)  1.89 us
  transfers between devices with their start and end apart: 4, of which 0 were waited for; matrix products, arithmetic and copies ran while one was open for 0% of the time, Pallas kernels for 4%

profile of v5, /device:TPU:1, one launch (start us, length us, event | category | flops | bytes accessed | tf_op | source)
XLA Modules:
  0.0 87.4 jit_solution(15133851002946508849)
XLA Ops:
  0.0 0.0 copy-start
  0.0 1.1 %copy-done = f32[4,4,5,15,128]{4,1,3,2,0:T(4,128)S(1)} copy-done((f32[4,4,5,15,128]{4,1,3,2,0:T(4,128)S(1)}, f32[4,4,5,15,128]{4,1,3,2,0:T(4,128)}, u32[]{:S(2)}) %copy-start) | copy-done | bytes 614424
  1.1 2.6 %collective-permute-start = (f32[4,5,15,128]{3,2,1,0:T(8,128)S(1)}, f32[4,5,15,128]{3,2,1,0:T(8,128)S(1)}, u32[]{:S(2)}, u32[]{:S(2)}) collective-permute-start(f32[4,5,15,128]{3,2,1,0:T(8,128)S(1)} %get-tuple-element.21), channel_id=1, source_target_pairs={{0,2},{2,0},{4,6},{6,4},{8,10},{10,8},{12,14},{14,12},{1,3},{3,1},... | collective-permute-start | bytes 460808 | tf_op jit(solution)/shard_map/ppermute | solution.py:625
  3.7 0.0 copy-start.1
  3.7 0.0 copy-start.2
  3.7 4.7 %collective-permute-start.1 = (f32[4,5,15,128]{3,2,1,0:T(8,128)S(1)}, f32[4,5,15,128]{3,2,1,0:T(8,128)S(1)}, u32[]{:S(2)}, u32[]{:S(2)}) collective-permute-start(f32[4,5,15,128]{3,2,1,0:T(8,128)S(1)} %get-tuple-element.22), channel_id=1, source_target_pairs={{0,14},{2,4},{4,2},{6,8},{8,6},{10,12},{12,10},{14,0},{1,15},{3,5}... | collective-permute-start | bytes 460808 | tf_op jit(solution)/shard_map/ppermute | solution.py:626
  8.3 0.1 copy.8.state_ref
  8.4 0.0 copy-start.4
  9.1 0.0 copy-done.1
  9.2 0.0 copy-done.2
  9.2 0.0 copy-done.3
  9.2 0.8 shard_map.64
  10.0 1.3 %collective-permute-start.2 = (f32[15,128]{1,0:T(8,128)S(1)}, f32[15,128]{1,0:T(8,128)S(1)}, u32[]{:S(2)}, u32[]{:S(2)}) collective-permute-start(f32[15,128]{1,0:T(8,128)S(1)} %get-tuple-element.23), channel_id=1, source_target_pairs={{0,1},{1,0},{2,3},{3,2},{4,5},{5,4},{6,7},{7,6},{8,9},{9,8},{10,11... | collective-permute-start | bytes 23048 | tf_op jit(solution)/shard_map/ppermute | solution.py:636
  11.3 0.0 copy-done.4
  11.3 0.1 copy.9.source_ref
  11.4 1.0 %shard_map.65.part_ref = f32[4,4,5,15,128]{4,3,2,1,0:T(8,128)S(1)} custom-call(f32[4,4,5,15,128]{4,3,2,1,0:T(8,128)S(1)} %copy.8.state_ref, f32[4,4,5,15,128]{4,3,2,1,0:T(8,128)S(1)} %copy.9.source_ref, f32[2,4,5,4,128]{4,3,2,1,0:T(4,128)S(1)} %bitcast.17, f32[15,15,128]{2,1,0:T(8,128)S(1)} %get-tuple-element.20.table), custom_call_target="tpu_custom_call" | custom-call | bytes 3600000 | tf_op jit(solution)/shard_map/pallas_call | solution.py:637
  12.4 0.0 collective-permute-done.2.halo_ref
  12.4 0.0 collective-permute-done.near_ref
  12.4 0.0 collective-permute-done.1.far_ref
  12.4 0.6 shard_map.67
  13.1 16.7 %all_to_all.20 = f32[16,96,128]{2,1,0:T(8,128)S(1)} all-to-all(f32[16,96,128]{2,1,0:T(8,128)S(1)} %get-tuple-element.26), channel_id=1, replica_groups={{0,16,32,48,64,80,96,112,128,144,160,176,192,208,224,240},{129,145,161,..., dimensions={0} | all-to-all | bytes 1572864 | tf_op jit(solution)/shard_map/all_to_all | solution.py:605
  29.8 1.9 %shard_map.68 = f32[640,128]{1,0:T(8,128)S(1)} custom-call(f32[1536,128]{1,0:T(8,128)S(1)} %bitcast.13), custom_call_target="tpu_custom_call" | custom-call | tf_op jit(solution)/shard_map/pallas_call | solution.py:646
  31.7 12.0 %all_to_all.21.ret_ref = f32[16,40,128]{2,1,0:T(8,128)S(1)} all-to-all(f32[16,40,128]{2,1,0:T(8,128)S(1)} %bitcast.21), channel_id=1, replica_groups={{0,16,32,48,64,80,96,112,128,144,160,176,192,208,224,240},{129,145,161,..., dimensions={0} | all-to-all | bytes 655360 | tf_op jit(solution)/shard_map/all_to_all | solution.py:605
  43.7 0.6 shard_map.69
  44.3 5.1 %collective-permute-start.3 = (f32[15,128]{1,0:T(8,128)S(1)}, f32[15,128]{1,0:T(8,128)S(1)}, u32[]{:S(2)}, u32[]{:S(2)}) collective-permute-start(f32[15,128]{1,0:T(8,128)S(1)} %get-tuple-element.30), channel_id=1, source_target_pairs={{0,1},{1,0},{2,3},{3,2},{4,5},{5,4},{6,7},{7,6},{8,9},{9,8},{10,11... | collective-permute-start | bytes 23048 | tf_op jit(solution)/shard_map/ppermute | solution.py:649
  49.4 1.2 %shard_map.70.part_ref = f32[4,4,5,15,128]{4,3,2,1,0:T(8,128)S(1)} custom-call(f32[4,4,5,15,128]{4,3,2,1,0:T(8,128)S(1)} %get-tuple-element.28.h_ref, f32[4,4,5,15,128]{4,3,2,1,0:T(8,128)S(1)} %copy.9.source_ref, f32[4,4,5,15,128]{4,3,2,1,0:T(8,128)S(1)} %get-tuple-element.29.r_ref, f32[4,5,5,4,128]{4,3,2,1,0:T(4,128)S(1)} %bitcast.23, ...), custom_call_target="tpu_custom_call" | custom-call | bytes 3600000 | tf_op jit(solution)/shard_map/pallas_call | solution.py:650
  50.7 0.0 collective-permute-done.3.halo_ref
  50.7 0.5 shard_map.71
  51.2 19.3 %all_to_all.22 = f32[8,128,128]{2,1,0:T(8,128)S(1)} all-to-all(f32[8,128,128]{2,1,0:T(8,128)S(1)} %get-tuple-element.33), channel_id=1, replica_groups={{0,2,4,6,8,10,12,14},{9,11,13,15,1,3,5,7},{16,18,20,22,24,26,28,30},{25..., dimensions={0} | all-to-all | bytes 1048576 | tf_op jit(solution)/shard_map/all_to_all | solution.py:605
  70.5 1.4 %shard_map.72 = f32[640,128]{1,0:T(8,128)S(1)} custom-call(f32[1024,128]{1,0:T(8,128)S(1)} %bitcast.15), custom_call_target="tpu_custom_call" | custom-call | tf_op jit(solution)/shard_map/pallas_call | solution.py:657
  71.8 14.2 %all_to_all.23.ret_ref = f32[8,80,128]{2,1,0:T(8,128)S(1)} all-to-all(f32[8,80,128]{2,1,0:T(8,128)S(1)} %bitcast.20), channel_id=1, replica_groups={{0,2,4,6,8,10,12,14},{9,11,13,15,1,3,5,7},{16,18,20,22,24,26,28,30},{25..., dimensions={0} | all-to-all | bytes 655360 | tf_op jit(solution)/shard_map/all_to_all | solution.py:605
  86.0 1.3 %shard_map.73 = f32[1200,128]{1,0:T(8,128)} custom-call(f32[8,80,128]{2,1,0:T(8,128)S(1)} %all_to_all.23.ret_ref, f32[4,3,5,15,128]{4,3,2,1,0:T(8,128)S(1)} %get-tuple-element.34.v_ref, f32[225,8,128]{2,1,0:T(8,128)S(1)} %get-tuple-element.24.fac_ref), custom_call_target="tpu_custom_call" | custom-call | tf_op jit(solution)/shard_map/pallas_call | solution.py:661
  (2 shorter events, 0.0 us)
Async XLA Ops:
  0.0 1.1 %copy-start = (f32[4,4,5,15,128]{4,1,3,2,0:T(4,128)S(1)}, f32[4,4,5,15,128]{4,1,3,2,0:T(4,128)}, u32[]{:S(2)}) copy-start(f32[4,4,5,15,128]{4,1,3,2,0:T(4,128)} %param.6) | copy-start | bytes 1843204
  1.1 11.3 %collective-permute-start = (f32[4,5,15,128]{3,2,1,0:T(8,128)S(1)}, f32[4,5,15,128]{3,2,1,0:T(8,128)S(1)}, u32[]{:S(2)}, u32[]{:S(2)}) collective-permute-start(f32[4,5,15,128]{3,2,1,0:T(8,128)S(1)} %get-tuple-element.21), channel_id=1, source_target_pairs={{0,2},{2,0},{4,6},{6,4},{8,10},{10,8},{12,14},{14,12},{1,3},{3,1},... | collective-permute-start | bytes 460808 | tf_op jit(solution)/shard_map/ppermute | solution.py:625
  3.7 5.5 %copy-start.1 = (f32[2,4,4,5,128]{4,2,3,1,0:T(4,128)S(1)}, f32[2,4,4,5,128]{4,2,3,1,0:T(4,128)}, u32[]{:S(2)}) copy-start(f32[2,4,4,5,128]{4,2,3,1,0:T(4,128)} %param.9) | copy-start | bytes 245764
  3.7 5.5 %copy-start.2 = (f32[4,4,5,5,128]{4,1,3,2,0:T(4,128)S(1)}, f32[4,4,5,5,128]{4,1,3,2,0:T(4,128)}, u32[]{:S(2)}) copy-start(f32[4,4,5,5,128]{4,1,3,2,0:T(4,128)} %param.10) | copy-start | bytes 614404
  3.7 5.5 %copy-start.3 = (f32[2,4,4,5,128]{4,2,3,1,0:T(4,128)S(1)}, f32[2,4,4,5,128]{4,2,3,1,0:T(4,128)}, u32[]{:S(2)}) copy-start(f32[2,4,4,5,128]{4,2,3,1,0:T(4,128)} %param.8) | copy-start | bytes 245764
  3.7 8.8 %collective-permute-start.1 = (f32[4,5,15,128]{3,2,1,0:T(8,128)S(1)}, f32[4,5,15,128]{3,2,1,0:T(8,128)S(1)}, u32[]{:S(2)}, u32[]{:S(2)}) collective-permute-start(f32[4,5,15,128]{3,2,1,0:T(8,128)S(1)} %get-tuple-element.22), channel_id=1, source_target_pairs={{0,14},{2,4},{4,2},{6,8},{8,6},{10,12},{12,10},{14,0},{1,15},{3,5}... | collective-permute-start | bytes 460808 | tf_op jit(solution)/shard_map/ppermute | solution.py:626
  8.4 2.9 %copy-start.4 = (f32[4,4,5,15,128]{4,1,3,2,0:T(4,128)S(1)}, f32[4,4,5,15,128]{4,1,3,2,0:T(4,128)}, u32[]{:S(2)}) copy-start(f32[4,4,5,15,128]{4,1,3,2,0:T(4,128)} %param.7) | copy-start | bytes 1843204
  10.0 2.4 %collective-permute-start.2 = (f32[15,128]{1,0:T(8,128)S(1)}, f32[15,128]{1,0:T(8,128)S(1)}, u32[]{:S(2)}, u32[]{:S(2)}) collective-permute-start(f32[15,128]{1,0:T(8,128)S(1)} %get-tuple-element.23), channel_id=1, source_target_pairs={{0,1},{1,0},{2,3},{3,2},{4,5},{5,4},{6,7},{7,6},{8,9},{9,8},{10,11... | collective-permute-start | bytes 23048 | tf_op jit(solution)/shard_map/ppermute | solution.py:636
  44.3 6.3 %collective-permute-start.3 = (f32[15,128]{1,0:T(8,128)S(1)}, f32[15,128]{1,0:T(8,128)S(1)}, u32[]{:S(2)}, u32[]{:S(2)}) collective-permute-start(f32[15,128]{1,0:T(8,128)S(1)} %get-tuple-element.30), channel_id=1, source_target_pairs={{0,1},{1,0},{2,3},{3,2},{4,5},{5,4},{6,7},{7,6},{8,9},{9,8},{10,11... | collective-permute-start | bytes 23048 | tf_op jit(solution)/shard_map/ppermute | solution.py:649

commit v6 on v5

--- a/solution.py
+++ b/solution.py
@@ -94,11 +94,16 @@
 
 def edge_kernel(state_ref, near_ref, far_ref):
     even = lax.axis_index("gy") % 2 == 0
+
+    def line(at):
+        p = state_ref[pl.ds(at, H, stride=B), :]
+        q = state_ref[pl.ds(at + (N - H) * B, H, stride=B), :]
+        return jnp.concatenate([p, q[2 * H - N :]], axis=0)
+
     for x in range(B):
         for i in range(V):
             at = (x * V + i) * N * B
-            first = state_ref[pl.ds(at, N, stride=B), :]
-            last = state_ref[pl.ds(at + B - 1, N, stride=B), :]
+            first, last = line(at), line(at + B - 1)
             near_ref[x, i], far_ref[x, i] = choose(even, first, last)
 
 
@@ -556,7 +561,9 @@
 
 def last_kernel(ret_ref, v_ref, fac_ref, w_ref):
     def put(x, y, i, v):
-        w_ref[pl.ds((x * V + i) * N * B + y, N, stride=B), :] = v
+        at = (x * V + i) * N * B + y
+        w_ref[pl.ds(at, H, stride=B), :] = v[:H]
+        w_ref[pl.ds(at + (N - H) * B, H, stride=B), :] = v[N - H :]
 
     for x in range(B):
         prev, cur = [], []

time: 87.6 us -> 87.6 us (level)
  no operation moved by 1% of the time
where the time goes in v6:
time: 87.6 us; the launch traced here: 87.4 us
  blocking collectives  62.2 us (71%)
  starting transfers between devices  13.6 us (16%)
  Pallas kernels  9.43 us (11%)
  local copies, waits for them, and re-layouts  1.22 us (1%)
    all_to_all x4, blocking collectives, exchange(): lax.all_to_all(msg, (axis, 'gz'), 0, 0, tiled=True, axis_index_groups=gro...  62.2 us
    ppermute x2, starting transfers between devices, body(): halo = lax.ppermute(edge, 'gz', flip)  6.41 us
    ppermute x1, starting transfers between devices, body(): far = lax.ppermute(far, 'gy', other_pairs)  4.67 us
    ppermute x1, starting transfers between devices, body(): near = lax.ppermute(near, 'gy', pairs)  2.55 us
    pallas_call x1, Pallas kernels, body(): call(x_solver_kernel, [vmem], sds(16 * 40, 128), mats)  1.89 us
  transfers between devices with their start and end apart: 4, of which 0 were waited for; matrix products, arithmetic and copies ran while one was open for 0% of the time, Pallas kernels for 4%

profile of v6, /device:TPU:1, one launch (start us, length us, event | category | flops | bytes accessed | tf_op | source)
XLA Modules:
  0.0 87.4 jit_solution(18009397622894798081)
XLA Ops:
  0.0 0.0 copy-start
  0.0 1.1 %copy-done = f32[4,4,5,15,128]{4,1,3,2,0:T(4,128)S(1)} copy-done((f32[4,4,5,15,128]{4,1,3,2,0:T(4,128)S(1)}, f32[4,4,5,15,128]{4,1,3,2,0:T(4,128)}, u32[]{:S(2)}) %copy-start) | copy-done | bytes 614424
  1.1 2.6 %collective-permute-start = (f32[4,5,15,128]{3,2,1,0:T(8,128)S(1)}, f32[4,5,15,128]{3,2,1,0:T(8,128)S(1)}, u32[]{:S(2)}, u32[]{:S(2)}) collective-permute-start(f32[4,5,15,128]{3,2,1,0:T(8,128)S(1)} %get-tuple-element.21), channel_id=1, source_target_pairs={{0,2},{2,0},{4,6},{6,4},{8,10},{10,8},{12,14},{14,12},{1,3},{3,1},... | collective-permute-start | bytes 460808 | tf_op jit(solution)/shard_map/ppermute | solution.py:632
  3.7 0.0 copy-start.1
  3.7 0.0 copy-start.2
  3.7 4.7 %collective-permute-start.1 = (f32[4,5,15,128]{3,2,1,0:T(8,128)S(1)}, f32[4,5,15,128]{3,2,1,0:T(8,128)S(1)}, u32[]{:S(2)}, u32[]{:S(2)}) collective-permute-start(f32[4,5,15,128]{3,2,1,0:T(8,128)S(1)} %get-tuple-element.22), channel_id=1, source_target_pairs={{0,14},{2,4},{4,2},{6,8},{8,6},{10,12},{12,10},{14,0},{1,15},{3,5}... | collective-permute-start | bytes 460808 | tf_op jit(solution)/shard_map/ppermute | solution.py:633
  8.3 0.1 copy.8.state_ref
  8.4 0.0 copy-start.4
  9.1 0.0 copy-done.1
  9.1 0.0 copy-done.2
  9.2 0.0 copy-done.3
  9.2 0.8 shard_map.64
  10.0 1.3 %collective-permute-start.2 = (f32[15,128]{1,0:T(8,128)S(1)}, f32[15,128]{1,0:T(8,128)S(1)}, u32[]{:S(2)}, u32[]{:S(2)}) collective-permute-start(f32[15,128]{1,0:T(8,128)S(1)} %get-tuple-element.23), channel_id=1, source_target_pairs={{0,1},{1,0},{2,3},{3,2},{4,5},{5,4},{6,7},{7,6},{8,9},{9,8},{10,11... | collective-permute-start | bytes 23048 | tf_op jit(solution)/shard_map/ppermute | solution.py:643
  11.3 0.0 copy-done.4
  11.3 0.1 copy.9.source_ref
  11.4 1.0 %shard_map.65.part_ref = f32[4,4,5,15,128]{4,3,2,1,0:T(8,128)S(1)} custom-call(f32[4,4,5,15,128]{4,3,2,1,0:T(8,128)S(1)} %copy.8.state_ref, f32[4,4,5,15,128]{4,3,2,1,0:T(8,128)S(1)} %copy.9.source_ref, f32[2,4,5,4,128]{4,3,2,1,0:T(4,128)S(1)} %bitcast.17, f32[15,15,128]{2,1,0:T(8,128)S(1)} %get-tuple-element.20.table), custom_call_target="tpu_custom_call" | custom-call | bytes 3600000 | tf_op jit(solution)/shard_map/pallas_call | solution.py:644
  12.4 0.0 collective-permute-done.2.halo_ref
  12.4 0.0 collective-permute-done.near_ref
  12.4 0.0 collective-permute-done.1.far_ref
  12.4 0.6 shard_map.67
  13.1 16.7 %all_to_all.20 = f32[16,96,128]{2,1,0:T(8,128)S(1)} all-to-all(f32[16,96,128]{2,1,0:T(8,128)S(1)} %get-tuple-element.26), channel_id=1, replica_groups={{0,16,32,48,64,80,96,112,128,144,160,176,192,208,224,240},{129,145,161,..., dimensions={0} | all-to-all | bytes 1572864 | tf_op jit(solution)/shard_map/all_to_all | solution.py:612
  29.8 1.9 %shard_map.68 = f32[640,128]{1,0:T(8,128)S(1)} custom-call(f32[1536,128]{1,0:T(8,128)S(1)} %bitcast.13), custom_call_target="tpu_custom_call" | custom-call | tf_op jit(solution)/shard_map/pallas_call | solution.py:653
  31.7 12.0 %all_to_all.21.ret_ref = f32[16,40,128]{2,1,0:T(8,128)S(1)} all-to-all(f32[16,40,128]{2,1,0:T(8,128)S(1)} %bitcast.21), channel_id=1, replica_groups={{0,16,32,48,64,80,96,112,128,144,160,176,192,208,224,240},{129,145,161,..., dimensions={0} | all-to-all | bytes 655360 | tf_op jit(solution)/shard_map/all_to_all | solution.py:612
  43.7 0.6 shard_map.69
  44.3 5.1 %collective-permute-start.3 = (f32[15,128]{1,0:T(8,128)S(1)}, f32[15,128]{1,0:T(8,128)S(1)}, u32[]{:S(2)}, u32[]{:S(2)}) collective-permute-start(f32[15,128]{1,0:T(8,128)S(1)} %get-tuple-element.30), channel_id=1, source_target_pairs={{0,1},{1,0},{2,3},{3,2},{4,5},{5,4},{6,7},{7,6},{8,9},{9,8},{10,11... | collective-permute-start | bytes 23048 | tf_op jit(solution)/shard_map/ppermute | solution.py:656
  49.4 1.2 %shard_map.70.part_ref = f32[4,4,5,15,128]{4,3,2,1,0:T(8,128)S(1)} custom-call(f32[4,4,5,15,128]{4,3,2,1,0:T(8,128)S(1)} %get-tuple-element.28.h_ref, f32[4,4,5,15,128]{4,3,2,1,0:T(8,128)S(1)} %copy.9.source_ref, f32[4,4,5,15,128]{4,3,2,1,0:T(8,128)S(1)} %get-tuple-element.29.r_ref, f32[4,5,5,4,128]{4,3,2,1,0:T(4,128)S(1)} %bitcast.23, ...), custom_call_target="tpu_custom_call" | custom-call | bytes 3600000 | tf_op jit(solution)/shard_map/pallas_call | solution.py:657
  50.7 0.0 collective-permute-done.3.halo_ref
  50.7 0.5 shard_map.71
  51.2 19.3 %all_to_all.22 = f32[8,128,128]{2,1,0:T(8,128)S(1)} all-to-all(f32[8,128,128]{2,1,0:T(8,128)S(1)} %get-tuple-element.33), channel_id=1, replica_groups={{0,2,4,6,8,10,12,14},{9,11,13,15,1,3,5,7},{16,18,20,22,24,26,28,30},{25..., dimensions={0} | all-to-all | bytes 1048576 | tf_op jit(solution)/shard_map/all_to_all | solution.py:612
  70.5 1.4 %shard_map.72 = f32[640,128]{1,0:T(8,128)S(1)} custom-call(f32[1024,128]{1,0:T(8,128)S(1)} %bitcast.15), custom_call_target="tpu_custom_call" | custom-call | tf_op jit(solution)/shard_map/pallas_call | solution.py:664
  71.8 14.2 %all_to_all.23.ret_ref = f32[8,80,128]{2,1,0:T(8,128)S(1)} all-to-all(f32[8,80,128]{2,1,0:T(8,128)S(1)} %bitcast.20), channel_id=1, replica_groups={{0,2,4,6,8,10,12,14},{9,11,13,15,1,3,5,7},{16,18,20,22,24,26,28,30},{25..., dimensions={0} | all-to-all | bytes 655360 | tf_op jit(solution)/shard_map/all_to_all | solution.py:612
  86.0 1.3 %shard_map.73 = f32[1200,128]{1,0:T(8,128)} custom-call(f32[8,80,128]{2,1,0:T(8,128)S(1)} %all_to_all.23.ret_ref, f32[4,3,5,15,128]{4,3,2,1,0:T(8,128)S(1)} %get-tuple-element.34.v_ref, f32[225,8,128]{2,1,0:T(8,128)S(1)} %get-tuple-element.24.fac_ref), custom_call_target="tpu_custom_call" | custom-call | tf_op jit(solution)/shard_map/pallas_call | solution.py:668
  (2 shorter events, 0.0 us)
Async XLA Ops:
  0.0 1.1 %copy-start = (f32[4,4,5,15,128]{4,1,3,2,0:T(4,128)S(1)}, f32[4,4,5,15,128]{4,1,3,2,0:T(4,128)}, u32[]{:S(2)}) copy-start(f32[4,4,5,15,128]{4,1,3,2,0:T(4,128)} %param.6) | copy-start | bytes 1843204
  1.1 11.3 %collective-permute-start = (f32[4,5,15,128]{3,2,1,0:T(8,128)S(1)}, f32[4,5,15,128]{3,2,1,0:T(8,128)S(1)}, u32[]{:S(2)}, u32[]{:S(2)}) collective-permute-start(f32[4,5,15,128]{3,2,1,0:T(8,128)S(1)} %get-tuple-element.21), channel_id=1, source_target_pairs={{0,2},{2,0},{4,6},{6,4},{8,10},{10,8},{12,14},{14,12},{1,3},{3,1},... | collective-permute-start | bytes 460808 | tf_op jit(solution)/shard_map/ppermute | solution.py:632
  3.7 5.5 %copy-start.1 = (f32[2,4,4,5,128]{4,2,3,1,0:T(4,128)S(1)}, f32[2,4,4,5,128]{4,2,3,1,0:T(4,128)}, u32[]{:S(2)}) copy-start(f32[2,4,4,5,128]{4,2,3,1,0:T(4,128)} %param.9) | copy-start | bytes 245764
  3.7 5.5 %copy-start.2 = (f32[4,4,5,5,128]{4,1,3,2,0:T(4,128)S(1)}, f32[4,4,5,5,128]{4,1,3,2,0:T(4,128)}, u32[]{:S(2)}) copy-start(f32[4,4,5,5,128]{4,1,3,2,0:T(4,128)} %param.10) | copy-start | bytes 614404
  3.7 5.5 %copy-start.3 = (f32[2,4,4,5,128]{4,2,3,1,0:T(4,128)S(1)}, f32[2,4,4,5,128]{4,2,3,1,0:T(4,128)}, u32[]{:S(2)}) copy-start(f32[2,4,4,5,128]{4,2,3,1,0:T(4,128)} %param.8) | copy-start | bytes 245764
  3.7 8.8 %collective-permute-start.1 = (f32[4,5,15,128]{3,2,1,0:T(8,128)S(1)}, f32[4,5,15,128]{3,2,1,0:T(8,128)S(1)}, u32[]{:S(2)}, u32[]{:S(2)}) collective-permute-start(f32[4,5,15,128]{3,2,1,0:T(8,128)S(1)} %get-tuple-element.22), channel_id=1, source_target_pairs={{0,14},{2,4},{4,2},{6,8},{8,6},{10,12},{12,10},{14,0},{1,15},{3,5}... | collective-permute-start | bytes 460808 | tf_op jit(solution)/shard_map/ppermute | solution.py:633
  8.4 2.9 %copy-start.4 = (f32[4,4,5,15,128]{4,1,3,2,0:T(4,128)S(1)}, f32[4,4,5,15,128]{4,1,3,2,0:T(4,128)}, u32[]{:S(2)}) copy-start(f32[4,4,5,15,128]{4,1,3,2,0:T(4,128)} %param.7) | copy-start | bytes 1843204
  10.0 2.4 %collective-permute-start.2 = (f32[15,128]{1,0:T(8,128)S(1)}, f32[15,128]{1,0:T(8,128)S(1)}, u32[]{:S(2)}, u32[]{:S(2)}) collective-permute-start(f32[15,128]{1,0:T(8,128)S(1)} %get-tuple-element.23), channel_id=1, source_target_pairs={{0,1},{1,0},{2,3},{3,2},{4,5},{5,4},{6,7},{7,6},{8,9},{9,8},{10,11... | collective-permute-start | bytes 23048 | tf_op jit(solution)/shard_map/ppermute | solution.py:643
  44.3 6.3 %collective-permute-start.3 = (f32[15,128]{1,0:T(8,128)S(1)}, f32[15,128]{1,0:T(8,128)S(1)}, u32[]{:S(2)}, u32[]{:S(2)}) collective-permute-start(f32[15,128]{1,0:T(8,128)S(1)} %get-tuple-element.30), channel_id=1, source_target_pairs={{0,1},{1,0},{2,3},{3,2},{4,5},{5,4},{6,7},{7,6},{8,9},{9,8},{10,11... | collective-permute-start | bytes 23048 | tf_op jit(solution)/shard_map/ppermute | solution.py:656
